TPU v7x, 256 devices: a whole 4x4x8 slice. The times are simulated.
256 devices in a mesh: depth: 4 (over x), row: 8 (over z_hi, core), col: 8 (over z_lo, y).
Axes of the slice: x: 4, y: 4, z: 8 (z_hi: 4, z_lo: 2; z = z_hi * 2 + z_lo), core: 2. Of those that a mesh axis runs over, the one named last changes fastest.
Arguments:
- queries: bfloat16 [4096, 6144], P(('depth', 'col'), 'row'), may hold values from -7 to 7
- keys: bfloat16 [4096, 6144], P(('depth', 'col'), 'row'), may hold values from -7 to 7
- values: bfloat16 [4096, 6144], P(('depth', 'col'), 'row'), may hold values from -6 to 6
- out_weight: bfloat16 [6144, 12288], P('row', 'col'), may hold values from -0.078125 to 0.078125
- out_grad: bfloat16 [4096, 12288], P(('depth', 'row'), 'col'), may hold values from -3 to 3
Outputs:
- output: bfloat16 [4096, 12288], P(('depth', 'row'), 'col')
- query_grad: bfloat16 [4096, 6144], P(('depth', 'col'), 'row')
- key_grad: bfloat16 [4096, 6144], P(('depth', 'col'), 'row')
- value_grad: bfloat16 [4096, 6144], P(('depth', 'col'), 'row')
- weight_grad: bfloat16 [6144, 12288], P(('row', 'depth'), 'col')
All inputs are finite; a program needn't handle non-finite values.
Results may differ from a plain program's by a relative error of at most 0.01.
Values may be sent and summed in bfloat16 or wider, within the bound.
No kernel may reach another device: no remote copies, remote signals or barrier semaphores. Data moves between devices by JAX's collectives and lax.ppermute only.
A program may use at most 128 MiB of HBM per device.

v0:
```python
import math

import jax
import jax.numpy as jnp
from jax import lax
from jax.sharding import PartitionSpec as P

DH = 128


def shards(queries, keys, values, out_weight, out_grad):
    tok_rows = queries.shape[0]
    head_cols = queries.shape[1]
    head_count = head_cols // DH
    score_scale = 1.0 / math.sqrt(DH)
    col_index = lax.axis_index("col")
    all_keys, all_values = (
        lax.all_gather(keys, "col", axis=0, tiled=True),
        lax.all_gather(values, "col", axis=0, tiled=True),
    )
    key_rows = all_keys.shape[0]
    query_places = col_index * tok_rows + jnp.arange(tok_rows, dtype=jnp.int32)
    key_places = jnp.arange(key_rows, dtype=jnp.int32)
    causal = query_places[:, None] >= key_places[None, :]
    query_heads = queries.reshape(tok_rows, head_count, DH)
    key_heads = all_keys.reshape(key_rows, head_count, DH)
    value_heads = all_values.reshape(key_rows, head_count, DH)
    scores = (
        jnp.einsum("qhd,khd->hqk", query_heads, key_heads, preferred_element_type=jnp.float32)
        * score_scale
    )
    scores = jnp.where(causal[None], scores, -jnp.inf)
    row_top = jnp.max(scores, axis=-1, keepdims=True)
    shifted = jnp.exp(scores - row_top)
    row_total = jnp.sum(shifted, axis=-1, keepdims=True)
    attend = shifted / row_total
    attend_low = attend.astype(jnp.bfloat16)
    context = jnp.einsum(
        "hqk,khd->qhd", attend_low, value_heads, preferred_element_type=jnp.float32
    )
    context = context.astype(jnp.bfloat16).reshape(tok_rows, head_cols)
    context_all = lax.all_gather(context, "col", axis=0, tiled=True)
    picked = context_all
    output = lax.psum_scatter(
        jnp.dot(picked, out_weight, preferred_element_type=jnp.float32),
        "row",
        scatter_dimension=0,
        tiled=True,
    ).astype(jnp.bfloat16)
    grad_all = lax.all_gather(out_grad, "row", axis=0, tiled=True)
    picked = grad_all
    context_grad = lax.psum_scatter(
        lax.dot_general(
            picked, out_weight, (((1,), (1,)), ((), ())), preferred_element_type=jnp.float32
        ),
        "col",
        scatter_dimension=0,
        tiled=True,
    ).astype(jnp.bfloat16)
    context_share = lax.all_to_all(context_all, "depth", split_axis=1, concat_axis=0, tiled=True)
    grad_every = lax.all_gather(grad_all, "depth", axis=0, tiled=True)
    weight_block = lax.dot_general(
        context_share, grad_every, (((0,), (0,)), ((), ())), preferred_element_type=jnp.float32
    )
    weight_grad = weight_block.astype(jnp.bfloat16)
    grad_heads = context_grad.reshape(tok_rows, head_count, DH)
    prob_grad = jnp.einsum(
        "qhd,khd->hqk", grad_heads, value_heads, preferred_element_type=jnp.float32
    )
    row_dot = jnp.sum(attend * prob_grad, axis=-1, keepdims=True)
    score_grad = (attend * (prob_grad - row_dot) * score_scale).astype(jnp.bfloat16)
    query_grad = jnp.einsum(
        "hqk,khd->qhd", score_grad, key_heads, preferred_element_type=jnp.float32
    )
    query_grad = query_grad.astype(jnp.bfloat16).reshape(tok_rows, head_cols)
    value_part = jnp.einsum(
        "hqk,qhd->khd", attend_low, grad_heads, preferred_element_type=jnp.float32
    )
    key_part = jnp.einsum(
        "hqk,qhd->khd", score_grad, query_heads, preferred_element_type=jnp.float32
    )
    key_sum, value_sum = (
        lax.psum_scatter(
            key_part.reshape(key_rows, head_cols), "col", scatter_dimension=0, tiled=True
        ),
        lax.psum_scatter(
            value_part.reshape(key_rows, head_cols), "col", scatter_dimension=0, tiled=True
        ),
    )
    return (
        output,
        query_grad,
        key_sum.astype(jnp.bfloat16),
        value_sum.astype(jnp.bfloat16),
        weight_grad,
    )


def solution(mesh):
    in_specs = (
        P(("depth", "col"), "row"),
        P(("depth", "col"), "row"),
        P(("depth", "col"), "row"),
        P("row", "col"),
        P(("depth", "row"), "col"),
    )
    out_specs = (
        P(("depth", "row"), "col"),
        P(("depth", "col"), "row"),
        P(("depth", "col"), "row"),
        P(("depth", "col"), "row"),
        P(("row", "depth"), "col"),
    )
    return jax.shard_map(shards, mesh=mesh, in_specs=in_specs, out_specs=out_specs, check_vma=False)
```

profile of v0, /device:TPU:8, one launch (start us, length us, event | category | flops | bytes accessed | tf_op | source)
XLA Modules:
  0.0 567.2 jit_solution(6258042514933932022)
XLA Ops:
  7.2 0.0 copy-start
  7.2 0.0 all-gather.8.cloned.1.call-start
  7.2 0.7 all-gather.8.cloned.1.call-update
  7.9 0.0 all-gather.6.cloned.1.call-start
  8.0 1.7 copy.32
  9.7 0.0 all-gather.6.cloned.1.call-update
  9.7 0.0 all-gather.12.cloned.1.call-start
  9.8 0.7 all-gather.12.cloned.1.call-update
  10.5 0.0 all-gather.10.cloned.1.call-start
  10.5 1.1 copy.31
  11.6 0.1 iota_compare_fusion
  11.8 41.5 %all-gather.8.cloned.1.call-done = bf16[1024,768]{1,0:T(8,128)(2,1)} async-done(((bf16[128,768]{1,0:T(8,128)(2,1)}), bf16[1024,768]{1,0:T(8,128)(2,1)}) %all-gather.8.cloned.1.call-update) | async-done | bytes 1572880 | tf_op jit(solution)/shard_map/all_gather | solution.py:19
  53.3 2.6 copy.35
  55.9 45.0 %all-gather.6.cloned.1.call-done = bf16[1024,768]{0,1:T(8,128)(2,1)} async-done(((bf16[128,768]{0,1:T(8,128)(2,1)}), bf16[1024,768]{0,1:T(8,128)(2,1)}) %all-gather.6.cloned.1.call-update) | async-done | bytes 1572880 | tf_op jit(solution)/shard_map/all_gather | solution.py:18
  100.9 4.4 fusion.31
  105.3 3.7 convolution_convert_fusion.1
  109.0 0.0 all-gather.10.cloned.1.call-update
  109.0 0.0 reduce-scatter.7.cloned.1.call-start
  109.1 39.7 %all-gather.12.cloned.1.call-done = bf16[1024,1536]{1,0:T(8,128)(2,1)} async-done(((bf16[128,1536]{1,0:T(8,128)(2,1)}), bf16[1024,1536]{1,0:T(8,128)(2,1)}) %all-gather.12.cloned.1.call-update) | async-done | bytes 3145744 | tf_op jit(solution)/shard_map/all_gather | solution.py:50
  148.7 0.0 copy-done
  148.7 6.2 %fusion.33 = f32[1024,768]{1,0:T(8,128)} fusion(bf16[1024,1536]{1,0:T(8,128)(2,1)} %all-gather.12.cloned.1.call-done, bf16[768,1536]{1,0:T(8,128)(2,1)S(1)} %copy-done), kind=kOutput, calls=%fused_computation.33 | convolution fusion | flops 2415919104 | bytes 8650752 | tf_op jit(solution)/shard_map/dot_general | solution.py:53
  154.9 0.0 reduce-scatter.7.cloned.1.call-update
  154.9 0.0 reduce-scatter.5.cloned.1.call-start
  155.0 37.6 %all-gather.10.cloned.1.call-done = bf16[1024,768]{0,1:T(8,128)(2,1)} async-done(((bf16[128,768]{0,1:T(8,128)(2,1)}), bf16[1024,768]{0,1:T(8,128)(2,1)}) %all-gather.10.cloned.1.call-update) | async-done | bytes 1572880 | tf_op jit(solution)/shard_map/all_gather | solution.py:42
  192.5 6.0 %fusion.32 = f32[1024,1536]{1,0:T(8,128)} fusion(bf16[1024,768]{0,1:T(8,128)(2,1)} %all-gather.10.cloned.1.call-done, bf16[768,1536]{1,0:T(8,128)(2,1)S(1)} %copy-done), kind=kOutput, calls=%fused_computation.32 | convolution fusion | flops 2415919104 | bytes 10223616 | tf_op jit(solution)/shard_map/dot_general | solution.py:45
  198.5 0.0 reduce-scatter.5.cloned.1.call-update
  198.6 0.0 reduce-scatter.9.cloned.1.call-start
  198.6 45.4 %reduce-scatter.7.cloned.1.call-done = f32[128,768]{1,0:T(8,128)} async-done(((f32[1024,768]{1,0:T(8,128)}), f32[128,768]{1,0:T(8,128)}) %reduce-scatter.7.cloned.1.call-update) | async-done | bytes 393232 | tf_op jit(solution)/shard_map/reduce_scatter | solution.py:52
  244.0 1.0 convert_element_type.37
  245.0 0.2 copy.36
  245.2 3.8 fusion.34
  249.0 10.5 %fusion.7 = f32[6,1024,128]{1,2,0:T(8,128)} fusion(bf16[128,6,128]{0,2,1:T(8,128)(2,1)S(1)} %bitcast.46, f32[6,128,1024]{2,1,0:T(8,128)} %fusion.34, f32[6,128,1024]{2,1,0:T(8,128)} %get-tuple-element.21, f32[6,128]{1,0:T(8,128)S(1)} %get-tuple-element.20), kind=kOutput, calls=%fused_computation.9 | convolution fusion | flops 206833408 | bytes 9636864 | tf_op jit(solution)/shard_map/hqk,qhd->khd/dot_general | solution.py:79
  259.5 3.6 copy.39
  263.1 0.0 reduce-scatter.9.cloned.1.call-update
  263.1 0.0 reduce-scatter.11.cloned.1.call-start
  263.2 4.2 fusion.20
  267.4 3.6 copy.40
  270.9 0.0 reduce-scatter.11.cloned.1.call-update
  271.0 0.0 all-gather.14.cloned.1.call-start
  271.0 0.7 all-gather.14.cloned.1.call-update
  271.7 21.3 %all_to_all.19 = bf16[1024,4,192]{0,2,1:T(8,128)(2,1)S(1)} all-to-all(bf16[1024,4,192]{0,2,1:T(8,128)(2,1)} %bitcast.41), channel_id=1, replica_groups=mesh['depth'=4,'row'=8,'col'=8] {'depth'}, dimensions={1} | all-to-all | bytes 3145728 | tf_op jit(solution)/shard_map/all_to_all | solution.py:60
  293.0 1.3 copy.47
  294.3 9.3 %fusion.17 = bf16[6,128,128]{1,2,0:T(8,128)(2,1)S(1)} fusion(bf16[1024,6,128]{0,2,1:T(8,128)(2,1)} %bitcast.50, f32[6,128,1024]{2,1,0:T(8,128)} %fusion.34, f32[6,128,1024]{2,1,0:T(8,128)} %get-tuple-element.21, f32[6,128]{1,0:T(8,128)S(1)} %get-tuple-element.20), kind=kOutput, calls=%fused_computation.17 | convolution fusion | flops 206931712 | bytes 8064000 | tf_op jit(solution)/shard_map/hqk,khd->qhd/dot_general | solution.py:72
  303.6 0.8 copy.42
  304.4 23.9 %reduce-scatter.5.cloned.1.call-done = f32[128,1536]{1,0:T(8,128)} async-done(((f32[1024,1536]{1,0:T(8,128)}), f32[128,1536]{1,0:T(8,128)}) %reduce-scatter.5.cloned.1.call-update) | async-done | bytes 786448 | tf_op jit(solution)/shard_map/reduce_scatter | solution.py:44
  328.3 1.9 convert_element_type.36
  330.2 47.1 %reduce-scatter.9.cloned.1.call-done = f32[128,768]{1,0:T(8,128)} async-done(((f32[1024,768]{1,0:T(8,128)}), f32[128,768]{1,0:T(8,128)}) %reduce-scatter.9.cloned.1.call-update) | async-done | bytes 393232 | tf_op jit(solution)/shard_map/reduce_scatter | solution.py:83
  377.3 1.7 convert_element_type.41
  379.0 49.2 %reduce-scatter.11.cloned.1.call-done = f32[128,768]{1,0:T(8,128)} async-done(((f32[1024,768]{1,0:T(8,128)}), f32[128,768]{1,0:T(8,128)}) %reduce-scatter.11.cloned.1.call-update) | async-done | bytes 393232 | tf_op jit(solution)/shard_map/reduce_scatter | solution.py:86
  428.3 1.7 convert_element_type.42
  430.0 122.2 %all-gather.14.cloned.1.call-done = bf16[4096,1536]{1,0:T(8,128)(2,1)} async-done(((bf16[1024,1536]{1,0:T(8,128)(2,1)}), bf16[4096,1536]{1,0:T(8,128)(2,1)}) %all-gather.14.cloned.1.call-update) | async-done | bytes 12582928 | tf_op jit(solution)/shard_map/all_gather | solution.py:61
  552.2 8.5 %convolution_convert_fusion = bf16[192,1536]{1,0:T(8,128)(2,1)} fusion(bf16[4096,192]{0,1:T(8,128)(2,1)} %bitcast.42, bf16[4096,1536]{1,0:T(8,128)(2,1)} %all-gather.14.cloned.1.call-done), kind=kOutput, calls=%fused_computation.7 | convolution fusion | flops 2416214016 | bytes 14745600 | tf_op jit(solution)/shard_map/dot_general | solution.py:62
  (1 shorter events, 0.0 us)
Async XLA Ops:
  7.2 141.6 %copy-start = (bf16[768,1536]{1,0:T(8,128)(2,1)S(1)}, bf16[768,1536]{1,0:T(8,128)(2,1)}, u32[]{:S(2)}) copy-start(bf16[768,1536]{1,0:T(8,128)(2,1)} %param.8) | copy-start | bytes 7077892
  7.2 46.1 %all-gather.8.cloned.1.call-start = ((), (), s32[]{:S(2)}) async-start(), calls=%async_computation.6 | async-start | bytes 1769472 | tf_op jit(solution)/shard_map/all_gather | solution.py:19
  7.9 93.0 %all-gather.6.cloned.1.call-start = ((), (), s32[]{:S(2)}) async-start(), calls=%async_computation.5 | async-start | bytes 1769472 | tf_op jit(solution)/shard_map/all_gather | solution.py:18
  9.7 139.0 %all-gather.12.cloned.1.call-start = ((), (), s32[]{:S(2)}) async-start(), calls=%async_computation.9 | async-start | bytes 3538944 | tf_op jit(solution)/shard_map/all_gather | solution.py:50
  10.5 182.1 %all-gather.10.cloned.1.call-start = ((), (), s32[]{:S(2)}) async-start(), calls=%async_computation.7 | async-start | bytes 1769472 | tf_op jit(solution)/shard_map/all_gather | solution.py:42
  109.0 135.0 %reduce-scatter.7.cloned.1.call-start = ((), (), s32[]{:S(2)}) async-start(), calls=%async_computation.10 | async-start | bytes 3538944 | tf_op jit(solution)/shard_map/reduce_scatter | solution.py:52
  154.9 173.4 %reduce-scatter.5.cloned.1.call-start = ((), (), s32[]{:S(2)}) async-start(), calls=%async_computation.8 | async-start | bytes 7077888 | tf_op jit(solution)/shard_map/reduce_scatter | solution.py:44
  198.6 178.8 %reduce-scatter.9.cloned.1.call-start = ((), (), s32[]{:S(2)}) async-start(), calls=%async_computation.11 | async-start | bytes 3538944 | tf_op jit(solution)/shard_map/reduce_scatter | solution.py:83
  263.1 165.1 %reduce-scatter.11.cloned.1.call-start = ((), (), s32[]{:S(2)}) async-start(), calls=%async_computation.12 | async-start | bytes 3538944 | tf_op jit(solution)/shard_map/reduce_scatter | solution.py:86
  271.0 281.2 %all-gather.14.cloned.1.call-start = ((), (), s32[]{:S(2)}) async-start(), calls=%async_computation.13 | async-start | bytes 15728640 | tf_op jit(solution)/shard_map/all_gather | solution.py:61
Sparse Core Ops, SparseCore 0:
  9.8 43.4 all-gather.7
  55.6 45.2 all-gather.5
  102.7 45.9 all-gather.11
  150.9 41.6 all-gather.9
  194.9 49.0 reduce-scatter.6
  246.4 81.8 reduce-scatter.4
  330.8 46.4 reduce-scatter.8
  379.9 48.3 reduce-scatter.10
  430.1 122.0 all-gather.13
where the time goes:
time: 569 us; the launch traced here: 567 us
  waiting for transfers between devices  454 us (80%)
  matrix products  56.5 us (10%)
  blocking collectives  21.3 us (4%)
  local copies, waits for them, and re-layouts  15 us (3%)
  between operations  13.9 us (2%)
  other arithmetic  6.46 us (1%)
    all_gather x1, waiting for transfers between devices, shards(): grad_every = lax.all_gather(grad_all, 'depth', axis=0, tiled=True)  122 us
    reduce_scatter x1, waiting for transfers between devices, shards(): lax.psum_scatter(value_part.reshape(key_rows, head_cols), 'col', scatter_...  49.2 us
    reduce_scatter x1, waiting for transfers between devices, shards(): lax.psum_scatter(key_part.reshape(key_rows, head_cols), 'col', scatter_di...  47.1 us
    reduce_scatter x1, waiting for transfers between devices, shards(): lax.psum_scatter(lax.dot_general(picked, out_weight, (((1,), (1,)), ((),...  45.4 us
    all_gather x1, waiting for transfers between devices, shards(): lax.all_gather(keys, 'col', axis=0, tiled=True)  45 us
    all_gather x1, waiting for transfers between devices, shards(): lax.all_gather(values, 'col', axis=0, tiled=True)  41.5 us
    all_gather x1, waiting for transfers between devices, shards(): grad_all = lax.all_gather(out_grad, 'row', axis=0, tiled=True)  39.7 us
    all_gather x1, waiting for transfers between devices, shards(): context_all = lax.all_gather(context, 'col', axis=0, tiled=True)  37.6 us
  transfers between devices with their start and end apart: 9, of which 9 were waited for; matrix products, arithmetic and copies ran while one was open for 12% of the time, Pallas kernels for 0%

commit v1 on v0

v1 whole, which is shorter than its diff:
```python
import functools
import math

import jax
import jax.numpy as jnp
from jax import lax
from jax.experimental import pallas as pl
from jax.experimental.pallas import tpu as pltpu
from jax.sharding import PartitionSpec as P

DH = 128
POS = 128
QB = 256
SCALE = 1.0 / math.sqrt(DH)
F32 = jnp.float32
BF16 = jnp.bfloat16
VMEM = pl.BlockSpec(memory_space=pltpu.VMEM)
PARAMS = pltpu.CompilerParams(vmem_limit_bytes=40 * 1024 * 1024)

NT = (((1,), (1,)), ((), ()))
TN = (((0,), (0,)), ((), ()))


def along_h(step):
    return [(2 * h + k, 2 * ((h + step) % 4) + k) for h in range(4) for k in range(2)]


ACROSS_CORE = [(r, r ^ 1) for r in range(8)]
ACROSS_Z = [(4 * z + y, 4 * (1 - z) + y) for z in range(2) for y in range(3)]


def from_owner(step):
    return [(4 * z + y, 4 * z + (y + step) % 4) for z in range(2) for y in range(3)]


def to_owner(step):
    return [
        (4 * z + y, 4 * z + (y + step) % 4)
        for z in range(2)
        for y in range(4)
        if (y + step) % 4 < 3
    ]


def attend_block(q, k, first):
    keys = k.shape[0]
    s = lax.dot_general(q, k, NT, preferred_element_type=F32) * SCALE
    rows = first + lax.broadcasted_iota(jnp.int32, (QB, keys), 0)
    cols = lax.broadcasted_iota(jnp.int32, (QB, keys), 1)
    s = jnp.where(rows >= cols, s, -jnp.inf)
    p = jnp.exp(s - jnp.max(s, axis=-1, keepdims=True))
    return p / jnp.sum(p, axis=-1, keepdims=True)


def forward_kernel(qkv, ctx):
    for i in range(qkv.shape[0] // QB):
        rows, seen = pl.ds(i * QB, QB), pl.ds(0, (i + 1) * QB)
        low = attend_block(qkv[rows, :DH], qkv[seen, DH : 2 * DH], i * QB).astype(BF16)
        ctx[rows, :] = jnp.dot(low, qkv[seen, 2 * DH :], preferred_element_type=F32).astype(BF16)


def backward_kernel(qkv, grad, out, dk, dv):
    blocks = qkv.shape[0] // QB
    for i in reversed(range(blocks)):
        rows, seen = pl.ds(i * QB, QB), pl.ds(0, (i + 1) * QB)
        q, k, v, g = qkv[rows, :DH], qkv[seen, DH : 2 * DH], qkv[seen, 2 * DH :], grad[rows, :]
        attend = attend_block(q, k, i * QB)
        dp = lax.dot_general(g, v, NT, preferred_element_type=F32)
        dot = jnp.sum(attend * dp, axis=-1, keepdims=True)
        ds = (attend * (dp - dot) * SCALE).astype(BF16)
        out[rows, :DH] = jnp.dot(ds, k, preferred_element_type=F32).astype(BF16)
        dk_part = lax.dot_general(ds, q, TN, preferred_element_type=F32)
        dv_part = lax.dot_general(attend.astype(BF16), g, TN, preferred_element_type=F32)
        if i == blocks - 1:
            dk[...] = dk_part
            dv[...] = dv_part
        else:
            dk[seen, :] += dk_part
            dv[seen, :] += dv_part
    out[:, DH : 2 * DH] = dk[...].astype(BF16)
    out[:, 2 * DH :] = dv[...].astype(BF16)


def forward(qkv):
    seq = qkv.shape[0]
    return pl.pallas_call(
        forward_kernel,
        out_shape=jax.ShapeDtypeStruct((seq, DH), BF16),
        in_specs=[VMEM],
        out_specs=VMEM,
        compiler_params=PARAMS,
        cost_estimate=pl.CostEstimate(
            flops=3 * seq * seq * DH, bytes_accessed=seq * DH * 8, transcendentals=seq * seq
        ),
        name="attend_forward",
    )(qkv)


def backward(qkv, grad):
    seq = qkv.shape[0]
    return pl.pallas_call(
        backward_kernel,
        out_shape=jax.ShapeDtypeStruct((seq, 3 * DH), BF16),
        in_specs=[VMEM, VMEM],
        out_specs=VMEM,
        scratch_shapes=[pltpu.VMEM((seq, DH), F32), pltpu.VMEM((seq, DH), F32)],
        compiler_params=PARAMS,
        cost_estimate=pl.CostEstimate(
            flops=7 * seq * seq * DH, bytes_accessed=seq * DH * 14, transcendentals=seq * seq
        ),
        name="attend_backward",
    )(qkv, grad)


def shards(queries, keys, values, weight, out_grad):
    row, col, d = lax.axis_index("row"), lax.axis_index("col"), lax.axis_index("depth")
    h, core = row // 2, row % 2
    z, y = col // 4, col % 4
    feats = weight.shape[1]
    half = feats // 2
    on_row = lambda a, perm: lax.ppermute(a, "row", perm)
    on_col = lambda a, perm: lax.ppermute(a, "col", perm)

    stacked = jnp.stack([a.reshape(POS, 6, DH) for a in (queries, keys, values)], axis=2)
    by_head = stacked.transpose(1, 0, 2, 3).reshape(6, POS, 3 * DH)
    none = jnp.zeros((1, POS, 3 * DH), BF16)
    slots = jnp.concatenate([by_head[:3], none, by_head[3:], none], axis=0)

    g_before = on_row(out_grad, along_h(1))
    g_after = on_row(out_grad, along_h(-1))
    qkv = lax.all_to_all(slots, "col", 0, 0, tiled=True).reshape(8 * POS, 3 * DH)
    far_a = on_row(g_before[:, :half], along_h(1))
    far_b = on_row(g_after[:, half:], along_h(-1))
    g_far = jnp.concatenate([far_a, far_b], axis=1)
    grad_all = jnp.zeros((4, 2, POS, feats), BF16)
    for block, shift in ((out_grad, 0), (g_before, 3), (g_after, 1), (g_far, 2)):
        other = on_row(block, ACROSS_CORE)
        place = (h + shift) % 4
        grad_all = lax.dynamic_update_slice(grad_all, block[None, None], (place, core, 0, 0))
        grad_all = lax.dynamic_update_slice(grad_all, other[None, None], (place, 1 - core, 0, 0))
    grad_all = grad_all.reshape(8 * POS, feats)

    w_heads = weight.reshape(6, DH, feats)
    w_rel = []
    for t in range(4):
        for b in range(2):
            head = 3 * (z ^ b) + jnp.minimum((y + t) % 4, 2)
            w_rel.append(lax.dynamic_slice_in_dim(w_heads, head, 1, 0))
    w_rel = jnp.concatenate(w_rel, axis=0).reshape(8 * DH, feats)

    ctx = forward(qkv)
    ctx_z = on_col(ctx, ACROSS_Z)
    pairs = [None] * 4
    pairs[0] = (ctx, ctx_z)
    near = [on_col(ctx, from_owner(s)) for s in (1, 2, 3)]
    across = [on_col(ctx_z, from_owner(s)) for s in (1, 2, 3)]
    for s in (1, 2, 3):
        pairs[4 - s] = (near[s - 1], across[s - 1])
    ctx_rel = jnp.concatenate([a for pair in pairs for a in pair], axis=1)

    sends = []
    for t in (1, 2, 3):
        part = lax.dot_general(
            grad_all, w_rel[2 * DH * t : 2 * DH * (t + 1)], NT, preferred_element_type=F32
        ).astype(BF16)
        sends.append(on_col(part, to_owner(t)))
    total = lax.dot_general(grad_all, w_rel[: 2 * DH], NT, preferred_element_type=F32)
    for part in sends:
        total = total + part.astype(F32)
    from_z = on_col(total[:, DH:].astype(BF16), ACROSS_Z)
    grad = (total[:, :DH] + from_z.astype(F32)).astype(BF16)

    blocks = ctx_rel.reshape(4, 2, POS, 8 * DH)

    def rows_of(k):
        picked = [
            lax.dynamic_slice(blocks, ((h + s) % 4, k, 0, 0), (1, 1, POS, 8 * DH)).reshape(
                POS, 8 * DH
            )
            for s in (2, 1, 3, 0)
        ]
        return jnp.concatenate(picked, axis=0)

    theirs = jnp.dot(rows_of(1 - core), w_rel, preferred_element_type=F32).astype(BF16)
    mine = jnp.dot(rows_of(core), w_rel, preferred_element_type=F32)
    mine = mine + on_row(theirs, ACROSS_CORE).astype(F32)
    far, up, down, own = [mine[POS * i : POS * (i + 1)] for i in range(4)]
    a = on_row(far[:, :half].astype(BF16), along_h(1))
    b = on_row(far[:, half:].astype(BF16), along_h(-1))
    up_b = on_row(up[:, half:].astype(BF16), along_h(1))
    down_a = on_row(down[:, :half].astype(BF16), along_h(-1))
    up_a = on_row((up[:, :half] + a.astype(F32)).astype(BF16), along_h(1))
    down_b = on_row((down[:, half:] + b.astype(F32)).astype(BF16), along_h(-1))
    output = jnp.concatenate(
        [
            own[:, :half] + up_a.astype(F32) + down_a.astype(F32),
            own[:, half:] + up_b.astype(F32) + down_b.astype(F32),
        ],
        axis=1,
    ).astype(BF16)

    w_part = lax.dot_general(ctx_rel, grad_all, TN, preferred_element_type=F32).astype(BF16)
    w_part = w_part.reshape(8, 2, DH // 2, feats)

    def share(target):
        picked = []
        for i in range(3):
            unit = target * 3 + i
            head = unit // 2
            hz, hy = head // 3, head % 3
            place = 2 * ((hy - y) % 4) + (hz ^ z)
            picked.append(
                lax.dynamic_slice(
                    w_part, (place, unit % 2, 0, 0), (1, 1, DH // 2, feats)
                ).reshape(DH // 2, feats)
            )
        return jnp.concatenate(picked, axis=0)

    weight_grad = share(d).astype(F32)
    for s in (1, 2, 3):
        moved = lax.ppermute(share((d + s) % 4), "depth", [(i, (i + s) % 4) for i in range(4)])
        weight_grad = weight_grad + moved.astype(F32)
    weight_grad = weight_grad.astype(BF16)

    back = backward(qkv, grad).reshape(8, POS, 3 * DH)
    back = lax.all_to_all(back, "col", 0, 0, tiled=True)
    back = jnp.concatenate([back[:3], back[4:7]], axis=0)
    grads = [
        back[:, :, DH * i : DH * (i + 1)].transpose(1, 0, 2).reshape(POS, 6 * DH) for i in range(3)
    ]
    return output, grads[0], grads[1], grads[2], weight_grad


def solution(mesh):
    in_specs = (
        P(("depth", "col"), "row"),
        P(("depth", "col"), "row"),
        P(("depth", "col"), "row"),
        P("row", "col"),
        P(("depth", "row"), "col"),
    )
    out_specs = (
        P(("depth", "row"), "col"),
        P(("depth", "col"), "row"),
        P(("depth", "col"), "row"),
        P(("depth", "col"), "row"),
        P(("row", "depth"), "col"),
    )
    return jax.shard_map(shards, mesh=mesh, in_specs=in_specs, out_specs=out_specs, check_vma=False)
```

time: 569 us -> 180 us (0.32)
  waiting for transfers between devices: 454 us -> 47.6 us
  starting transfers between devices: 0.36 us -> 66.9 us
  matrix products: 56.5 us -> 16 us
  blocking collectives: 21.3 us -> 0 us
  local copies, waits for them, and re-layouts: 15 us -> 28.7 us
  between operations: 13.9 us -> 2.26 us
    all_gather x5 -> x0, waiting for transfers between devices: 286 us -> none  [the longest x1 122 us: shards(): grad_every = lax.all_gather(grad_all, 'depth', axis=0, tiled=True)]
    reduce_scatter x4 -> x0, waiting for transfers between devices: 166 us -> none  [the longest x1 49.2 us: shards(): lax.psum_scatter(value_part.reshape(key_rows, head_cols), 'col', scatter_...]
    ppermute x0 -> x29, starting transfers between devices: none -> 56.8 us  [the longest x11 27.7 us: shards(): on_col = lambda a, perm: lax.ppermute(a, 'col', perm)]
    ppermute x0 -> x29, waiting for transfers between devices: none -> 47.6 us  [the longest x15 22.2 us: shards(): on_row = lambda a, perm: lax.ppermute(a, 'row', perm)]
    dot_general x8 -> x7, matrix products: 52.1 us -> 16 us  [the longest x3 5.52 us: shards(): lax.dot_general(grad_all, w_rel[2 * DH * t:2 * DH * (t + 1)], NT, preferr...]
    all_to_all x1 -> x0, blocking collectives: 21.3 us -> none  [shards(): lax.all_to_all(context_all, 'depth', split_axis=1, concat_axis=0, tiled=T...]
    unnamed x5 -> x43, local copies, waits for them, and re-layouts: 3.67 us -> 17.9 us
    all_to_all x0 -> x2, starting transfers between devices: none -> 10.1 us  [the longest x1 5.37 us: shards(): lax.all_to_all(slots, 'col', 0, 0, tiled=True).reshape(8 * POS, 3 * DH)]
  transfers between devices with their start and end apart: 9 -> 31, of which waited for: 9 -> 10; matrix products, arithmetic and copies ran while one was open for 12% -> 29% of each run, Pallas kernels for 0% -> 3%
where the time goes in v1:
time: 180 us; the launch traced here: 177 us
  starting transfers between devices  66.9 us (37%)
  waiting for transfers between devices  47.6 us (26%)
  local copies, waits for them, and re-layouts  28.7 us (16%)
  matrix products  16 us (9%)
  other arithmetic  9.7 us (5%)
  Pallas kernels  5.65 us (3%)
  between operations  2.26 us (1%)
    ppermute x11, starting transfers between devices, shards(): on_col = lambda a, perm: lax.ppermute(a, 'col', perm)  27.7 us
    ppermute x15, starting transfers between devices, shards(): on_row = lambda a, perm: lax.ppermute(a, 'row', perm)  23.2 us
    ppermute x15, waiting for transfers between devices, shards(): on_row = lambda a, perm: lax.ppermute(a, 'row', perm)  22.2 us
    ppermute x11, waiting for transfers between devices, shards(): on_col = lambda a, perm: lax.ppermute(a, 'col', perm)  18.6 us
    unnamed x43, local copies, waits for them, and re-layouts  17.9 us
    ppermute x3, waiting for transfers between devices, shards(): lax.ppermute(share((d + s) % 4), 'depth', [(i, (i + s) % 4) for i in rang...  6.85 us
    ppermute x3, starting transfers between devices, shards(): lax.ppermute(share((d + s) % 4), 'depth', [(i, (i + s) % 4) for i in rang...  5.92 us
    dot_general x3, matrix products, shards(): lax.dot_general(grad_all, w_rel[2 * DH * t:2 * DH * (t + 1)], NT, preferr...  5.52 us
  transfers between devices with their start and end apart: 31, of which 10 were waited for; matrix products, arithmetic and copies ran while one was open for 29% of the time, Pallas kernels for 3%

profile of v1, /device:TPU:8, one launch (start us, length us, event | category | flops | bytes accessed | tf_op | source)
XLA Modules:
  0.0 176.8 jit_solution(14181650874568559770)
XLA Ops:
  0.7 3.3 %collective-permute-start.15 = (bf16[128,1536]{1,0:T(8,128)(2,1)}, bf16[128,1536]{1,0:T(8,128)(2,1)}, u32[]{:S(2)}, u32[]{:S(2)}) collective-permute-start(bf16[128,1536]{1,0:T(8,128)(2,1)} %param.9), channel_id=1, source_target_pairs={{0,16},{8,24},{16,32},{24,40},{32,48},{40,56},{48,0},{56,8},{1,17}... | collective-permute-start | bytes 1179656 | tf_op jit(solution)/shard_map/ppermute | solution.py:121
  4.1 3.1 %collective-permute-start.17 = (bf16[128,1536]{1,0:T(8,128)(2,1)}, bf16[128,1536]{1,0:T(8,128)(2,1)}, u32[]{:S(2)}, u32[]{:S(2)}) collective-permute-start(bf16[128,1536]{1,0:T(8,128)(2,1)} %param.9), channel_id=1, source_target_pairs={{0,48},{8,56},{16,0},{24,8},{32,16},{40,24},{48,32},{56,40},{1,49}... | collective-permute-start | bytes 1179656 | tf_op jit(solution)/shard_map/ppermute | solution.py:121
  7.2 1.1 copy.15
  8.3 1.1 copy.16
  9.4 1.1 copy.17
  10.7 1.0 pad_maximum_fusion
  11.7 5.4 %all-to-all-start = ((bf16[8,128,384]{1,2,0:T(8,128)(2,1)}), bf16[8,128,384]{1,2,0:T(8,128)(2,1)S(1)}, u32[]{:S(2)}, u32[]{:S(2)}) async-start(bf16[8,128,384]{1,2,0:T(8,128)(2,1)} %pad_maximum_fusion), calls=%async_computation | async-start | bytes 1572864 | tf_op jit(solution)/shard_map/all_to_all | solution.py:131
  17.9 0.9 constant_dynamic-update-slice_fusion.14
  18.8 0.9 constant_dynamic-update-slice_fusion.13
  20.6 2.0 %pad_maximum_fusion.2 = bf16[2,128,1536]{2,1,0:T(8,128)(2,1)} fusion(bf16[1,128,1536]{2,1,0:T(8,128)(2,1)S(1)} %get-tuple-element.19, bf16[1,128,1536]{2,1,0:T(8,128)(2,1)} %get-tuple-element.21), kind=kLoop, calls=%fused_computation.27 | loop fusion | flops 393216 | bytes 1572864 | tf_op jit(solution)/shard_map/concatenate | solution.py:149
  22.6 0.9 constant_dynamic-update-slice_fusion.11
  24.3 2.0 %pad_maximum_fusion.3 = bf16[2,128,1536]{2,1,0:T(8,128)(2,1)} fusion(bf16[1,128,1536]{2,1,0:T(8,128)(2,1)S(1)} %get-tuple-element.15, bf16[1,128,1536]{2,1,0:T(8,128)(2,1)} %get-tuple-element.17), kind=kLoop, calls=%fused_computation.28 | loop fusion | flops 393216 | bytes 1572864 | tf_op jit(solution)/shard_map/concatenate | solution.py:149
  26.4 0.9 constant_dynamic-update-slice_fusion.9
  28.1 1.1 pad_maximum_fusion.4
  29.6 0.9 slice.135
  30.5 1.4 collective-permute-start.19
  32.0 0.9 slice.136
  32.9 2.8 %collective-permute-start.20 = (bf16[128,768]{1,0:T(8,128)(2,1)S(1)}, bf16[128,768]{1,0:T(8,128)(2,1)S(1)}, u32[]{:S(2)}, u32[]{:S(2)}) collective-permute-start(bf16[128,768]{1,0:T(8,128)(2,1)S(1)} %slice.136), channel_id=1, source_target_pairs={{0,48},{8,56},{16,0},{24,8},{32,16},{40,24},{48,32},{56,40},{1,49}... | collective-permute-start | bytes 589832 | tf_op jit(solution)/shard_map/ppermute | solution.py:121
  36.3 1.0 bitcast_dynamic-update-slice_fusion.6
  37.3 1.0 bitcast_dynamic-update-slice_fusion.5
  38.4 1.0 collective-permute-done.19
  39.4 6.1 %collective-permute-done.20 = bf16[128,768]{1,0:T(8,128)(2,1)S(1)} collective-permute-done((bf16[128,768]{1,0:T(8,128)(2,1)S(1)}, bf16[128,768]{1,0:T(8,128)(2,1)S(1)}, u32[]{:S(2)}, u32[]{:S(2)}) %collective-permute-start.20) | collective-permute-done | bytes 196640 | tf_op jit(solution)/shard_map/ppermute | solution.py:121
  45.7 1.0 bitcast_dynamic-update-slice_fusion.3
  47.4 1.9 %convolution_convert_fusion.4 = bf16[1024,256]{1,0:T(8,128)(2,1)} fusion(bf16[1024,1536]{1,0:T(8,128)(2,1)S(1)} %bitcast.106, bf16[256,1536]{1,0:T(8,128)(2,1)S(1)} %bitcast.122), kind=kOutput, calls=%fused_computation.8 | convolution fusion | flops 805568512 | bytes 4456448 | tf_op jit(solution)/shard_map/dot_general | solution.py:163
  49.3 3.4 %collective-permute-start.22 = (bf16[1024,256]{1,0:T(8,128)(2,1)}, bf16[1024,256]{1,0:T(8,128)(2,1)S(1)}, u32[]{:S(2)}, u32[]{:S(2)}) collective-permute-start(bf16[1024,256]{1,0:T(8,128)(2,1)} %convolution_convert_fusion.4), channel_id=1, source_target_pairs={{0,1},{1,2},{3,0},{4,5},{5,6},{7,4},{8,9},{9,10},{11,8},{12,13},{1... | collective-permute-start | bytes 1572872 | tf_op jit(solution)/shard_map/ppermute | solution.py:122
  52.6 1.8 %convolution_convert_fusion.3 = bf16[1024,256]{1,0:T(8,128)(2,1)} fusion(bf16[1024,1536]{1,0:T(8,128)(2,1)S(1)} %bitcast.107, bf16[256,1536]{1,0:T(8,128)(2,1)S(1)} %bitcast.123), kind=kOutput, calls=%fused_computation.7 | convolution fusion | flops 805568512 | bytes 4456448 | tf_op jit(solution)/shard_map/dot_general | solution.py:163
  54.5 1.3 collective-permute-start.23
  55.8 1.8 %convolution_convert_fusion.2 = bf16[1024,256]{1,0:T(8,128)(2,1)} fusion(bf16[1024,1536]{1,0:T(8,128)(2,1)S(1)} %bitcast.108, bf16[256,1536]{1,0:T(8,128)(2,1)S(1)} %bitcast.124), kind=kOutput, calls=%fused_computation.6 | convolution fusion | flops 805568512 | bytes 4456448 | tf_op jit(solution)/shard_map/dot_general | solution.py:163
  57.6 4.1 %collective-permute-start.24 = (bf16[1024,256]{1,0:T(8,128)(2,1)}, bf16[1024,256]{1,0:T(8,128)(2,1)}, u32[]{:S(2)}, u32[]{:S(2)}) collective-permute-start(bf16[1024,256]{1,0:T(8,128)(2,1)} %convolution_convert_fusion.2), channel_id=1, source_target_pairs={{1,0},{2,1},{3,2},{5,4},{6,5},{7,6},{9,8},{10,9},{11,10},{13,12},{... | collective-permute-start | bytes 1572872 | tf_op jit(solution)/shard_map/ppermute | solution.py:122
  63.2 2.2 %attend_forward.1 = bf16[1024,128]{1,0:T(8,128)(2,1)S(1)} custom-call(bf16[1024,384]{1,0:T(8,128)(2,1)S(1)} %bitcast.95), custom_call_target="tpu_custom_call" | custom-call | flops 402653184 | bytes 1048576 | tf_op jit(solution)/shard_map/attend_forward/pallas_call | solution.py:86
  65.5 2.0 %collective-permute-start = (bf16[1024,128]{1,0:T(8,128)(2,1)S(1)}, bf16[1024,128]{1,0:T(8,128)(2,1)S(1)}, u32[]{:S(2)}, u32[]{:S(2)}) collective-permute-start(bf16[1024,128]{1,0:T(8,128)(2,1)S(1)} %attend_forward.1), channel_id=1, source_target_pairs={{0,4},{1,5},{2,6},{4,0},{5,1},{6,2},{8,12},{9,13},{10,14},{12,8},{... | collective-permute-start | bytes 786440 | tf_op jit(solution)/shard_map/ppermute | solution.py:122
  67.4 1.9 %collective-permute-start.1 = (bf16[1024,128]{1,0:T(8,128)(2,1)S(1)}, bf16[1024,128]{1,0:T(8,128)(2,1)S(1)}, u32[]{:S(2)}, u32[]{:S(2)}) collective-permute-start(bf16[1024,128]{1,0:T(8,128)(2,1)S(1)} %attend_forward.1), channel_id=1, source_target_pairs={{0,3},{1,0},{2,1},{4,7},{5,4},{6,5},{8,11},{9,8},{10,9},{12,15},{1... | collective-permute-start | bytes 786440 | tf_op jit(solution)/shard_map/ppermute | solution.py:122
  69.4 3.7 %collective-permute-done.23 = bf16[1024,256]{1,0:T(8,128)(2,1)} collective-permute-done((bf16[1024,256]{1,0:T(8,128)(2,1)}, bf16[1024,256]{1,0:T(8,128)(2,1)}, u32[]{:S(2)}, u32[]{:S(2)}) %collective-permute-start.23) | collective-permute-done | bytes 524320 | tf_op jit(solution)/shard_map/ppermute | solution.py:122
  73.0 10.1 %collective-permute-done.24 = bf16[1024,256]{1,0:T(8,128)(2,1)} collective-permute-done((bf16[1024,256]{1,0:T(8,128)(2,1)}, bf16[1024,256]{1,0:T(8,128)(2,1)}, u32[]{:S(2)}, u32[]{:S(2)}) %collective-permute-start.24) | collective-permute-done | bytes 524320 | tf_op jit(solution)/shard_map/ppermute | solution.py:122
  83.2 3.2 %fusion.1 = f32[1024,256]{1,0:T(8,128)S(1)} fusion(bf16[1024,1536]{1,0:T(8,128)(2,1)} %bitcast.109, bf16[256,1536]{1,0:T(8,128)(2,1)S(1)} %bitcast.125, bf16[1024,256]{1,0:T(8,128)(2,1)} %collective-permute-done.24, bf16[1024,256]{1,0:T(8,128)(2,1)} %collective-permute-done.23, bf16[1024,256]{1,0:T(8,128)(2,1)S(1)} %collective-permute-done.22), kind=kOutput, calls=%fused_computation.5 | convolution fusion | flops 806879232 | bytes 6553600 | tf_op jit(solution)/shard_map/dot_general | solution.py:167
  86.4 2.0 %collective-permute-start.25 = (bf16[1024,128]{1,0:T(8,128)(2,1)S(1)}, bf16[1024,128]{1,0:T(8,128)(2,1)S(1)}, u32[]{:S(2)}, u32[]{:S(2)}) collective-permute-start(bf16[1024,128]{1,0:T(8,128)(2,1)S(1)} %slice.177), channel_id=1, source_target_pairs={{0,4},{1,5},{2,6},{4,0},{5,1},{6,2},{8,12},{9,13},{10,14},{12,8},{... | collective-permute-start | bytes 786440 | tf_op jit(solution)/shard_map/ppermute | solution.py:122
  88.5 1.3 collective-permute-start.3
  89.8 3.0 %collective-permute-start.5 = (bf16[1024,128]{1,0:T(8,128)(2,1)S(1)}, bf16[1024,128]{1,0:T(8,128)(2,1)S(1)}, u32[]{:S(2)}, u32[]{:S(2)}) collective-permute-start(bf16[1024,128]{1,0:T(8,128)(2,1)S(1)} %attend_forward.1), channel_id=1, source_target_pairs={{0,1},{1,2},{2,3},{4,5},{5,6},{6,7},{8,9},{9,10},{10,11},{12,13},{... | collective-permute-start | bytes 786440 | tf_op jit(solution)/shard_map/ppermute | solution.py:122
  92.8 3.4 %collective-permute-start.2 = (bf16[1024,128]{1,0:T(8,128)(2,1)S(1)}, bf16[1024,128]{1,0:T(8,128)(2,1)}, u32[]{:S(2)}, u32[]{:S(2)}) collective-permute-start(bf16[1024,128]{1,0:T(8,128)(2,1)S(1)} %collective-permute-done), channel_id=1, source_target_pairs={{0,3},{1,0},{2,1},{4,7},{5,4},{6,5},{8,11},{9,8},{10,9},{12,15},{1... | collective-permute-start | bytes 786440 | tf_op jit(solution)/shard_map/ppermute | solution.py:122
  96.3 1.3 collective-permute-start.4
  97.7 1.3 copy-done.3
  99.1 4.0 %collective-permute-start.6 = (bf16[1024,128]{1,0:T(8,128)(2,1)S(1)}, bf16[1024,128]{1,0:T(8,128)(2,1)S(1)}, u32[]{:S(2)}, u32[]{:S(2)}) collective-permute-start(bf16[1024,128]{1,0:T(8,128)(2,1)S(1)} %collective-permute-done), channel_id=1, source_target_pairs={{0,1},{1,2},{2,3},{4,5},{5,6},{6,7},{8,9},{9,10},{10,11},{12,13},{... | collective-permute-start | bytes 786440 | tf_op jit(solution)/shard_map/ppermute | solution.py:122
  103.1 3.4 %attend_backward.1 = bf16[1024,384]{1,0:T(8,128)(2,1)S(1)} custom-call(bf16[1024,384]{1,0:T(8,128)(2,1)S(1)} %bitcast.96, bf16[1024,128]{1,0:T(8,128)(2,1)S(1)} %fusion.19.grad), custom_call_target="tpu_custom_call" | custom-call | flops 939524096 | bytes 1835008 | tf_op jit(solution)/shard_map/attend_backward/pallas_call | solution.py:101
  106.6 1.2 copy.21
  107.7 4.7 %all-to-all-start.1 = ((bf16[8,128,384]{1,2,0:T(8,128)(2,1)}), bf16[8,128,384]{1,2,0:T(8,128)(2,1)S(1)}, u32[]{:S(2)}, u32[]{:S(2)}) async-start(bf16[8,128,384]{1,2,0:T(8,128)(2,1)} %copy.21), calls=%async_computation.1 | async-start | bytes 1572864 | tf_op jit(solution)/shard_map/all_to_all | solution.py:226
  112.5 1.7 constant_dynamic-update-slice_fusion.4
  116.5 4.8 %collective-permute-done.6 = bf16[1024,128]{1,0:T(8,128)(2,1)S(1)} collective-permute-done((bf16[1024,128]{1,0:T(8,128)(2,1)S(1)}, bf16[1024,128]{1,0:T(8,128)(2,1)S(1)}, u32[]{:S(2)}, u32[]{:S(2)}) %collective-permute-start.6) | collective-permute-done | bytes 262176 | tf_op jit(solution)/shard_map/ppermute | solution.py:122
  122.1 1.7 dynamic-slice_bitcast_fusion.7
  123.8 1.8 %convolution_convert_fusion.1 = bf16[512,1536]{1,0:T(8,128)(2,1)S(1)} fusion(bf16[1024,1536]{1,0:T(8,128)(2,1)S(1)} %bitcast.126, bf16[128,1024]{1,0:T(8,128)(2,1)S(1)} %get-tuple-element.41, bf16[128,1024]{1,0:T(8,128)(2,1)S(1)} %get-tuple-element.42, bf16[128,1024]{1,0:T(8,128)(2,1)S(1)} %get-tuple-element.43, bf16[128,1024]{1,0:T(8,128)(2,1)S(1)} %get-tuple-element.44), kind=kOutput, calls=%fused_computation.2 | convolution fusion | flops 1615593472 | bytes 5767168 | tf_op jit(solution)/shard_map/dot_general | solution.py:184
  126.3 3.8 %convolution_convert_fusion = bf16[1024,1536]{1,0:T(8,128)(2,1)S(1)} fusion(bf16[1024,1024]{1,0:T(8,128)(2,1)S(1)} %copy-done.4, bf16[1024,1536]{1,0:T(8,128)(2,1)S(1)} %bitcast.110), kind=kOutput, calls=%fused_computation | convolution fusion | flops 3222798336 | bytes 8388608 | tf_op jit(solution)/shard_map/dot_general | solution.py:202
  130.4 1.6 collective-permute-start.26
  132.1 2.8 %collective-permute-start.27 = (bf16[192,1536]{1,0:T(8,128)(2,1)S(1)}, bf16[192,1536]{1,0:T(8,128)(2,1)S(1)}, u32[]{:S(2)}, u32[]{:S(2)}) collective-permute-start(bf16[192,1536]{1,0:T(8,128)(2,1)S(1)} %pad_maximum_fusion.6), channel_id=1, source_target_pairs={{0,128},{64,192},{128,0},{192,64},{1,129},{65,193},{129,1},{193,65... | collective-permute-start | bytes 1769480 | tf_op jit(solution)/shard_map/ppermute | solution.py:221
  134.9 1.5 collective-permute-start.28
  136.4 1.8 %fusion.33 = (bf16[512,1536]{1,0:T(8,128)(2,1)S(1)}, f32[512,1536]{1,0:T(8,128)S(1)}) fusion(bf16[512,1536]{1,0:T(8,128)(2,1)S(1)} %collective-permute-done.7, bf16[1024,1536]{1,0:T(8,128)(2,1)S(1)} %bitcast.127, bf16[128,1024]{1,0:T(8,128)(2,1)S(1)} %get-tuple-element.45, bf16[128,1024]{1,0:T(8,128)(2,1)S(1)} %get-tuple-element.46, ...), kind=kOutput, calls=%fused_computation.114 | convolution fusion | flops 1617166336 | bytes 10485760 | tf_op jit(solution)/shard_map/dot_general | solution.py:185
  138.3 4.1 %collective-permute-start.8 = (bf16[128,768]{1,0:T(8,128)(2,1)S(1)}, bf16[128,768]{1,0:T(8,128)(2,1)S(1)}, u32[]{:S(2)}, u32[]{:S(2)}) collective-permute-start(bf16[128,768]{1,0:T(8,128)(2,1)S(1)} %get-tuple-element.48), channel_id=1, source_target_pairs={{0,16},{8,24},{16,32},{24,40},{32,48},{40,56},{48,0},{56,8},{1,17}... | collective-permute-start | bytes 589832 | tf_op jit(solution)/shard_map/ppermute | solution.py:121
  142.5 8.2 %collective-permute-done.8 = bf16[128,768]{1,0:T(8,128)(2,1)S(1)} collective-permute-done((bf16[128,768]{1,0:T(8,128)(2,1)S(1)}, bf16[128,768]{1,0:T(8,128)(2,1)S(1)}, u32[]{:S(2)}, u32[]{:S(2)}) %collective-permute-start.8) | collective-permute-done | bytes 196640 | tf_op jit(solution)/shard_map/ppermute | solution.py:121
  150.8 3.0 %collective-permute-start.9 = (bf16[128,768]{1,0:T(8,128)(2,1)S(1)}, bf16[128,768]{1,0:T(8,128)(2,1)S(1)}, u32[]{:S(2)}, u32[]{:S(2)}) collective-permute-start(bf16[128,768]{1,0:T(8,128)(2,1)S(1)} %fusion.23), channel_id=1, source_target_pairs={{0,16},{8,24},{16,32},{24,40},{32,48},{40,56},{48,0},{56,8},{1,17}... | collective-permute-start | bytes 589832 | tf_op jit(solution)/shard_map/ppermute | solution.py:121
  153.8 6.8 %collective-permute-done.27 = bf16[192,1536]{1,0:T(8,128)(2,1)S(1)} collective-permute-done((bf16[192,1536]{1,0:T(8,128)(2,1)S(1)}, bf16[192,1536]{1,0:T(8,128)(2,1)S(1)}, u32[]{:S(2)}, u32[]{:S(2)}) %collective-permute-start.27) | collective-permute-done | bytes 589856 | tf_op jit(solution)/shard_map/ppermute | solution.py:221
  160.7 1.1 add_convert_fusion
  161.8 4.0 %collective-permute-start.11 = (bf16[128,768]{1,0:T(8,128)(2,1)S(1)}, bf16[128,768]{1,0:T(8,128)(2,1)S(1)}, u32[]{:S(2)}, u32[]{:S(2)}) collective-permute-start(bf16[128,768]{1,0:T(8,128)(2,1)S(1)} %get-tuple-element.50), channel_id=1, source_target_pairs={{0,16},{8,24},{16,32},{24,40},{32,48},{40,56},{48,0},{56,8},{1,17}... | collective-permute-start | bytes 589832 | tf_op jit(solution)/shard_map/ppermute | solution.py:121
  166.2 0.8 copy.22
  168.7 4.4 %collective-permute-done.11 = bf16[128,768]{1,0:T(8,128)(2,1)S(1)} collective-permute-done((bf16[128,768]{1,0:T(8,128)(2,1)S(1)}, bf16[128,768]{1,0:T(8,128)(2,1)S(1)}, u32[]{:S(2)}, u32[]{:S(2)}) %collective-permute-start.11) | collective-permute-done | bytes 196640 | tf_op jit(solution)/shard_map/ppermute | solution.py:121
  173.2 1.8 %collective-permute-done.13 = bf16[128,768]{1,0:T(8,128)(2,1)S(1)} collective-permute-done((bf16[128,768]{1,0:T(8,128)(2,1)S(1)}, bf16[128,768]{1,0:T(8,128)(2,1)S(1)}, u32[]{:S(2)}, u32[]{:S(2)}) %collective-permute-start.13) | collective-permute-done | bytes 196640 | tf_op jit(solution)/shard_map/ppermute | solution.py:121
  175.0 1.1 fusion.22
  (92 shorter events, 13.2 us)
Async XLA Ops:
  0.6 35.7 %collective-permute-start.14 = (bf16[128,1536]{1,0:T(8,128)(2,1)}, bf16[128,1536]{1,0:T(8,128)(2,1)}, u32[]{:S(2)}, u32[]{:S(2)}) collective-permute-start(bf16[128,1536]{1,0:T(8,128)(2,1)} %param.9), channel_id=1, source_target_pairs={{0,8},{8,0},{16,24},{24,16},{32,40},{40,32},{48,56},{56,48},{1,9},... | collective-permute-start | bytes 1179656 | tf_op jit(solution)/shard_map/ppermute | solution.py:121
  0.7 28.9 %collective-permute-start.15 = (bf16[128,1536]{1,0:T(8,128)(2,1)}, bf16[128,1536]{1,0:T(8,128)(2,1)}, u32[]{:S(2)}, u32[]{:S(2)}) collective-permute-start(bf16[128,1536]{1,0:T(8,128)(2,1)} %param.9), channel_id=1, source_target_pairs={{0,16},{8,24},{16,32},{24,40},{32,48},{40,56},{48,0},{56,8},{1,17}... | collective-permute-start | bytes 1179656 | tf_op jit(solution)/shard_map/ppermute | solution.py:121
  4.1 27.9 %collective-permute-start.17 = (bf16[128,1536]{1,0:T(8,128)(2,1)}, bf16[128,1536]{1,0:T(8,128)(2,1)}, u32[]{:S(2)}, u32[]{:S(2)}) collective-permute-start(bf16[128,1536]{1,0:T(8,128)(2,1)} %param.9), channel_id=1, source_target_pairs={{0,48},{8,56},{16,0},{24,8},{32,16},{40,24},{48,32},{56,40},{1,49}... | collective-permute-start | bytes 1179656 | tf_op jit(solution)/shard_map/ppermute | solution.py:121
  10.6 6.5 %copy-start = (bf16[768,1536]{1,0:T(8,128)(2,1)S(1)}, bf16[768,1536]{1,0:T(8,128)(2,1)}, u32[]{:S(2)}) copy-start(bf16[768,1536]{1,0:T(8,128)(2,1)} %param.8) | copy-start | bytes 7077892
  11.7 51.2 %all-to-all-start = ((bf16[8,128,384]{1,2,0:T(8,128)(2,1)}), bf16[8,128,384]{1,2,0:T(8,128)(2,1)S(1)}, u32[]{:S(2)}, u32[]{:S(2)}) async-start(bf16[8,128,384]{1,2,0:T(8,128)(2,1)} %pad_maximum_fusion), calls=%async_computation | async-start | bytes 1572864 | tf_op jit(solution)/shard_map/all_to_all | solution.py:131
  28.1 1.4 copy-start.9
  30.5 8.9 %collective-permute-start.19 = (bf16[128,768]{1,0:T(8,128)(2,1)S(1)}, bf16[128,768]{1,0:T(8,128)(2,1)S(1)}, u32[]{:S(2)}, u32[]{:S(2)}) collective-permute-start(bf16[128,768]{1,0:T(8,128)(2,1)S(1)} %slice.135), channel_id=1, source_target_pairs={{0,16},{8,24},{16,32},{24,40},{32,48},{40,56},{48,0},{56,8},{1,17}... | collective-permute-start | bytes 589832 | tf_op jit(solution)/shard_map/ppermute | solution.py:121
  32.9 12.6 %collective-permute-start.20 = (bf16[128,768]{1,0:T(8,128)(2,1)S(1)}, bf16[128,768]{1,0:T(8,128)(2,1)S(1)}, u32[]{:S(2)}, u32[]{:S(2)}) collective-permute-start(bf16[128,768]{1,0:T(8,128)(2,1)S(1)} %slice.136), channel_id=1, source_target_pairs={{0,48},{8,56},{16,0},{24,8},{32,16},{40,24},{48,32},{56,40},{1,49}... | collective-permute-start | bytes 589832 | tf_op jit(solution)/shard_map/ppermute | solution.py:121
  35.8 9.8 %collective-permute-start.16 = (bf16[128,1536]{1,0:T(8,128)(2,1)}, bf16[128,1536]{1,0:T(8,128)(2,1)S(1)}, u32[]{:S(2)}, u32[]{:S(2)}) collective-permute-start(bf16[128,1536]{1,0:T(8,128)(2,1)} %collective-permute-done.15), channel_id=1, source_target_pairs={{0,8},{8,0},{16,24},{24,16},{32,40},{40,32},{48,56},{56,48},{1,9},... | collective-permute-start | bytes 1179656 | tf_op jit(solution)/shard_map/ppermute | solution.py:121
  35.8 10.9 %collective-permute-start.18 = (bf16[128,1536]{1,0:T(8,128)(2,1)}, bf16[128,1536]{1,0:T(8,128)(2,1)S(1)}, u32[]{:S(2)}, u32[]{:S(2)}) collective-permute-start(bf16[128,1536]{1,0:T(8,128)(2,1)} %collective-permute-done.17), channel_id=1, source_target_pairs={{0,8},{8,0},{16,24},{24,16},{32,40},{40,32},{48,56},{56,48},{1,9},... | collective-permute-start | bytes 1179656 | tf_op jit(solution)/shard_map/ppermute | solution.py:121
  38.4 9.0 %copy-start.7 = (bf16[2,128,1536]{2,1,0:T(8,128)(2,1)S(1)}, bf16[2,128,1536]{2,1,0:T(8,128)(2,1)}, u32[]{:S(2)}) copy-start(bf16[2,128,1536]{2,1,0:T(8,128)(2,1)} %pad_maximum_fusion.2) | copy-start | bytes 2359300
  45.5 1.8 %collective-permute-start.21 = (bf16[128,1536]{1,0:T(8,128)(2,1)S(1)}, bf16[128,1536]{1,0:T(8,128)(2,1)S(1)}, u32[]{:S(2)}, u32[]{:S(2)}) collective-permute-start(bf16[128,1536]{1,0:T(8,128)(2,1)S(1)} %constant_dynamic-update-slice_fusion.16), channel_id=1, source_target_pairs={{0,8},{8,0},{16,24},{24,16},{32,40},{40,32},{48,56},{56,48},{1,9},... | collective-permute-start | bytes 1179656 | tf_op jit(solution)/shard_map/ppermute | solution.py:121
  47.4 8.4 %copy-start.1 = (bf16[4,2,128,1536]{3,2,1,0:T(8,128)(2,1)}, bf16[4,2,128,1536]{3,2,1,0:T(8,128)(2,1)S(1)}, u32[]{:S(2)}) copy-start(bf16[4,2,128,1536]{3,2,1,0:T(8,128)(2,1)S(1)} %bitcast_dynamic-update-slice_fusion) | copy-start | bytes 9437188
  47.4 5.2 %copy-start.8 = (bf16[2,128,1536]{2,1,0:T(8,128)(2,1)S(1)}, bf16[2,128,1536]{2,1,0:T(8,128)(2,1)}, u32[]{:S(2)}) copy-start(bf16[2,128,1536]{2,1,0:T(8,128)(2,1)} %pad_maximum_fusion.3) | copy-start | bytes 2359300
  49.3 20.1 %collective-permute-start.22 = (bf16[1024,256]{1,0:T(8,128)(2,1)}, bf16[1024,256]{1,0:T(8,128)(2,1)S(1)}, u32[]{:S(2)}, u32[]{:S(2)}) collective-permute-start(bf16[1024,256]{1,0:T(8,128)(2,1)} %convolution_convert_fusion.4), channel_id=1, source_target_pairs={{0,1},{1,2},{3,0},{4,5},{5,6},{7,4},{8,9},{9,10},{11,8},{12,13},{1... | collective-permute-start | bytes 1572872 | tf_op jit(solution)/shard_map/ppermute | solution.py:122
  54.5 18.6 %collective-permute-start.23 = (bf16[1024,256]{1,0:T(8,128)(2,1)}, bf16[1024,256]{1,0:T(8,128)(2,1)}, u32[]{:S(2)}, u32[]{:S(2)}) collective-permute-start(bf16[1024,256]{1,0:T(8,128)(2,1)} %convolution_convert_fusion.3), channel_id=1, source_target_pairs={{0,2},{2,0},{3,1},{4,6},{6,4},{7,5},{8,10},{10,8},{11,9},{12,14},{... | collective-permute-start | bytes 1572872 | tf_op jit(solution)/shard_map/ppermute | solution.py:122
  55.8 7.0 %copy-start.5 = (bf16[1,128,1536]{2,1,0:T(8,128)(2,1)S(1)}, bf16[1,128,1536]{2,1,0:T(8,128)(2,1)}, u32[]{:S(2)}) copy-start(bf16[1,128,1536]{2,1,0:T(8,128)(2,1)} %get-tuple-element.23) | copy-start | bytes 1179652
  57.6 25.6 %collective-permute-start.24 = (bf16[1024,256]{1,0:T(8,128)(2,1)}, bf16[1024,256]{1,0:T(8,128)(2,1)}, u32[]{:S(2)}, u32[]{:S(2)}) collective-permute-start(bf16[1024,256]{1,0:T(8,128)(2,1)} %convolution_convert_fusion.2), channel_id=1, source_target_pairs={{1,0},{2,1},{3,2},{5,4},{6,5},{7,6},{9,8},{10,9},{11,10},{13,12},{... | collective-permute-start | bytes 1572872 | tf_op jit(solution)/shard_map/ppermute | solution.py:122
  65.5 27.4 %collective-permute-start = (bf16[1024,128]{1,0:T(8,128)(2,1)S(1)}, bf16[1024,128]{1,0:T(8,128)(2,1)S(1)}, u32[]{:S(2)}, u32[]{:S(2)}) collective-permute-start(bf16[1024,128]{1,0:T(8,128)(2,1)S(1)} %attend_forward.1), channel_id=1, source_target_pairs={{0,4},{1,5},{2,6},{4,0},{5,1},{6,2},{8,12},{9,13},{10,14},{12,8},{... | collective-permute-start | bytes 786440 | tf_op jit(solution)/shard_map/ppermute | solution.py:122
  67.4 28.9 %collective-permute-start.1 = (bf16[1024,128]{1,0:T(8,128)(2,1)S(1)}, bf16[1024,128]{1,0:T(8,128)(2,1)S(1)}, u32[]{:S(2)}, u32[]{:S(2)}) collective-permute-start(bf16[1024,128]{1,0:T(8,128)(2,1)S(1)} %attend_forward.1), channel_id=1, source_target_pairs={{0,3},{1,0},{2,1},{4,7},{5,4},{6,5},{8,11},{9,8},{10,9},{12,15},{1... | collective-permute-start | bytes 786440 | tf_op jit(solution)/shard_map/ppermute | solution.py:122
  86.4 11.3 %collective-permute-start.25 = (bf16[1024,128]{1,0:T(8,128)(2,1)S(1)}, bf16[1024,128]{1,0:T(8,128)(2,1)S(1)}, u32[]{:S(2)}, u32[]{:S(2)}) collective-permute-start(bf16[1024,128]{1,0:T(8,128)(2,1)S(1)} %slice.177), channel_id=1, source_target_pairs={{0,4},{1,5},{2,6},{4,0},{5,1},{6,2},{8,12},{9,13},{10,14},{12,8},{... | collective-permute-start | bytes 786440 | tf_op jit(solution)/shard_map/ppermute | solution.py:122
  88.5 25.7 %collective-permute-start.3 = (bf16[1024,128]{1,0:T(8,128)(2,1)S(1)}, bf16[1024,128]{1,0:T(8,128)(2,1)S(1)}, u32[]{:S(2)}, u32[]{:S(2)}) collective-permute-start(bf16[1024,128]{1,0:T(8,128)(2,1)S(1)} %attend_forward.1), channel_id=1, source_target_pairs={{0,2},{1,3},{2,0},{4,6},{5,7},{6,4},{8,10},{9,11},{10,8},{12,14},{... | collective-permute-start | bytes 786440 | tf_op jit(solution)/shard_map/ppermute | solution.py:122
  89.8 26.0 %collective-permute-start.5 = (bf16[1024,128]{1,0:T(8,128)(2,1)S(1)}, bf16[1024,128]{1,0:T(8,128)(2,1)S(1)}, u32[]{:S(2)}, u32[]{:S(2)}) collective-permute-start(bf16[1024,128]{1,0:T(8,128)(2,1)S(1)} %attend_forward.1), channel_id=1, source_target_pairs={{0,1},{1,2},{2,3},{4,5},{5,6},{6,7},{8,9},{9,10},{10,11},{12,13},{... | collective-permute-start | bytes 786440 | tf_op jit(solution)/shard_map/ppermute | solution.py:122
  92.8 19.6 %collective-permute-start.2 = (bf16[1024,128]{1,0:T(8,128)(2,1)S(1)}, bf16[1024,128]{1,0:T(8,128)(2,1)}, u32[]{:S(2)}, u32[]{:S(2)}) collective-permute-start(bf16[1024,128]{1,0:T(8,128)(2,1)S(1)} %collective-permute-done), channel_id=1, source_target_pairs={{0,3},{1,0},{2,1},{4,7},{5,4},{6,5},{8,11},{9,8},{10,9},{12,15},{1... | collective-permute-start | bytes 786440 | tf_op jit(solution)/shard_map/ppermute | solution.py:122
  96.3 18.6 %collective-permute-start.4 = (bf16[1024,128]{1,0:T(8,128)(2,1)S(1)}, bf16[1024,128]{1,0:T(8,128)(2,1)S(1)}, u32[]{:S(2)}, u32[]{:S(2)}) collective-permute-start(bf16[1024,128]{1,0:T(8,128)(2,1)S(1)} %collective-permute-done), channel_id=1, source_target_pairs={{0,2},{1,3},{2,0},{4,6},{5,7},{6,4},{8,10},{9,11},{10,8},{12,14},{... | collective-permute-start | bytes 786440 | tf_op jit(solution)/shard_map/ppermute | solution.py:122
  97.7 1.4 copy-start.3
  99.1 22.2 %collective-permute-start.6 = (bf16[1024,128]{1,0:T(8,128)(2,1)S(1)}, bf16[1024,128]{1,0:T(8,128)(2,1)S(1)}, u32[]{:S(2)}, u32[]{:S(2)}) collective-permute-start(bf16[1024,128]{1,0:T(8,128)(2,1)S(1)} %collective-permute-done), channel_id=1, source_target_pairs={{0,1},{1,2},{2,3},{4,5},{5,6},{6,7},{8,9},{9,10},{10,11},{12,13},{... | collective-permute-start | bytes 786440 | tf_op jit(solution)/shard_map/ppermute | solution.py:122
  107.7 58.4 %all-to-all-start.1 = ((bf16[8,128,384]{1,2,0:T(8,128)(2,1)}), bf16[8,128,384]{1,2,0:T(8,128)(2,1)S(1)}, u32[]{:S(2)}, u32[]{:S(2)}) async-start(bf16[8,128,384]{1,2,0:T(8,128)(2,1)} %copy.21), calls=%async_computation.1 | async-start | bytes 1572864 | tf_op jit(solution)/shard_map/all_to_all | solution.py:226
  116.5 7.3 %copy-start.10 = (bf16[8,128,1536]{2,1,0:T(8,128)(2,1)S(1)}, bf16[8,128,1536]{2,1,0:T(8,128)(2,1)}, u32[]{:S(2)}) copy-start(bf16[8,128,1536]{2,1,0:T(8,128)(2,1)} %get-tuple-element.10) | copy-start | bytes 9437188
  123.8 2.1 %copy-start.2 = (bf16[4,2,128,1536]{3,2,1,0:T(8,128)(2,1)S(1)}, bf16[4,2,128,1536]{3,2,1,0:T(8,128)(2,1)}, u32[]{:S(2)}) copy-start(bf16[4,2,128,1536]{3,2,1,0:T(8,128)(2,1)} %copy-done.1) | copy-start | bytes 9437188
  123.8 2.5 %copy-start.4 = (bf16[1024,1024]{1,0:T(8,128)(2,1)S(1)}, bf16[1024,1024]{1,0:T(8,128)(2,1)}, u32[]{:S(2)}) copy-start(bf16[1024,1024]{1,0:T(8,128)(2,1)} %constant_dynamic-update-slice_fusion) | copy-start | bytes 6291460
  125.6 10.8 %collective-permute-start.7 = (bf16[512,1536]{1,0:T(8,128)(2,1)S(1)}, bf16[512,1536]{1,0:T(8,128)(2,1)S(1)}, u32[]{:S(2)}, u32[]{:S(2)}) collective-permute-start(bf16[512,1536]{1,0:T(8,128)(2,1)S(1)} %convolution_convert_fusion.1), channel_id=1, source_target_pairs={{0,8},{8,0},{16,24},{24,16},{32,40},{40,32},{48,56},{56,48},{1,9},... | collective-permute-start | bytes 4718600 | tf_op jit(solution)/shard_map/ppermute | solution.py:121
  130.4 20.4 %collective-permute-start.26 = (bf16[192,1536]{1,0:T(8,128)(2,1)S(1)}, bf16[192,1536]{1,0:T(8,128)(2,1)S(1)}, u32[]{:S(2)}, u32[]{:S(2)}) collective-permute-start(bf16[192,1536]{1,0:T(8,128)(2,1)S(1)} %pad_maximum_fusion.5), channel_id=1, source_target_pairs={{0,64},{64,128},{128,192},{192,0},{1,65},{65,129},{129,193},{193,1... | collective-permute-start | bytes 1769480 | tf_op jit(solution)/shard_map/ppermute | solution.py:221
  132.1 28.6 %collective-permute-start.27 = (bf16[192,1536]{1,0:T(8,128)(2,1)S(1)}, bf16[192,1536]{1,0:T(8,128)(2,1)S(1)}, u32[]{:S(2)}, u32[]{:S(2)}) collective-permute-start(bf16[192,1536]{1,0:T(8,128)(2,1)S(1)} %pad_maximum_fusion.6), channel_id=1, source_target_pairs={{0,128},{64,192},{128,0},{192,64},{1,129},{65,193},{129,1},{193,65... | collective-permute-start | bytes 1769480 | tf_op jit(solution)/shard_map/ppermute | solution.py:221
  134.9 25.8 %collective-permute-start.28 = (bf16[192,1536]{1,0:T(8,128)(2,1)S(1)}, bf16[192,1536]{1,0:T(8,128)(2,1)S(1)}, u32[]{:S(2)}, u32[]{:S(2)}) collective-permute-start(bf16[192,1536]{1,0:T(8,128)(2,1)S(1)} %pad_maximum_fusion.7), channel_id=1, source_target_pairs={{0,192},{64,0},{128,64},{192,128},{1,193},{65,1},{129,65},{193,129... | collective-permute-start | bytes 1769480 | tf_op jit(solution)/shard_map/ppermute | solution.py:221
  138.2 27.6 %copy-start.6 = (f32[512,1536]{1,0:T(8,128)}, f32[512,1536]{1,0:T(8,128)S(1)}, u32[]{:S(2)}) copy-start(f32[512,1536]{1,0:T(8,128)S(1)} %get-tuple-element.60) | copy-start | bytes 9437188
  138.3 12.5 %collective-permute-start.8 = (bf16[128,768]{1,0:T(8,128)(2,1)S(1)}, bf16[128,768]{1,0:T(8,128)(2,1)S(1)}, u32[]{:S(2)}, u32[]{:S(2)}) collective-permute-start(bf16[128,768]{1,0:T(8,128)(2,1)S(1)} %get-tuple-element.48), channel_id=1, source_target_pairs={{0,16},{8,24},{16,32},{24,40},{32,48},{40,56},{48,0},{56,8},{1,17}... | collective-permute-start | bytes 589832 | tf_op jit(solution)/shard_map/ppermute | solution.py:121
  142.4 23.4 %collective-permute-start.10 = (bf16[128,768]{1,0:T(8,128)(2,1)S(1)}, bf16[128,768]{1,0:T(8,128)(2,1)S(1)}, u32[]{:S(2)}, u32[]{:S(2)}) collective-permute-start(bf16[128,768]{1,0:T(8,128)(2,1)S(1)} %get-tuple-element.51), channel_id=1, source_target_pairs={{0,48},{8,56},{16,0},{24,8},{32,16},{40,24},{48,32},{56,40},{1,49}... | collective-permute-start | bytes 589832 | tf_op jit(solution)/shard_map/ppermute | solution.py:121
  150.8 15.0 %collective-permute-start.12 = (bf16[128,768]{1,0:T(8,128)(2,1)S(1)}, bf16[128,768]{1,0:T(8,128)(2,1)S(1)}, u32[]{:S(2)}, u32[]{:S(2)}) collective-permute-start(bf16[128,768]{1,0:T(8,128)(2,1)S(1)} %get-tuple-element.49), channel_id=1, source_target_pairs={{0,48},{8,56},{16,0},{24,8},{32,16},{40,24},{48,32},{56,40},{1,49}... | collective-permute-start | bytes 589832 | tf_op jit(solution)/shard_map/ppermute | solution.py:121
  150.8 15.0 %collective-permute-start.9 = (bf16[128,768]{1,0:T(8,128)(2,1)S(1)}, bf16[128,768]{1,0:T(8,128)(2,1)S(1)}, u32[]{:S(2)}, u32[]{:S(2)}) collective-permute-start(bf16[128,768]{1,0:T(8,128)(2,1)S(1)} %fusion.23), channel_id=1, source_target_pairs={{0,16},{8,24},{16,32},{24,40},{32,48},{40,56},{48,0},{56,8},{1,17}... | collective-permute-start | bytes 589832 | tf_op jit(solution)/shard_map/ppermute | solution.py:121
  161.8 11.4 %collective-permute-start.11 = (bf16[128,768]{1,0:T(8,128)(2,1)S(1)}, bf16[128,768]{1,0:T(8,128)(2,1)S(1)}, u32[]{:S(2)}, u32[]{:S(2)}) collective-permute-start(bf16[128,768]{1,0:T(8,128)(2,1)S(1)} %get-tuple-element.50), channel_id=1, source_target_pairs={{0,16},{8,24},{16,32},{24,40},{32,48},{40,56},{48,0},{56,8},{1,17}... | collective-permute-start | bytes 589832 | tf_op jit(solution)/shard_map/ppermute | solution.py:121
  165.9 9.0 %collective-permute-start.13 = (bf16[128,768]{1,0:T(8,128)(2,1)S(1)}, bf16[128,768]{1,0:T(8,128)(2,1)S(1)}, u32[]{:S(2)}, u32[]{:S(2)}) collective-permute-start(bf16[128,768]{1,0:T(8,128)(2,1)S(1)} %get-tuple-element.39), channel_id=1, source_target_pairs={{0,48},{8,56},{16,0},{24,8},{32,16},{40,24},{48,32},{56,40},{1,49}... | collective-permute-start | bytes 589832 | tf_op jit(solution)/shard_map/ppermute | solution.py:121

commit v2 on v0

v2 whole, which is shorter than its diff:
```python
import math

import jax
import jax.numpy as jnp
from jax import lax
from jax.experimental import pallas as pl
from jax.experimental.pallas import tpu as pltpu
from jax.sharding import PartitionSpec as P

DH = 128
POS = 128
QB = 256
SCALE = 1.0 / math.sqrt(DH)
F32 = jnp.float32
BF16 = jnp.bfloat16
NT = (((1,), (1,)), ((), ()))
TN = (((0,), (0,)), ((), ()))

OWNERS = (0, 1, 2, 4, 5, 6)

SAME_Z = [[0, 1, 2, 3], [4, 5, 6, 7]]
ACROSS_Z = [(c, (c + 4) % 8) for c in range(8)]
ACROSS_CORE = [(r, r ^ 1) for r in range(8)]


def by_core(step):
    return [(2 * h + k, 2 * ((h + step * (1 - 2 * k)) % 4) + k) for h in range(4) for k in range(2)]


ARRAY = jax.ShapeDtypeStruct
IN_HBM = pltpu.HBM
HBM = pl.BlockSpec(memory_space=pltpu.HBM)
WHOLE = pl.BlockSpec(memory_space=pltpu.VMEM)


def local(kernel, name, outs, args, out_specs=None, in_specs=None, grid=(), scratch=(), after=(), flops=1024, vmem=56):
    count = len(args)

    def body(*refs):
        kernel(*refs[:count], *refs[count + len(after) :])

    return pl.pallas_call(
        body,
        out_shape=[kind(shape, dtype) for shape, dtype, kind in outs],
        grid=grid,
        in_specs=list(in_specs or [WHOLE] * count)
        + [pl.BlockSpec(memory_space=pl.ANY)] * len(after),
        out_specs=list(out_specs or [WHOLE] * len(outs)),
        scratch_shapes=list(scratch),
        compiler_params=pltpu.CompilerParams(vmem_limit_bytes=vmem * 1024 * 1024),
        cost_estimate=pl.CostEstimate(flops=flops, bytes_accessed=1024, transcendentals=0),
        name=name,
    )(*args, *after)


def pack_kernel(q, k, v, slots):
    for j, slot in enumerate(OWNERS):
        for i, a in enumerate((q, k, v)):
            slots[slot, :, i * DH : (i + 1) * DH] = a[:, j * DH : (j + 1) * DH]
    for slot in (3, 7):
        slots[slot] = jnp.zeros(slots.shape[1:], slots.dtype)


def unpack_kernel(slots, q, k, v):
    for j, slot in enumerate(OWNERS):
        for i, a in enumerate((q, k, v)):
            a[:, j * DH : (j + 1) * DH] = slots[slot, :, i * DH : (i + 1) * DH]


def attend_block(q, k, first):
    keys = k.shape[0]
    s = lax.dot_general(q, k, NT, preferred_element_type=F32) * SCALE
    rows = first + lax.broadcasted_iota(jnp.int32, (QB, keys), 0)
    cols = lax.broadcasted_iota(jnp.int32, (QB, keys), 1)
    s = jnp.where(rows >= cols, s, -jnp.inf)
    p = jnp.exp(s - jnp.max(s, axis=-1, keepdims=True))
    return p / jnp.sum(p, axis=-1, keepdims=True)


def forward_kernel(qkv, copies, ctx, sems):
    blocks = qkv.shape[0] // QB
    out = []
    for i in range(blocks):
        rows, seen = pl.ds(i * QB, QB), pl.ds(0, (i + 1) * QB)
        low = attend_block(qkv[rows, :DH], qkv[seen, DH : 2 * DH], i * QB).astype(BF16)
        ctx[rows, :] = jnp.dot(low, qkv[seen, 2 * DH :], preferred_element_type=F32).astype(BF16)
        for c in range(copies.shape[0]):
            out.append(
                pltpu.make_async_copy(ctx.at[rows, :], copies.at[c, rows, :], sems.at[i, c])
            )
            out[-1].start()
    for copy in out:
        copy.wait()


def backward_kernel(qkv, parts, out, dk, dv):
    blocks = qkv.shape[0] // QB
    step = pl.program_id(0)

    for i in reversed(range(blocks)):

        @pl.when(step == blocks - 1 - i)
        def _(i=i):
            rows, seen = pl.ds(i * QB, QB), pl.ds(0, (i + 1) * QB)
            q, k, v = qkv[rows, :DH], qkv[seen, DH : 2 * DH], qkv[seen, 2 * DH :]
            g = parts[0].astype(F32)
            for c in range(1, parts.shape[0]):
                g = g + parts[c].astype(F32)
            g = g.astype(BF16)
            attend = attend_block(q, k, i * QB)
            dp = lax.dot_general(g, v, NT, preferred_element_type=F32)
            dot = jnp.sum(attend * dp, axis=-1, keepdims=True)
            ds = (attend * (dp - dot) * SCALE).astype(BF16)
            out[rows, :DH] = jnp.dot(ds, k, preferred_element_type=F32).astype(BF16)
            dk_part = lax.dot_general(ds, q, TN, preferred_element_type=F32)
            dv_part = lax.dot_general(attend.astype(BF16), g, TN, preferred_element_type=F32)
            if i == blocks - 1:
                dk[...] = dk_part
                dv[...] = dv_part
            else:
                dk[seen, :] += dk_part
                dv[seen, :] += dv_part
            out[rows, DH : 2 * DH] = dk[rows, :].astype(BF16)
            out[rows, 2 * DH :] = dv[rows, :].astype(BF16)


def context_grad_kernel(grad_all, w, slots, token, part, sems):
    token[...] = jnp.zeros(token.shape, token.dtype)
    leave = []
    for j in range(0, 6, 2):
        both = lax.dot_general(
            grad_all[...], w[j * DH : (j + 2) * DH, :], NT, preferred_element_type=F32
        ).astype(BF16)
        for k in range(2):
            part[j + k] = both[:, k * DH : (k + 1) * DH]
            leave.append(
                pltpu.make_async_copy(part.at[j + k], slots.at[OWNERS[j + k]], sems.at[j + k])
            )
            leave[-1].start()
    for copy in leave:
        copy.wait()


def rows_for(ctx, h, core):
    first = [pl.multiple_of((2 * lax.rem(h + s, 4) + core) * POS, POS) for s in (2, 1, 3, 0)]
    return jnp.concatenate([ctx[pl.ds(f, POS), :] for f in first], axis=0)


def theirs_kernel(place, near, other, weight, ctx, left, right, w, sems_in, sems_w):
    h, core, z = place[0], place[1], place[2]
    wide = left.shape[1]
    lanes = [pl.ds(i * wide, wide) for i in range(2)]
    arrive = []
    for i, (blocks, zz) in enumerate(((near, z), (other, 1 - z))):
        for y in range(3):
            first = pl.multiple_of((3 * zz + y) * DH, DH)
            arrive.append(
                pltpu.make_async_copy(blocks.at[y], ctx.at[:, pl.ds(first, DH)], sems_in.at[i, y])
            )
    weights = [
        pltpu.make_async_copy(weight.at[:, lane], w.at[:, lane], sems_w.at[i])
        for i, lane in enumerate(lanes)
    ]
    for copy in arrive + weights:
        copy.start()
    for copy in arrive:
        copy.wait()
    rows = rows_for(ctx, h, 1 - core)
    for i, out in enumerate((left, right)):
        weights[i].wait()
        out[...] = jnp.dot(rows, w[:, lanes[i]], preferred_element_type=F32).astype(BF16)


def mine_kernel(place, ctx, w, left, right, far, now, later, own):
    h, core = place[0], place[1]
    rows = rows_for(ctx, h, core)
    wide = left.shape[1]
    for i, theirs in enumerate((left, right)):
        lane = pl.ds(i * wide, wide)
        part = jnp.dot(rows, w[:, lane], preferred_element_type=F32)
        part = part + theirs[...].astype(F32)
        far[:, lane] = part[:POS].astype(BF16)
        up, down = part[POS : 2 * POS], part[2 * POS : 3 * POS]
        now[:, lane] = jnp.where(core == 0, down, up).astype(BF16)
        later[:, lane] = jnp.where(core == 0, up, down)
        own[:, lane] = part[3 * POS :]


def add_kernel(a, *parts):
    total = a[...]
    for part in parts[:-1]:
        total = total + part[...].astype(F32)
    parts[-1][...] = total.astype(BF16)


def weight_kernel(ctx, grad_all, out, token):
    token[...] = jnp.zeros(token.shape, token.dtype)
    out[...] = lax.dot_general(
        ctx[...], grad_all[...], TN, preferred_element_type=F32
    ).astype(out.dtype)


def shards(queries, keys, values, weight, out_grad):
    feats = weight.shape[1]
    seq = 8 * POS
    width = 6 * DH
    steps = seq // QB
    row, col = lax.axis_index("row"), lax.axis_index("col")
    place = jnp.stack([row // 2, row % 2, col // 4]).astype(jnp.int32)
    on_row = lambda a, perm: lax.ppermute(a, "row", perm)
    scalars = pl.BlockSpec(memory_space=pltpu.SMEM)
    trade = lambda a: lax.all_to_all(a, "col", 0, 0, tiled=True)
    whole = lambda shape: pl.BlockSpec(shape, lambda i: (0,) * len(shape))
    lanes_of = lambda rows: pl.BlockSpec((rows, 512), lambda i: (0, i))

    grad_all = lax.all_gather(out_grad, "row", axis=0, tiled=True)

    (slots,) = local(
        pack_kernel, "pack_heads", [((8, POS, 3 * DH), BF16, IN_HBM)], (queries, keys, values)
    )
    qkv = trade(slots).reshape(seq, 3 * DH)

    (copies,) = local(
        forward_kernel,
        "attend_forward",
        [((4, seq, DH), BF16, IN_HBM)],
        (qkv,),
        out_specs=[HBM],
        scratch=[pltpu.VMEM((seq, DH), BF16), pltpu.SemaphoreType.DMA((steps, 4))],
    )
    near = lax.all_to_all(copies, "col", 0, 0, tiled=True, axis_index_groups=SAME_Z)
    other = lax.ppermute(near[:3], "col", ACROSS_Z)

    parts, token = local(
        context_grad_kernel,
        "context_grad",
        [((8, seq, DH), BF16, IN_HBM), ((8, DH), F32, ARRAY)],
        (grad_all, weight),
        out_specs=[HBM, WHOLE],
        scratch=[pltpu.VMEM((6, seq, DH), BF16), pltpu.SemaphoreType.DMA((6,))],
        vmem=24,
    )
    parts = trade(parts)

    ctx, *theirs = local(
        theirs_kernel,
        "project_theirs",
        [((seq, width), BF16, ARRAY)] + [((seq // 2, feats // 2), BF16, ARRAY)] * 2,
        (place, near, other, weight),
        in_specs=[scalars, HBM, HBM, HBM],
        scratch=[
            pltpu.VMEM((width, feats), BF16),
            pltpu.SemaphoreType.DMA((2, 3)),
            pltpu.SemaphoreType.DMA((2,)),
        ],
        after=[token],
        flops=60_000_000_000,
    )
    w_part, token = local(
        weight_kernel,
        "weight_grad",
        [((width, feats), BF16, ARRAY), ((8, DH), F32, ARRAY)],
        (ctx, grad_all),
        vmem=24,
        grid=(feats // 512,),
        in_specs=[whole((seq, width)), lanes_of(seq)],
        out_specs=[lanes_of(width), whole((8, DH))],
    )
    weight_grad = lax.psum_scatter(w_part, "depth", scatter_dimension=0, tiled=True)

    block = (POS, feats)
    far, now, later, own = local(
        mine_kernel,
        "project_mine",
        [(block, BF16, ARRAY), (block, BF16, ARRAY), (block, F32, ARRAY), (block, F32, ARRAY)],
        (place, ctx, weight, *[on_row(a, ACROSS_CORE) for a in theirs]),
        in_specs=[scalars] + [WHOLE] * 4,
        after=[token],
        vmem=24,
    )
    far = on_row(far, by_core(1))
    now = on_row(now, by_core(-1))
    (later,) = local(add_kernel, "add_output", [(block, BF16, ARRAY)], (later, far), flops=60_000_000_000, vmem=24)
    later = on_row(later, by_core(1))
    (output,) = local(
        add_kernel,
        "sum_output",
        [(block, BF16, ARRAY)],
        (own, now, later),
        vmem=24,
    )

    (back,) = local(
        backward_kernel,
        "attend_backward",
        [((seq, 3 * DH), BF16, IN_HBM)],
        (qkv, parts),
        after=[own],
        vmem=24,
        grid=(steps,),
        in_specs=[
            whole((seq, 3 * DH)),
            pl.BlockSpec((8, QB, DH), lambda i: (0, steps - 1 - i, 0)),
        ],
        out_specs=[whole((seq, 3 * DH))],
        scratch=[pltpu.VMEM((seq, DH), F32), pltpu.VMEM((seq, DH), F32)],
    )
    back = trade(back.reshape(8, POS, 3 * DH))
    grads = local(unpack_kernel, "unpack_heads", [((POS, width), BF16, ARRAY)] * 3, (back,), vmem=24)

    return output, grads[0], grads[1], grads[2], weight_grad


def solution(mesh):
    in_specs = (
        P(("depth", "col"), "row"),
        P(("depth", "col"), "row"),
        P(("depth", "col"), "row"),
        P("row", "col"),
        P(("depth", "row"), "col"),
    )
    out_specs = (
        P(("depth", "row"), "col"),
        P(("depth", "col"), "row"),
        P(("depth", "col"), "row"),
        P(("depth", "col"), "row"),
        P(("row", "depth"), "col"),
    )
    return jax.shard_map(shards, mesh=mesh, in_specs=in_specs, out_specs=out_specs, check_vma=False)
```

time: 569 us -> 140 us (0.25)
  waiting for transfers between devices: 454 us -> 29.2 us
  matrix products: 56.5 us -> 0 us
  Pallas kernels: 0 us -> 29.7 us
  starting transfers between devices: 0.36 us -> 20.2 us
  blocking collectives: 21.3 us -> 34.9 us
  other arithmetic: 6.46 us -> 0.59 us
    all_gather x4 -> x0, waiting for transfers between devices: 246 us -> none  [the longest x1 122 us: shards(): grad_every = lax.all_gather(grad_all, 'depth', axis=0, tiled=True)]
    reduce_scatter x4 -> x1, waiting for transfers between devices: 166 us -> 0.01 us  [shards(): lax.psum_scatter(w_part, 'depth', scatter_dimension=0, tiled=True)]
    dot_general x8 -> x0, matrix products: 52.1 us -> none  [the longest x1 10.5 us: shards(): jnp.einsum('hqk,qhd->khd', score_grad, query_heads, preferred_element_typ...]
    all_gather x1, waiting for transfers between devices: 39.7 us -> 4.95 us  [shards(): grad_all = lax.all_gather(out_grad, 'row', axis=0, tiled=True)]
    pallas_call x0 -> x10, Pallas kernels: none -> 29.7 us  [local(): pl.pallas_call(body, out_shape=[kind(shape, dtype) for shape, dtype, kind...]
    all_to_all x1 -> x2, blocking collectives: 21.3 us -> 34.9 us  [the longest x1 17.5 us: shards(): trade = lambda a: lax.all_to_all(a, 'col', 0, 0, tiled=True)]
    ppermute x0 -> x6, waiting for transfers between devices: none -> 12.9 us  [the longest x5 12.4 us: shards(): on_row = lambda a, perm: lax.ppermute(a, 'row', perm)]
    all_to_all x0 -> x2, starting transfers between devices: none -> 11.3 us  [shards(): trade = lambda a: lax.all_to_all(a, 'col', 0, 0, tiled=True)]
  transfers between devices with their start and end apart: 9 -> 10, of which waited for: 9 -> 4; matrix products, arithmetic and copies ran while one was open for 12% -> 1% of each run, Pallas kernels for 0% -> 21%
where the time goes in v2:
time: 140 us
  blocking collectives  34.9 us (25%)
  Pallas kernels  29.7 us (21%)
  waiting for transfers between devices  29.2 us (21%)
  starting transfers between devices  20.2 us (14%)
  between operations  14.1 us (10%)
  local copies, waits for them, and re-layouts  11.2 us (8%)
    pallas_call x10, Pallas kernels, local(): pl.pallas_call(body, out_shape=[kind(shape, dtype) for shape, dtype, kind...  29.7 us
    all_to_all x1, blocking collectives, shards(): trade = lambda a: lax.all_to_all(a, 'col', 0, 0, tiled=True)  17.5 us
    all_to_all x1, blocking collectives, shards(): lax.all_to_all(copies, 'col', 0, 0, tiled=True, axis_index_groups=SAME_Z)  17.5 us
    ppermute x5, waiting for transfers between devices, shards(): on_row = lambda a, perm: lax.ppermute(a, 'row', perm)  12.4 us
    all_to_all x2, starting transfers between devices, shards(): trade = lambda a: lax.all_to_all(a, 'col', 0, 0, tiled=True)  11.3 us
    all_to_all x2, waiting for transfers between devices, shards(): trade = lambda a: lax.all_to_all(a, 'col', 0, 0, tiled=True)  10.6 us
    unnamed x32, local copies, waits for them, and re-layouts  10.1 us
    ppermute x5, starting transfers between devices, shards(): on_row = lambda a, perm: lax.ppermute(a, 'row', perm)  7.8 us
  transfers between devices with their start and end apart: 10, of which 4 were waited for; matrix products, arithmetic and copies ran while one was open for 1% of the time, Pallas kernels for 21%

profile of v2, /device:TPU:8, one launch (start us, length us, event | category | flops | bytes accessed | tf_op | source)
XLA Modules:
  0.0 139.9 jit_solution(3063548862609902600)
XLA Ops:
  7.2 0.0 all-gather.2.cloned.1.call-start
  7.2 0.7 all-gather.2.cloned.1.call-update
  7.9 2.1 %pack_heads.1 = bf16[8,128,384]{2,1,0:T(8,128)(2,1)} custom-call(bf16[128,768]{1,0:T(8,128)(2,1)} %refs_0_.1, bf16[128,768]{1,0:T(8,128)(2,1)} %refs_1_.2, bf16[128,768]{1,0:T(8,128)(2,1)} %refs_2_.2), custom_call_target="tpu_custom_call" | custom-call | flops 1024 | bytes 1024 | tf_op jit(solution)/shard_map/pack_heads/pallas_call | solution.py:42
  10.0 17.5 %all_to_all.20 = bf16[8,128,384]{2,1,0:T(8,128)(2,1)} all-to-all(bf16[8,128,384]{2,1,0:T(8,128)(2,1)} %pack_heads.1), channel_id=1, replica_groups=mesh['depth'=4,'row'=8,'col'=8] {'col'}, dimensions={0} | all-to-all | bytes 1572864 | tf_op jit(solution)/shard_map/all_to_all | solution.py:212
  27.5 0.0 copy-start.2
  27.5 4.4 %attend_forward.1 = bf16[4,1024,128]{2,1,0:T(8,128)(2,1)} custom-call(bf16[1024,384]{1,0:T(8,128)(2,1)} %bitcast.5), custom_call_target="tpu_custom_call" | custom-call | flops 1024 | bytes 1024 | tf_op jit(solution)/shard_map/attend_forward/pallas_call | solution.py:42
  31.9 17.5 %all_to_all.21.refs_1_ = bf16[4,1024,128]{2,1,0:T(8,128)(2,1)S(1)} all-to-all(bf16[4,1024,128]{2,1,0:T(8,128)(2,1)} %attend_forward.1), channel_id=1, replica_groups={{0,1,2,3},{4,5,6,7},{8,9,10,11},{12,13,14,15},{16,17,18,19},{20,21,22,2..., dimensions={0} | all-to-all | bytes 2097152 | tf_op jit(solution)/shard_map/all_to_all | solution.py:231
  49.3 0.0 copy-start.15
  49.3 1.0 slice.4
  50.4 1.0 collective-permute-start
  51.4 0.6 pad_add_fusion.refs_0_
  52.0 5.0 %all-gather.2.cloned.1.call-done.refs_0_.refs_1_ = bf16[1024,1536]{1,0:T(8,128)(2,1)} async-done(((bf16[128,1536]{1,0:T(8,128)(2,1)}), bf16[1024,1536]{1,0:T(8,128)(2,1)}) %all-gather.2.cloned.1.call-update) | async-done | bytes 3145744 | tf_op jit(solution)/shard_map/all_gather | solution.py:216
  56.9 0.0 copy-done.2
  57.0 0.0 copy-start
  57.0 1.9 %copy-done = bf16[1024,1536]{1,0:T(8,128)(2,1)S(1)} copy-done((bf16[1024,1536]{1,0:T(8,128)(2,1)S(1)}, bf16[1024,1536]{1,0:T(8,128)(2,1)}, u32[]{:S(2)}) %copy-start) | copy-done | bytes 3145752
  58.8 3.7 %context_grad.1 = (bf16[8,1024,128]{2,1,0:T(8,128)(2,1)}, f32[8,128]{1,0:T(8,128)S(1)}) custom-call(bf16[1024,1536]{1,0:T(8,128)(2,1)S(1)} %copy-done, bf16[768,1536]{1,0:T(8,128)(2,1)S(1)} %copy-done.2), custom_call_target="tpu_custom_call" | custom-call | flops 1024 | bytes 1024 | tf_op jit(solution)/shard_map/context_grad/pallas_call | solution.py:42
  62.5 0.0 copy-done.15
  62.6 0.0 copy-start.14
  62.6 0.6 copy-done.14
  63.1 6.5 %all-to-all-start.2 = ((bf16[8,1024,128]{2,1,0:T(8,128)(2,1)}), bf16[8,1024,128]{2,1,0:T(8,128)(2,1)S(1)}, u32[]{:S(2)}, u32[]{:S(2)}) async-start(bf16[8,1024,128]{2,1,0:T(8,128)(2,1)} %get-tuple-element.28), calls=%async_computation.2 | async-start | bytes 4194304 | tf_op jit(solution)/shard_map/all_to_all | solution.py:212
  69.6 0.0 reduce-scatter.2.cloned.1.call-start
  69.6 0.5 collective-permute-done.refs_2_
  70.1 0.0 copy-start.1
  70.1 5.6 %project_theirs.1 = (bf16[1024,768]{1,0:T(8,128)(2,1)}, bf16[512,768]{1,0:T(8,128)(2,1)}, bf16[512,768]{1,0:T(8,128)(2,1)}) custom-call(s32[3]{0:T(128)} %pad_add_fusion.refs_0_, bf16[4,1024,128]{2,1,0:T(8,128)(2,1)} %copy-done.15, bf16[3,1024,128]{2,1,0:T(8,128)(2,1)} %collective-permute-done.refs_2_, bf16[768,1536]{1,0:T(8,128)(2,1)} %refs_2_.3, ...), custom_call_target="tpu_custom_call" | custom-call | flops 60000002048 | bytes 1024 | tf_op jit(solution)/shard_map/project_theirs/pallas_call | solution.py:42
  75.7 0.1 collective-permute-start.1
  75.8 0.5 collective-permute-start.2
  76.3 0.0 copy-done.1
  76.3 0.0 copy-start.5
  76.4 1.4 %copy-done.5 = bf16[1024,768]{1,0:T(8,128)(2,1)S(1)} copy-done((bf16[1024,768]{1,0:T(8,128)(2,1)S(1)}, bf16[1024,768]{1,0:T(8,128)(2,1)}, u32[]{:S(2)}) %copy-start.5) | copy-done | bytes 1572888
  77.8 0.0 copy-start.3
  77.8 0.0 copy-start.10
  77.8 3.4 %weight_grad.1 = (bf16[768,1536]{1,0:T(8,128)(2,1)S(1)}, f32[8,128]{1,0:T(8,128)S(1)}) custom-call(bf16[1024,768]{1,0:T(8,128)(2,1)S(1)} %copy-done.5, bf16[1024,1536]{1,0:T(8,128)(2,1)S(1)} %copy-done.1), custom_call_target="tpu_custom_call" | custom-call | flops 1024 | bytes 1024 | tf_op jit(solution)/shard_map/weight_grad/pallas_call | solution.py:42
  81.2 0.0 copy-start.9
  81.2 1.4 %copy-done.9 = bf16[768,1536]{1,0:T(8,128)(2,1)} copy-done((bf16[768,1536]{1,0:T(8,128)(2,1)}, bf16[768,1536]{1,0:T(8,128)(2,1)S(1)}, u32[]{:S(2)}) %copy-start.9) | copy-done | bytes 2359320
  82.6 0.0 collective-permute-done.1.refs_3_
  82.6 0.0 collective-permute-done.2.refs_4_
  82.6 0.0 copy-done.3
  82.6 0.0 copy-done.10
  82.6 2.6 %project_mine.1 = (bf16[128,1536]{1,0:T(8,128)(2,1)}, bf16[128,1536]{1,0:T(8,128)(2,1)S(1)}, f32[128,1536]{1,0:T(8,128)S(1)}, f32[128,1536]{1,0:T(8,128)S(1)}) custom-call(s32[3]{0:T(128)S(1)} %copy-done.10, bf16[1024,768]{1,0:T(8,128)(2,1)S(1)} %copy-done.5, bf16[768,1536]{1,0:T(8,128)(2,1)S(1)} %copy-done.3, ...), custom_call_target="tpu_custom_call" | custom-call | flops 1024 | bytes 1024 | tf_op jit(solution)/shard_map/project_mine/pallas_call | solution.py:42
  85.2 0.0 copy-start.6
  85.2 0.9 copy-done.6
  86.1 0.0 copy-start.11
  86.1 0.9 copy-done.11
  87.0 0.0 copy-start.13
  87.0 0.8 copy-done.13
  87.8 0.0 copy-start.4
  87.8 3.2 %collective-permute-start.4 = (bf16[128,1536]{1,0:T(8,128)(2,1)}, bf16[128,1536]{1,0:T(8,128)(2,1)}, u32[]{:S(2)}, u32[]{:S(2)}) collective-permute-start(bf16[128,1536]{1,0:T(8,128)(2,1)} %get-tuple-element.27), channel_id=1, source_target_pairs={{0,16},{8,56},{16,32},{24,8},{32,48},{40,24},{48,0},{56,40},{1,17}... | collective-permute-start | bytes 1179656 | tf_op jit(solution)/shard_map/ppermute | solution.py:210
  91.0 0.0 reduce-scatter.2.cloned.1.call-update
  91.0 2.2 %collective-permute-start.3 = (bf16[128,1536]{1,0:T(8,128)(2,1)}, bf16[128,1536]{1,0:T(8,128)(2,1)S(1)}, u32[]{:S(2)}, u32[]{:S(2)}) collective-permute-start(bf16[128,1536]{1,0:T(8,128)(2,1)} %copy-done.13), channel_id=1, source_target_pairs={{0,48},{8,24},{16,0},{24,40},{32,16},{40,56},{48,32},{56,8},{1,49}... | collective-permute-start | bytes 1179656 | tf_op jit(solution)/shard_map/ppermute | solution.py:210
  93.2 10.6 %all-to-all-done.2.refs_1_ = bf16[8,1024,128]{2,1,0:T(8,128)(2,1)S(1)} async-done(((bf16[8,1024,128]{2,1,0:T(8,128)(2,1)}), bf16[8,1024,128]{2,1,0:T(8,128)(2,1)S(1)}, u32[]{:S(2)}, u32[]{:S(2)}) %all-to-all-start.2) | async-done | bytes 2097184 | tf_op jit(solution)/shard_map/all_to_all | solution.py:212
  103.8 0.0 copy-done.4
  103.8 1.1 copy-done.7
  104.9 5.0 %attend_backward.1 = bf16[1024,384]{1,0:T(8,128)(2,1)} custom-call(bf16[1024,384]{1,0:T(8,128)(2,1)S(1)} %bitcast.6, bf16[8,1024,128]{2,1,0:T(8,128)(2,1)S(1)} %all-to-all-done.2.refs_1_, f32[128,1536]{1,0:T(8,128)S(1)} %copy-done.7), custom_call_target="tpu_custom_call" | custom-call | flops 1024 | bytes 1024 | tf_op jit(solution)/shard_map/attend_backward/pallas_call | solution.py:42
  110.0 4.8 %all-to-all-start.3 = ((bf16[8,128,384]{2,1,0:T(8,128)(2,1)}), bf16[8,128,384]{2,1,0:T(8,128)(2,1)S(1)}, u32[]{:S(2)}, u32[]{:S(2)}) async-start(bf16[8,128,384]{2,1,0:T(8,128)(2,1)} %bitcast.7), calls=%async_computation.3 | async-start | bytes 1572864 | tf_op jit(solution)/shard_map/all_to_all | solution.py:212
  114.8 0.0 collective-permute-done.4.refs_1_
  114.8 1.1 copy-done.12
  115.9 1.1 add_output.1
  117.1 1.8 %collective-permute-start.5 = (bf16[128,1536]{1,0:T(8,128)(2,1)S(1)}, bf16[128,1536]{1,0:T(8,128)(2,1)S(1)}, u32[]{:S(2)}, u32[]{:S(2)}) collective-permute-start(bf16[128,1536]{1,0:T(8,128)(2,1)S(1)} %add_output.1), channel_id=1, source_target_pairs={{0,16},{8,56},{16,32},{24,8},{32,48},{40,24},{48,0},{56,40},{1,17}... | collective-permute-start | bytes 1179656 | tf_op jit(solution)/shard_map/ppermute | solution.py:210
  118.9 0.0 collective-permute-done.3.refs_1_
  118.9 12.4 %collective-permute-done.5.refs_2_ = bf16[128,1536]{1,0:T(8,128)(2,1)S(1)} collective-permute-done((bf16[128,1536]{1,0:T(8,128)(2,1)S(1)}, bf16[128,1536]{1,0:T(8,128)(2,1)S(1)}, u32[]{:S(2)}, u32[]{:S(2)}) %collective-permute-start.5) | collective-permute-done | bytes 393248 | tf_op jit(solution)/shard_map/ppermute | solution.py:210
  131.3 0.0 copy-done.8
  131.3 0.9 sum_output.1
  132.1 0.0 all-to-all-done.3.refs_0_
  132.1 0.9 unpack_heads.1
  (4 shorter events, 0.0 us)
Async XLA Ops:
  7.2 49.8 %all-gather.2.cloned.1.call-start = ((), (), s32[]{:S(2)}) async-start(), calls=%async_computation.5 | async-start | bytes 3538944 | tf_op jit(solution)/shard_map/all_gather | solution.py:216
  27.5 29.5 %copy-start.2 = (bf16[768,1536]{1,0:T(8,128)(2,1)S(1)}, bf16[768,1536]{1,0:T(8,128)(2,1)}, u32[]{:S(2)}) copy-start(bf16[768,1536]{1,0:T(8,128)(2,1)} %refs_2_.3) | copy-start | bytes 7077892
  49.3 13.2 %copy-start.15 = (bf16[4,1024,128]{2,1,0:T(8,128)(2,1)}, bf16[4,1024,128]{2,1,0:T(8,128)(2,1)S(1)}, u32[]{:S(2)}) copy-start(bf16[4,1024,128]{2,1,0:T(8,128)(2,1)S(1)} %all_to_all.21.refs_1_) | copy-start | bytes 3145732
  50.4 19.8 %collective-permute-start = (bf16[3,1024,128]{2,1,0:T(8,128)(2,1)}, bf16[3,1024,128]{2,1,0:T(8,128)(2,1)}, u32[]{:S(2)}, u32[]{:S(2)}) collective-permute-start(bf16[3,1024,128]{2,1,0:T(8,128)(2,1)} %slice.4), channel_id=1, source_target_pairs={{0,4},{1,5},{2,6},{3,7},{4,0},{5,1},{6,2},{7,3},{8,12},{9,13},{10,... | collective-permute-start | bytes 2359304 | tf_op jit(solution)/shard_map/ppermute | solution.py:232
  57.0 1.9 %copy-start = (bf16[1024,1536]{1,0:T(8,128)(2,1)S(1)}, bf16[1024,1536]{1,0:T(8,128)(2,1)}, u32[]{:S(2)}) copy-start(bf16[1024,1536]{1,0:T(8,128)(2,1)} %all-gather.2.cloned.1.call-done.refs_0_.refs_1_) | copy-start | bytes 9437188
  62.6 0.6 copy-start.14
  63.1 40.7 %all-to-all-start.2 = ((bf16[8,1024,128]{2,1,0:T(8,128)(2,1)}), bf16[8,1024,128]{2,1,0:T(8,128)(2,1)S(1)}, u32[]{:S(2)}, u32[]{:S(2)}) async-start(bf16[8,1024,128]{2,1,0:T(8,128)(2,1)} %get-tuple-element.28), calls=%async_computation.2 | async-start | bytes 4194304 | tf_op jit(solution)/shard_map/all_to_all | solution.py:212
  69.6 63.4 %reduce-scatter.2.cloned.1.call-start = ((), (), s32[]{:S(2)}) async-start(), calls=%async_computation.6 | async-start | bytes 2949120 | tf_op jit(solution)/shard_map/reduce_scatter | solution.py:269
  70.1 6.2 %copy-start.1 = (bf16[1024,1536]{1,0:T(8,128)(2,1)S(1)}, bf16[1024,1536]{1,0:T(8,128)(2,1)}, u32[]{:S(2)}) copy-start(bf16[1024,1536]{1,0:T(8,128)(2,1)} %all-gather.2.cloned.1.call-done.refs_0_.refs_1_) | copy-start | bytes 9437188
  75.7 6.8 %collective-permute-start.1 = (bf16[512,768]{1,0:T(8,128)(2,1)}, bf16[512,768]{1,0:T(8,128)(2,1)S(1)}, u32[]{:S(2)}, u32[]{:S(2)}) collective-permute-start(bf16[512,768]{1,0:T(8,128)(2,1)} %get-tuple-element.21), channel_id=1, source_target_pairs={{0,8},{8,0},{16,24},{24,16},{32,40},{40,32},{48,56},{56,48},{1,9},... | collective-permute-start | bytes 2359304 | tf_op jit(solution)/shard_map/ppermute | solution.py:210
  75.8 6.7 %collective-permute-start.2 = (bf16[512,768]{1,0:T(8,128)(2,1)}, bf16[512,768]{1,0:T(8,128)(2,1)S(1)}, u32[]{:S(2)}, u32[]{:S(2)}) collective-permute-start(bf16[512,768]{1,0:T(8,128)(2,1)} %get-tuple-element.22), channel_id=1, source_target_pairs={{0,8},{8,0},{16,24},{24,16},{32,40},{40,32},{48,56},{56,48},{1,9},... | collective-permute-start | bytes 2359304 | tf_op jit(solution)/shard_map/ppermute | solution.py:210
  76.3 1.4 %copy-start.5 = (bf16[1024,768]{1,0:T(8,128)(2,1)S(1)}, bf16[1024,768]{1,0:T(8,128)(2,1)}, u32[]{:S(2)}) copy-start(bf16[1024,768]{1,0:T(8,128)(2,1)} %get-tuple-element.20.refs_0_.refs_1_) | copy-start | bytes 4718596
  77.8 4.8 %copy-start.3 = (bf16[768,1536]{1,0:T(8,128)(2,1)S(1)}, bf16[768,1536]{1,0:T(8,128)(2,1)}, u32[]{:S(2)}) copy-start(bf16[768,1536]{1,0:T(8,128)(2,1)} %refs_2_.3) | copy-start | bytes 7077892
  77.8 4.8 %copy-start.10 = (s32[3]{0:T(128)S(1)}, s32[3]{0:T(128)}, u32[]{:S(2)}) copy-start(s32[3]{0:T(128)} %pad_add_fusion.refs_0_) | copy-start | bytes 40
  81.2 1.4 %copy-start.9 = (bf16[768,1536]{1,0:T(8,128)(2,1)}, bf16[768,1536]{1,0:T(8,128)(2,1)S(1)}, u32[]{:S(2)}) copy-start(bf16[768,1536]{1,0:T(8,128)(2,1)S(1)} %get-tuple-element.32) | copy-start | bytes 7077892
  85.2 0.9 copy-start.6
  86.1 0.9 copy-start.11
  87.0 0.8 copy-start.13
  87.8 16.0 %copy-start.4 = (bf16[8,128,384]{2,1,0:T(8,128)(2,1)S(1)}, bf16[8,128,384]{2,1,0:T(8,128)(2,1)}, u32[]{:S(2)}) copy-start(bf16[8,128,384]{2,1,0:T(8,128)(2,1)} %all_to_all.20) | copy-start | bytes 2359300
  87.8 27.0 %collective-permute-start.4 = (bf16[128,1536]{1,0:T(8,128)(2,1)}, bf16[128,1536]{1,0:T(8,128)(2,1)}, u32[]{:S(2)}, u32[]{:S(2)}) collective-permute-start(bf16[128,1536]{1,0:T(8,128)(2,1)} %get-tuple-element.27), channel_id=1, source_target_pairs={{0,16},{8,56},{16,32},{24,8},{32,48},{40,24},{48,0},{56,40},{1,17}... | collective-permute-start | bytes 1179656 | tf_op jit(solution)/shard_map/ppermute | solution.py:210
  91.0 27.9 %collective-permute-start.3 = (bf16[128,1536]{1,0:T(8,128)(2,1)}, bf16[128,1536]{1,0:T(8,128)(2,1)S(1)}, u32[]{:S(2)}, u32[]{:S(2)}) collective-permute-start(bf16[128,1536]{1,0:T(8,128)(2,1)} %copy-done.13), channel_id=1, source_target_pairs={{0,48},{8,24},{16,0},{24,40},{32,16},{40,56},{48,32},{56,8},{1,49}... | collective-permute-start | bytes 1179656 | tf_op jit(solution)/shard_map/ppermute | solution.py:210
  103.8 1.1 copy-start.7
  110.0 22.2 %all-to-all-start.3 = ((bf16[8,128,384]{2,1,0:T(8,128)(2,1)}), bf16[8,128,384]{2,1,0:T(8,128)(2,1)S(1)}, u32[]{:S(2)}, u32[]{:S(2)}) async-start(bf16[8,128,384]{2,1,0:T(8,128)(2,1)} %bitcast.7), calls=%async_computation.3 | async-start | bytes 1572864 | tf_op jit(solution)/shard_map/all_to_all | solution.py:212
  114.8 1.1 copy-start.12
  115.9 15.4 %copy-start.8 = (f32[128,1536]{1,0:T(8,128)S(1)}, f32[128,1536]{1,0:T(8,128)}, u32[]{:S(2)}) copy-start(f32[128,1536]{1,0:T(8,128)} %copy-done.6) | copy-start | bytes 2359300
  117.1 14.2 %collective-permute-start.5 = (bf16[128,1536]{1,0:T(8,128)(2,1)S(1)}, bf16[128,1536]{1,0:T(8,128)(2,1)S(1)}, u32[]{:S(2)}, u32[]{:S(2)}) collective-permute-start(bf16[128,1536]{1,0:T(8,128)(2,1)S(1)} %add_output.1), channel_id=1, source_target_pairs={{0,16},{8,56},{16,32},{24,8},{32,48},{40,24},{48,0},{56,40},{1,17}... | collective-permute-start | bytes 1179656 | tf_op jit(solution)/shard_map/ppermute | solution.py:210
Sparse Core Ops, SparseCore 0:
  9.8 47.0 all-gather.1
  91.1 34.1 reduce-scatter.1

commit v3 on v2

--- a/solution.py
+++ b/solution.py
@@ -111,7 +111,7 @@
             dp = lax.dot_general(g, v, NT, preferred_element_type=F32)
             dot = jnp.sum(attend * dp, axis=-1, keepdims=True)
             ds = (attend * (dp - dot) * SCALE).astype(BF16)
-            out[rows, :DH] = jnp.dot(ds, k, preferred_element_type=F32).astype(BF16)
+            out[:, :DH] = jnp.dot(ds, k, preferred_element_type=F32).astype(BF16)
             dk_part = lax.dot_general(ds, q, TN, preferred_element_type=F32)
             dv_part = lax.dot_general(attend.astype(BF16), g, TN, preferred_element_type=F32)
             if i == blocks - 1:
@@ -120,8 +120,8 @@
             else:
                 dk[seen, :] += dk_part
                 dv[seen, :] += dv_part
-            out[rows, DH : 2 * DH] = dk[rows, :].astype(BF16)
-            out[rows, 2 * DH :] = dv[rows, :].astype(BF16)
+            out[:, DH : 2 * DH] = dk[rows, :].astype(BF16)
+            out[:, 2 * DH :] = dv[rows, :].astype(BF16)
 
 
 def context_grad_kernel(grad_all, w, slots, token, part, sems):
@@ -171,7 +171,8 @@
         out[...] = jnp.dot(rows, w[:, lanes[i]], preferred_element_type=F32).astype(BF16)
 
 
-def mine_kernel(place, ctx, w, left, right, far, now, later, own):
+def mine_kernel(place, ctx, w, left, right, far, now, later, own, token):
+    token[...] = jnp.zeros(token.shape, token.dtype)
     h, core = place[0], place[1]
     rows = rows_for(ctx, h, core)
     wide = left.shape[1]
@@ -255,27 +256,17 @@
         ],
         after=[token],
         flops=60_000_000_000,
-    )
-    w_part, token = local(
-        weight_kernel,
-        "weight_grad",
-        [((width, feats), BF16, ARRAY), ((8, DH), F32, ARRAY)],
-        (ctx, grad_all),
-        vmem=24,
-        grid=(feats // 512,),
-        in_specs=[whole((seq, width)), lanes_of(seq)],
-        out_specs=[lanes_of(width), whole((8, DH))],
-    )
-    weight_grad = lax.psum_scatter(w_part, "depth", scatter_dimension=0, tiled=True)
-
+        vmem=24,
+    )
     block = (POS, feats)
-    far, now, later, own = local(
+    far, now, later, own, token = local(
         mine_kernel,
         "project_mine",
-        [(block, BF16, ARRAY), (block, BF16, ARRAY), (block, F32, ARRAY), (block, F32, ARRAY)],
+        [(block, BF16, ARRAY)] * 2
+        + [(block, F32, IN_HBM)] * 2
+        + [((8, DH), F32, ARRAY)],
         (place, ctx, weight, *[on_row(a, ACROSS_CORE) for a in theirs]),
         in_specs=[scalars] + [WHOLE] * 4,
-        after=[token],
         vmem=24,
     )
     far = on_row(far, by_core(1))
@@ -290,19 +281,32 @@
         vmem=24,
     )
 
+    w_part, token = local(
+        weight_kernel,
+        "weight_grad",
+        [((width, feats), BF16, IN_HBM), ((8, DH), F32, ARRAY)],
+        (ctx, grad_all),
+        after=[token],
+        vmem=24,
+        grid=(feats // 512,),
+        in_specs=[whole((seq, width)), lanes_of(seq)],
+        out_specs=[lanes_of(width), whole((8, DH))],
+    )
+    weight_grad = lax.psum_scatter(w_part, "depth", scatter_dimension=0, tiled=True)
+
     (back,) = local(
         backward_kernel,
         "attend_backward",
         [((seq, 3 * DH), BF16, IN_HBM)],
         (qkv, parts),
-        after=[own],
+        after=[token],
         vmem=24,
         grid=(steps,),
         in_specs=[
             whole((seq, 3 * DH)),
             pl.BlockSpec((8, QB, DH), lambda i: (0, steps - 1 - i, 0)),
         ],
-        out_specs=[whole((seq, 3 * DH))],
+        out_specs=[pl.BlockSpec((QB, 3 * DH), lambda i: (steps - 1 - i, 0))],
         scratch=[pltpu.VMEM((seq, DH), F32), pltpu.VMEM((seq, DH), F32)],
     )
     back = trade(back.reshape(8, POS, 3 * DH))

time: 140 us -> 141 us (level)
  waiting for transfers between devices: 29.2 us -> 39 us
  local copies, waits for them, and re-layouts: 11.2 us -> 2.91 us
    unnamed x32 -> x12, local copies, waits for them, and re-layouts: 10.1 us -> 1.91 us
    ppermute x5, waiting for transfers between devices: 12.4 us -> 19 us  [shards(): on_row = lambda a, perm: lax.ppermute(a, 'row', perm)]
    all_to_all x2, waiting for transfers between devices: 10.6 us -> 12.6 us  [shards(): trade = lambda a: lax.all_to_all(a, 'col', 0, 0, tiled=True)]
  transfers between devices with their start and end apart: 10 -> 10, of which waited for: 4 -> 6; matrix products, arithmetic and copies ran while one was open for 1% -> 1% of each run, Pallas kernels for 21% -> 21%
where the time goes in v3:
time: 141 us
  waiting for transfers between devices  39 us (28%)
  blocking collectives  35 us (25%)
  Pallas kernels  29.3 us (21%)
  starting transfers between devices  20.5 us (15%)
  between operations  14.1 us (10%)
  local copies, waits for them, and re-layouts  2.91 us (2%)
    pallas_call x10, Pallas kernels, local(): pl.pallas_call(body, out_shape=[kind(shape, dtype) for shape, dtype, kind...  29.3 us
    ppermute x5, waiting for transfers between devices, shards(): on_row = lambda a, perm: lax.ppermute(a, 'row', perm)  19 us
    all_to_all x1, blocking collectives, shards(): lax.all_to_all(copies, 'col', 0, 0, tiled=True, axis_index_groups=SAME_Z)  17.5 us
    all_to_all x1, blocking collectives, shards(): trade = lambda a: lax.all_to_all(a, 'col', 0, 0, tiled=True)  17.5 us
    all_to_all x2, waiting for transfers between devices, shards(): trade = lambda a: lax.all_to_all(a, 'col', 0, 0, tiled=True)  12.6 us
    all_to_all x2, starting transfers between devices, shards(): trade = lambda a: lax.all_to_all(a, 'col', 0, 0, tiled=True)  11.3 us
    ppermute x5, starting transfers between devices, shards(): on_row = lambda a, perm: lax.ppermute(a, 'row', perm)  8.07 us
    all_gather x1, waiting for transfers between devices, shards(): grad_all = lax.all_gather(out_grad, 'row', axis=0, tiled=True)  5.47 us
  transfers between devices with their start and end apart: 10, of which 6 were waited for; matrix products, arithmetic and copies ran while one was open for 1% of the time, Pallas kernels for 21%

profile of v3, /device:TPU:8, one launch (start us, length us, event | category | flops | bytes accessed | tf_op | source)
XLA Modules:
  0.0 140.8 jit_solution(10937952154531197188)
XLA Ops:
  7.2 0.0 all-gather.2.cloned.1.call-start
  7.2 0.7 all-gather.2.cloned.1.call-update
  7.9 2.1 %pack_heads.1 = bf16[8,128,384]{2,1,0:T(8,128)(2,1)} custom-call(bf16[128,768]{1,0:T(8,128)(2,1)} %refs_0_.1, bf16[128,768]{1,0:T(8,128)(2,1)} %refs_1_.2, bf16[128,768]{1,0:T(8,128)(2,1)} %refs_2_.2), custom_call_target="tpu_custom_call" | custom-call | flops 1024 | bytes 1024 | tf_op jit(solution)/shard_map/pack_heads/pallas_call | solution.py:42
  10.0 17.5 %all_to_all.20 = bf16[8,128,384]{2,1,0:T(8,128)(2,1)} all-to-all(bf16[8,128,384]{2,1,0:T(8,128)(2,1)} %pack_heads.1), channel_id=1, replica_groups=mesh['depth'=4,'row'=8,'col'=8] {'col'}, dimensions={0} | all-to-all | bytes 1572864 | tf_op jit(solution)/shard_map/all_to_all | solution.py:213
  27.5 0.0 copy-start.2
  27.5 4.4 %attend_forward.1 = bf16[4,1024,128]{2,1,0:T(8,128)(2,1)} custom-call(bf16[1024,384]{1,0:T(8,128)(2,1)} %bitcast.5), custom_call_target="tpu_custom_call" | custom-call | flops 1024 | bytes 1024 | tf_op jit(solution)/shard_map/attend_forward/pallas_call | solution.py:42
  31.9 17.5 %all_to_all.21.refs_1_ = bf16[4,1024,128]{2,1,0:T(8,128)(2,1)S(1)} all-to-all(bf16[4,1024,128]{2,1,0:T(8,128)(2,1)} %attend_forward.1), channel_id=1, replica_groups={{0,1,2,3},{4,5,6,7},{8,9,10,11},{12,13,14,15},{16,17,18,19},{20,21,22,2..., dimensions={0} | all-to-all | bytes 2097152 | tf_op jit(solution)/shard_map/all_to_all | solution.py:232
  49.4 1.0 slice.4
  50.4 1.0 collective-permute-start
  51.4 0.1 pad_add_fusion.refs_0_
  51.5 5.5 %all-gather.2.cloned.1.call-done.refs_0_.refs_1_ = bf16[1024,1536]{1,0:T(8,128)(2,1)} async-done(((bf16[128,1536]{1,0:T(8,128)(2,1)}), bf16[1024,1536]{1,0:T(8,128)(2,1)}) %all-gather.2.cloned.1.call-update) | async-done | bytes 3145744 | tf_op jit(solution)/shard_map/all_gather | solution.py:217
  57.0 0.0 copy-done.2
  57.0 0.0 copy-start
  57.0 1.9 %copy-done = bf16[1024,1536]{1,0:T(8,128)(2,1)S(1)} copy-done((bf16[1024,1536]{1,0:T(8,128)(2,1)S(1)}, bf16[1024,1536]{1,0:T(8,128)(2,1)}, u32[]{:S(2)}) %copy-start) | copy-done | bytes 3145752
  58.9 3.7 %context_grad.1 = (bf16[8,1024,128]{2,1,0:T(8,128)(2,1)}, f32[8,128]{1,0:T(8,128)S(1)}) custom-call(bf16[1024,1536]{1,0:T(8,128)(2,1)S(1)} %copy-done, bf16[768,1536]{1,0:T(8,128)(2,1)S(1)} %copy-done.2), custom_call_target="tpu_custom_call" | custom-call | flops 1024 | bytes 1024 | tf_op jit(solution)/shard_map/context_grad/pallas_call | solution.py:42
  62.5 6.5 %all-to-all-start.2 = ((bf16[8,1024,128]{2,1,0:T(8,128)(2,1)}), bf16[8,1024,128]{2,1,0:T(8,128)(2,1)}, u32[]{:S(2)}, u32[]{:S(2)}) async-start(bf16[8,1024,128]{2,1,0:T(8,128)(2,1)} %get-tuple-element.28), calls=%async_computation.2 | async-start | bytes 4194304 | tf_op jit(solution)/shard_map/all_to_all | solution.py:213
  69.0 0.0 reduce-scatter.2.cloned.1.call-start
  69.0 1.1 collective-permute-done.refs_2_
  70.1 3.8 %project_theirs.1 = (bf16[1024,768]{1,0:T(8,128)(2,1)S(1)}, bf16[512,768]{1,0:T(8,128)(2,1)S(1)}, bf16[512,768]{1,0:T(8,128)(2,1)S(1)}) custom-call(s32[3]{0:T(128)S(1)} %pad_add_fusion.refs_0_, bf16[4,1024,128]{2,1,0:T(8,128)(2,1)S(1)} %all_to_all.21.refs_1_, bf16[3,1024,128]{2,1,0:T(8,128)(2,1)} %collective-permute-done.refs_2_, ...), custom_call_target="tpu_custom_call" | custom-call | flops 60000002048 | bytes 1024 | tf_op jit(solution)/shard_map/project_theirs/pallas_call | solution.py:42
  74.0 0.1 collective-permute-start.1
  74.1 0.5 collective-permute-start.2
  74.6 1.8 %collective-permute-done.1.refs_3_ = bf16[512,768]{1,0:T(8,128)(2,1)S(1)} collective-permute-done((bf16[512,768]{1,0:T(8,128)(2,1)S(1)}, bf16[512,768]{1,0:T(8,128)(2,1)S(1)}, u32[]{:S(2)}, u32[]{:S(2)}) %collective-permute-start.1) | collective-permute-done | bytes 786464 | tf_op jit(solution)/shard_map/ppermute | solution.py:211
  76.4 1.1 collective-permute-done.2.refs_4_
  77.5 0.0 copy-start.1
  77.5 3.2 %project_mine.1 = (bf16[128,1536]{1,0:T(8,128)(2,1)S(1)}, bf16[128,1536]{1,0:T(8,128)(2,1)S(1)}, f32[128,1536]{1,0:T(8,128)}, f32[128,1536]{1,0:T(8,128)}, f32[8,128]{1,0:T(8,128)S(1)}) custom-call(s32[3]{0:T(128)S(1)} %pad_add_fusion.refs_0_, bf16[1024,768]{1,0:T(8,128)(2,1)S(1)} %get-tuple-element.21.refs_1_.refs_0_, bf16[768,1536]{1,0:T(8,128)(2,1)S(1)} %copy-done.2, ...), custom_call_target="tpu_custom_call" | custom-call | flops 1024 | bytes 1024 | tf_op jit(solution)/shard_map/project_mine/pallas_call | solution.py:42
  80.7 3.5 %collective-permute-start.4 = (bf16[128,1536]{1,0:T(8,128)(2,1)S(1)}, bf16[128,1536]{1,0:T(8,128)(2,1)S(1)}, u32[]{:S(2)}, u32[]{:S(2)}) collective-permute-start(bf16[128,1536]{1,0:T(8,128)(2,1)S(1)} %get-tuple-element.27), channel_id=1, source_target_pairs={{0,16},{8,56},{16,32},{24,8},{32,48},{40,24},{48,0},{56,40},{1,17}... | collective-permute-start | bytes 1179656 | tf_op jit(solution)/shard_map/ppermute | solution.py:211
  84.2 2.2 %collective-permute-start.3 = (bf16[128,1536]{1,0:T(8,128)(2,1)S(1)}, bf16[128,1536]{1,0:T(8,128)(2,1)S(1)}, u32[]{:S(2)}, u32[]{:S(2)}) collective-permute-start(bf16[128,1536]{1,0:T(8,128)(2,1)S(1)} %get-tuple-element.25), channel_id=1, source_target_pairs={{0,48},{8,24},{16,0},{24,40},{32,16},{40,56},{48,32},{56,8},{1,49}... | collective-permute-start | bytes 1179656 | tf_op jit(solution)/shard_map/ppermute | solution.py:211
  86.4 0.0 copy-done.1
  86.4 4.3 %weight_grad.1 = (bf16[768,1536]{1,0:T(8,128)(2,1)}, f32[8,128]{1,0:T(8,128)S(1)}) custom-call(bf16[1024,768]{1,0:T(8,128)(2,1)S(1)} %get-tuple-element.21.refs_1_.refs_0_, bf16[1024,1536]{1,0:T(8,128)(2,1)S(1)} %copy-done.1, f32[8,128]{1,0:T(8,128)S(1)} %get-tuple-element.29.refs_2_), custom_call_target="tpu_custom_call" | custom-call | flops 1024 | bytes 1024 | tf_op jit(solution)/shard_map/weight_grad/pallas_call | solution.py:42
  90.7 0.0 copy-start.3
  90.7 0.0 reduce-scatter.2.cloned.1.call-update
  90.7 12.6 %all-to-all-done.2.refs_1_ = bf16[8,1024,128]{2,1,0:T(8,128)(2,1)} async-done(((bf16[8,1024,128]{2,1,0:T(8,128)(2,1)}), bf16[8,1024,128]{2,1,0:T(8,128)(2,1)}, u32[]{:S(2)}, u32[]{:S(2)}) %all-to-all-start.2) | async-done | bytes 2097184 | tf_op jit(solution)/shard_map/all_to_all | solution.py:213
  103.3 0.0 copy-done.3
  103.3 0.0 copy-start.5
  103.3 6.0 %attend_backward.1 = bf16[1024,384]{1,0:T(8,128)(2,1)} custom-call(bf16[1024,384]{1,0:T(8,128)(2,1)S(1)} %bitcast.6, bf16[8,1024,128]{2,1,0:T(8,128)(2,1)} %all-to-all-done.2.refs_1_, f32[8,128]{1,0:T(8,128)S(1)} %get-tuple-element.30.refs_2_), custom_call_target="tpu_custom_call" | custom-call | flops 1024 | bytes 1024 | tf_op jit(solution)/shard_map/attend_backward/pallas_call | solution.py:42
  109.3 4.8 %all-to-all-start.3 = ((bf16[8,128,384]{2,1,0:T(8,128)(2,1)}), bf16[8,128,384]{2,1,0:T(8,128)(2,1)S(1)}, u32[]{:S(2)}, u32[]{:S(2)}) async-start(bf16[8,128,384]{2,1,0:T(8,128)(2,1)} %bitcast.7), calls=%async_computation.3 | async-start | bytes 1572864 | tf_op jit(solution)/shard_map/all_to_all | solution.py:213
  114.2 0.0 collective-permute-done.4.refs_1_
  114.2 0.0 copy-done.5
  114.2 0.0 copy-start.4
  114.2 0.1 add_output.1
  114.3 1.8 %collective-permute-start.5 = (bf16[128,1536]{1,0:T(8,128)(2,1)S(1)}, bf16[128,1536]{1,0:T(8,128)(2,1)S(1)}, u32[]{:S(2)}, u32[]{:S(2)}) collective-permute-start(bf16[128,1536]{1,0:T(8,128)(2,1)S(1)} %add_output.1), channel_id=1, source_target_pairs={{0,16},{8,56},{16,32},{24,8},{32,48},{40,24},{48,0},{56,40},{1,17}... | collective-permute-start | bytes 1179656 | tf_op jit(solution)/shard_map/ppermute | solution.py:211
  116.0 0.0 collective-permute-done.3.refs_1_
  116.1 16.1 %collective-permute-done.5.refs_2_ = bf16[128,1536]{1,0:T(8,128)(2,1)S(1)} collective-permute-done((bf16[128,1536]{1,0:T(8,128)(2,1)S(1)}, bf16[128,1536]{1,0:T(8,128)(2,1)S(1)}, u32[]{:S(2)}, u32[]{:S(2)}) %collective-permute-start.5) | collective-permute-done | bytes 393248 | tf_op jit(solution)/shard_map/ppermute | solution.py:211
  132.2 0.0 copy-done.4
  132.2 0.9 sum_output.1
  133.1 0.0 all-to-all-done.3.refs_0_
  133.1 0.9 unpack_heads.1
  134.0 0.0 reduce-scatter.2.cloned.1.call-done
Async XLA Ops:
  7.2 49.8 %all-gather.2.cloned.1.call-start = ((), (), s32[]{:S(2)}) async-start(), calls=%async_computation.5 | async-start | bytes 3538944 | tf_op jit(solution)/shard_map/all_gather | solution.py:217
  27.5 29.5 %copy-start.2 = (bf16[768,1536]{1,0:T(8,128)(2,1)S(1)}, bf16[768,1536]{1,0:T(8,128)(2,1)}, u32[]{:S(2)}) copy-start(bf16[768,1536]{1,0:T(8,128)(2,1)} %refs_2_.3) | copy-start | bytes 7077892
  50.4 19.8 %collective-permute-start = (bf16[3,1024,128]{2,1,0:T(8,128)(2,1)}, bf16[3,1024,128]{2,1,0:T(8,128)(2,1)}, u32[]{:S(2)}, u32[]{:S(2)}) collective-permute-start(bf16[3,1024,128]{2,1,0:T(8,128)(2,1)} %slice.4), channel_id=1, source_target_pairs={{0,4},{1,5},{2,6},{3,7},{4,0},{5,1},{6,2},{7,3},{8,12},{9,13},{10,... | collective-permute-start | bytes 2359304 | tf_op jit(solution)/shard_map/ppermute | solution.py:233
  57.0 1.9 %copy-start = (bf16[1024,1536]{1,0:T(8,128)(2,1)S(1)}, bf16[1024,1536]{1,0:T(8,128)(2,1)}, u32[]{:S(2)}) copy-start(bf16[1024,1536]{1,0:T(8,128)(2,1)} %all-gather.2.cloned.1.call-done.refs_0_.refs_1_) | copy-start | bytes 9437188
  62.5 40.8 %all-to-all-start.2 = ((bf16[8,1024,128]{2,1,0:T(8,128)(2,1)}), bf16[8,1024,128]{2,1,0:T(8,128)(2,1)}, u32[]{:S(2)}, u32[]{:S(2)}) async-start(bf16[8,1024,128]{2,1,0:T(8,128)(2,1)} %get-tuple-element.28), calls=%async_computation.2 | async-start | bytes 4194304 | tf_op jit(solution)/shard_map/all_to_all | solution.py:213
  69.0 65.0 %reduce-scatter.2.cloned.1.call-start = ((), (), s32[]{:S(2)}) async-start(), calls=%async_computation.6 | async-start | bytes 2949120 | tf_op jit(solution)/shard_map/reduce_scatter | solution.py:295
  74.0 2.4 %collective-permute-start.1 = (bf16[512,768]{1,0:T(8,128)(2,1)S(1)}, bf16[512,768]{1,0:T(8,128)(2,1)S(1)}, u32[]{:S(2)}, u32[]{:S(2)}) collective-permute-start(bf16[512,768]{1,0:T(8,128)(2,1)S(1)} %get-tuple-element.22), channel_id=1, source_target_pairs={{0,8},{8,0},{16,24},{24,16},{32,40},{40,32},{48,56},{56,48},{1,9},... | collective-permute-start | bytes 2359304 | tf_op jit(solution)/shard_map/ppermute | solution.py:211
  74.1 3.4 %collective-permute-start.2 = (bf16[512,768]{1,0:T(8,128)(2,1)S(1)}, bf16[512,768]{1,0:T(8,128)(2,1)S(1)}, u32[]{:S(2)}, u32[]{:S(2)}) collective-permute-start(bf16[512,768]{1,0:T(8,128)(2,1)S(1)} %get-tuple-element.23), channel_id=1, source_target_pairs={{0,8},{8,0},{16,24},{24,16},{32,40},{40,32},{48,56},{56,48},{1,9},... | collective-permute-start | bytes 2359304 | tf_op jit(solution)/shard_map/ppermute | solution.py:211
  77.5 8.9 %copy-start.1 = (bf16[1024,1536]{1,0:T(8,128)(2,1)S(1)}, bf16[1024,1536]{1,0:T(8,128)(2,1)}, u32[]{:S(2)}) copy-start(bf16[1024,1536]{1,0:T(8,128)(2,1)} %all-gather.2.cloned.1.call-done.refs_0_.refs_1_) | copy-start | bytes 9437188
  80.7 33.5 %collective-permute-start.4 = (bf16[128,1536]{1,0:T(8,128)(2,1)S(1)}, bf16[128,1536]{1,0:T(8,128)(2,1)S(1)}, u32[]{:S(2)}, u32[]{:S(2)}) collective-permute-start(bf16[128,1536]{1,0:T(8,128)(2,1)S(1)} %get-tuple-element.27), channel_id=1, source_target_pairs={{0,16},{8,56},{16,32},{24,8},{32,48},{40,24},{48,0},{56,40},{1,17}... | collective-permute-start | bytes 1179656 | tf_op jit(solution)/shard_map/ppermute | solution.py:211
  84.2 31.9 %collective-permute-start.3 = (bf16[128,1536]{1,0:T(8,128)(2,1)S(1)}, bf16[128,1536]{1,0:T(8,128)(2,1)S(1)}, u32[]{:S(2)}, u32[]{:S(2)}) collective-permute-start(bf16[128,1536]{1,0:T(8,128)(2,1)S(1)} %get-tuple-element.25), channel_id=1, source_target_pairs={{0,48},{8,24},{16,0},{24,40},{32,16},{40,56},{48,32},{56,8},{1,49}... | collective-permute-start | bytes 1179656 | tf_op jit(solution)/shard_map/ppermute | solution.py:211
  90.7 12.7 %copy-start.3 = (bf16[8,128,384]{2,1,0:T(8,128)(2,1)S(1)}, bf16[8,128,384]{2,1,0:T(8,128)(2,1)}, u32[]{:S(2)}) copy-start(bf16[8,128,384]{2,1,0:T(8,128)(2,1)} %all_to_all.20) | copy-start | bytes 2359300
  103.3 10.9 %copy-start.5 = (f32[128,1536]{1,0:T(8,128)S(1)}, f32[128,1536]{1,0:T(8,128)}, u32[]{:S(2)}) copy-start(f32[128,1536]{1,0:T(8,128)} %get-tuple-element.26.refs_0_) | copy-start | bytes 2359300
  109.3 23.7 %all-to-all-start.3 = ((bf16[8,128,384]{2,1,0:T(8,128)(2,1)}), bf16[8,128,384]{2,1,0:T(8,128)(2,1)S(1)}, u32[]{:S(2)}, u32[]{:S(2)}) async-start(bf16[8,128,384]{2,1,0:T(8,128)(2,1)} %bitcast.7), calls=%async_computation.3 | async-start | bytes 1572864 | tf_op jit(solution)/shard_map/all_to_all | solution.py:213
  114.2 18.0 %copy-start.4 = (f32[128,1536]{1,0:T(8,128)S(1)}, f32[128,1536]{1,0:T(8,128)}, u32[]{:S(2)}) copy-start(f32[128,1536]{1,0:T(8,128)} %get-tuple-element.24.refs_0_) | copy-start | bytes 2359300
  114.3 17.9 %collective-permute-start.5 = (bf16[128,1536]{1,0:T(8,128)(2,1)S(1)}, bf16[128,1536]{1,0:T(8,128)(2,1)S(1)}, u32[]{:S(2)}, u32[]{:S(2)}) collective-permute-start(bf16[128,1536]{1,0:T(8,128)(2,1)S(1)} %add_output.1), channel_id=1, source_target_pairs={{0,16},{8,56},{16,32},{24,8},{32,48},{40,24},{48,0},{56,40},{1,17}... | collective-permute-start | bytes 1179656 | tf_op jit(solution)/shard_map/ppermute | solution.py:211
Sparse Core Ops, SparseCore 0:
  9.8 47.0 all-gather.1
  90.8 33.8 reduce-scatter.1

commit v4 on v2

--- a/solution.py
+++ b/solution.py
@@ -53,12 +53,20 @@
     )(*args, *after)
 
 
-def pack_kernel(q, k, v, slots):
-    for j, slot in enumerate(OWNERS):
-        for i, a in enumerate((q, k, v)):
-            slots[slot, :, i * DH : (i + 1) * DH] = a[:, j * DH : (j + 1) * DH]
-    for slot in (3, 7):
-        slots[slot] = jnp.zeros(slots.shape[1:], slots.dtype)
+def pack_kernel(q, k, v, slots, sems):
+    copies = [
+        pltpu.make_async_copy(
+            a.at[:, j * DH : (j + 1) * DH],
+            slots.at[slot, :, i * DH : (i + 1) * DH],
+            sems.at[i, j],
+        )
+        for i, a in enumerate((q, k, v))
+        for j, slot in enumerate(OWNERS)
+    ]
+    for copy in copies:
+        copy.start()
+    for copy in copies:
+        copy.wait()
 
 
 def unpack_kernel(slots, q, k, v):
@@ -111,7 +119,7 @@
             dp = lax.dot_general(g, v, NT, preferred_element_type=F32)
             dot = jnp.sum(attend * dp, axis=-1, keepdims=True)
             ds = (attend * (dp - dot) * SCALE).astype(BF16)
-            out[rows, :DH] = jnp.dot(ds, k, preferred_element_type=F32).astype(BF16)
+            out[:, :DH] = jnp.dot(ds, k, preferred_element_type=F32).astype(BF16)
             dk_part = lax.dot_general(ds, q, TN, preferred_element_type=F32)
             dv_part = lax.dot_general(attend.astype(BF16), g, TN, preferred_element_type=F32)
             if i == blocks - 1:
@@ -120,8 +128,8 @@
             else:
                 dk[seen, :] += dk_part
                 dv[seen, :] += dv_part
-            out[rows, DH : 2 * DH] = dk[rows, :].astype(BF16)
-            out[rows, 2 * DH :] = dv[rows, :].astype(BF16)
+            out[:, DH : 2 * DH] = dk[rows, :].astype(BF16)
+            out[:, 2 * DH :] = dv[rows, :].astype(BF16)
 
 
 def context_grad_kernel(grad_all, w, slots, token, part, sems):
@@ -171,7 +179,8 @@
         out[...] = jnp.dot(rows, w[:, lanes[i]], preferred_element_type=F32).astype(BF16)
 
 
-def mine_kernel(place, ctx, w, left, right, far, now, later, own):
+def mine_kernel(place, ctx, w, left, right, far, now, later, own, token):
+    token[...] = jnp.zeros(token.shape, token.dtype)
     h, core = place[0], place[1]
     rows = rows_for(ctx, h, core)
     wide = left.shape[1]
@@ -216,7 +225,13 @@
     grad_all = lax.all_gather(out_grad, "row", axis=0, tiled=True)
 
     (slots,) = local(
-        pack_kernel, "pack_heads", [((8, POS, 3 * DH), BF16, IN_HBM)], (queries, keys, values)
+        pack_kernel,
+        "pack_heads",
+        [((8, POS, 3 * DH), BF16, IN_HBM)],
+        (queries, keys, values),
+        in_specs=[HBM] * 3,
+        out_specs=[HBM],
+        scratch=[pltpu.SemaphoreType.DMA((3, 6))],
     )
     qkv = trade(slots).reshape(seq, 3 * DH)
 
@@ -255,6 +270,7 @@
         ],
         after=[token],
         flops=60_000_000_000,
+        vmem=24,
     )
     w_part, token = local(
         weight_kernel,
@@ -269,10 +285,10 @@
     weight_grad = lax.psum_scatter(w_part, "depth", scatter_dimension=0, tiled=True)
 
     block = (POS, feats)
-    far, now, later, own = local(
+    far, now, later, own, token = local(
         mine_kernel,
         "project_mine",
-        [(block, BF16, ARRAY), (block, BF16, ARRAY), (block, F32, ARRAY), (block, F32, ARRAY)],
+        [(block, dtype, ARRAY) for dtype in (BF16, BF16, F32, F32)] + [((8, DH), F32, ARRAY)],
         (place, ctx, weight, *[on_row(a, ACROSS_CORE) for a in theirs]),
         in_specs=[scalars] + [WHOLE] * 4,
         after=[token],
@@ -295,14 +311,14 @@
         "attend_backward",
         [((seq, 3 * DH), BF16, IN_HBM)],
         (qkv, parts),
-        after=[own],
+        after=[token],
         vmem=24,
         grid=(steps,),
         in_specs=[
             whole((seq, 3 * DH)),
             pl.BlockSpec((8, QB, DH), lambda i: (0, steps - 1 - i, 0)),
         ],
-        out_specs=[whole((seq, 3 * DH))],
+        out_specs=[pl.BlockSpec((QB, 3 * DH), lambda i: (steps - 1 - i, 0))],
         scratch=[pltpu.VMEM((seq, DH), F32), pltpu.VMEM((seq, DH), F32)],
     )
     back = trade(back.reshape(8, POS, 3 * DH))

time: 140 us -> 176 us (1.26)
  blocking collectives: 34.9 us -> 52.6 us
  Pallas kernels: 29.7 us -> 45.3 us
  waiting for transfers between devices: 29.2 us -> 36.9 us
  local copies, waits for them, and re-layouts: 11.2 us -> 5.22 us
    all_to_all x1, blocking collectives: 17.5 us -> 34.6 us  [shards(): trade = lambda a: lax.all_to_all(a, 'col', 0, 0, tiled=True)]
    pallas_call x10, Pallas kernels: 29.7 us -> 45.3 us  [local(): pl.pallas_call(body, out_shape=[kind(shape, dtype) for shape, dtype, kind...]
    ppermute x5, waiting for transfers between devices: 12.4 us -> 27.4 us  [shards(): on_row = lambda a, perm: lax.ppermute(a, 'row', perm)]
    all_to_all x2, waiting for transfers between devices: 10.6 us -> 0.72 us  [shards(): trade = lambda a: lax.all_to_all(a, 'col', 0, 0, tiled=True)]
    ppermute x1, waiting for transfers between devices: 0.52 us -> 8.02 us  [shards(): other = lax.ppermute(near[:3], 'col', ACROSS_Z)]
    unnamed x32 -> x14, local copies, waits for them, and re-layouts: 10.1 us -> 4.23 us
    all_gather x1, waiting for transfers between devices: 4.95 us -> 0.01 us  [shards(): grad_all = lax.all_gather(out_grad, 'row', axis=0, tiled=True)]
  transfers between devices with their start and end apart: 10 -> 10, of which waited for: 4 -> 4; matrix products, arithmetic and copies ran while one was open for 1% -> 1% of each run, Pallas kernels for 21% -> 26%
where the time goes in v4:
time: 176 us; the launch traced here: 175 us
  blocking collectives  52.6 us (30%)
  Pallas kernels  45.3 us (26%)
  waiting for transfers between devices  36.9 us (21%)
  starting transfers between devices  21.2 us (12%)
  between operations  14.1 us (8%)
  local copies, waits for them, and re-layouts  5.22 us (3%)
    pallas_call x10, Pallas kernels, local(): pl.pallas_call(body, out_shape=[kind(shape, dtype) for shape, dtype, kind...  45.3 us
    all_to_all x1, blocking collectives, shards(): trade = lambda a: lax.all_to_all(a, 'col', 0, 0, tiled=True)  34.6 us
    ppermute x5, waiting for transfers between devices, shards(): on_row = lambda a, perm: lax.ppermute(a, 'row', perm)  27.4 us
    all_to_all x1, blocking collectives, shards(): lax.all_to_all(copies, 'col', 0, 0, tiled=True, axis_index_groups=SAME_Z)  18 us
    all_to_all x2, starting transfers between devices, shards(): trade = lambda a: lax.all_to_all(a, 'col', 0, 0, tiled=True)  10.5 us
    ppermute x5, starting transfers between devices, shards(): on_row = lambda a, perm: lax.ppermute(a, 'row', perm)  9.24 us
    ppermute x1, waiting for transfers between devices, shards(): other = lax.ppermute(near[:3], 'col', ACROSS_Z)  8.02 us
    unnamed x14, local copies, waits for them, and re-layouts  4.23 us
  transfers between devices with their start and end apart: 10, of which 4 were waited for; matrix products, arithmetic and copies ran while one was open for 1% of the time, Pallas kernels for 26%

profile of v4, /device:TPU:8, one launch (start us, length us, event | category | flops | bytes accessed | tf_op | source)
XLA Modules:
  0.0 175.4 jit_solution(14173050107402888360)
XLA Ops:
  7.2 0.0 all-gather.2.cloned.1.call-start
  7.2 0.7 all-gather.2.cloned.1.call-update
  7.9 19.1 %pack_heads.1 = bf16[8,128,384]{2,1,0:T(8,128)(2,1)} custom-call(bf16[128,768]{1,0:T(8,128)(2,1)} %refs_0_.1, bf16[128,768]{1,0:T(8,128)(2,1)} %refs_1_.2, bf16[128,768]{1,0:T(8,128)(2,1)} %refs_2_.2), custom_call_target="tpu_custom_call" | custom-call | flops 1024 | bytes 1024 | tf_op jit(solution)/shard_map/pack_heads/pallas_call | solution.py:42
  27.0 34.6 %all_to_all.20 = bf16[8,128,384]{2,1,0:T(8,128)(2,1)} all-to-all(bf16[8,128,384]{2,1,0:T(8,128)(2,1)} %pack_heads.1), channel_id=1, replica_groups=mesh['depth'=4,'row'=8,'col'=8] {'col'}, dimensions={0} | all-to-all | bytes 1572864 | tf_op jit(solution)/shard_map/all_to_all | solution.py:221
  61.7 0.0 copy-start.2
  61.7 4.4 %attend_forward.1 = bf16[4,1024,128]{2,1,0:T(8,128)(2,1)} custom-call(bf16[1024,384]{1,0:T(8,128)(2,1)} %bitcast.5), custom_call_target="tpu_custom_call" | custom-call | flops 1024 | bytes 1024 | tf_op jit(solution)/shard_map/attend_forward/pallas_call | solution.py:42
  66.0 18.0 %all_to_all.21.refs_1_ = bf16[4,1024,128]{2,1,0:T(8,128)(2,1)S(1)} all-to-all(bf16[4,1024,128]{2,1,0:T(8,128)(2,1)} %attend_forward.1), channel_id=1, replica_groups={{0,1,2,3},{4,5,6,7},{8,9,10,11},{12,13,14,15},{16,17,18,19},{20,21,22,2..., dimensions={0} | all-to-all | bytes 2097152 | tf_op jit(solution)/shard_map/all_to_all | solution.py:246
  84.0 1.0 slice.4
  85.0 1.4 collective-permute-start
  86.4 0.1 pad_add_fusion.refs_0_
  86.5 0.0 all-gather.2.cloned.1.call-done.refs_0_.refs_1_
  86.5 0.0 copy-done.2
  86.5 0.0 copy-start
  86.5 1.9 %copy-done = bf16[1024,1536]{1,0:T(8,128)(2,1)S(1)} copy-done((bf16[1024,1536]{1,0:T(8,128)(2,1)S(1)}, bf16[1024,1536]{1,0:T(8,128)(2,1)}, u32[]{:S(2)}) %copy-start) | copy-done | bytes 3145752
  88.4 3.7 %context_grad.1 = (bf16[8,1024,128]{2,1,0:T(8,128)(2,1)}, f32[8,128]{1,0:T(8,128)S(1)}) custom-call(bf16[1024,1536]{1,0:T(8,128)(2,1)S(1)} %copy-done, bf16[768,1536]{1,0:T(8,128)(2,1)S(1)} %copy-done.2), custom_call_target="tpu_custom_call" | custom-call | flops 1024 | bytes 1024 | tf_op jit(solution)/shard_map/context_grad/pallas_call | solution.py:42
  92.1 5.7 %all-to-all-start.2 = ((bf16[8,1024,128]{2,1,0:T(8,128)(2,1)}), bf16[8,1024,128]{2,1,0:T(8,128)(2,1)}, u32[]{:S(2)}, u32[]{:S(2)}) async-start(bf16[8,1024,128]{2,1,0:T(8,128)(2,1)} %get-tuple-element.29), calls=%async_computation.2 | async-start | bytes 4194304 | tf_op jit(solution)/shard_map/all_to_all | solution.py:221
  97.8 0.0 reduce-scatter.2.cloned.1.call-start
  97.8 8.0 %collective-permute-done.refs_2_ = bf16[3,1024,128]{2,1,0:T(8,128)(2,1)} collective-permute-done((bf16[3,1024,128]{2,1,0:T(8,128)(2,1)}, bf16[3,1024,128]{2,1,0:T(8,128)(2,1)}, u32[]{:S(2)}, u32[]{:S(2)}) %collective-permute-start) | collective-permute-done | bytes 786464 | tf_op jit(solution)/shard_map/ppermute | solution.py:247
  105.8 0.0 copy-start.1
  105.8 4.1 %project_theirs.1 = (bf16[1024,768]{1,0:T(8,128)(2,1)S(1)}, bf16[512,768]{1,0:T(8,128)(2,1)S(1)}, bf16[512,768]{1,0:T(8,128)(2,1)S(1)}) custom-call(s32[3]{0:T(128)S(1)} %pad_add_fusion.refs_0_, bf16[4,1024,128]{2,1,0:T(8,128)(2,1)S(1)} %all_to_all.21.refs_1_, bf16[3,1024,128]{2,1,0:T(8,128)(2,1)} %collective-permute-done.refs_2_, ...), custom_call_target="tpu_custom_call" | custom-call | flops 60000002048 | bytes 1024 | tf_op jit(solution)/shard_map/project_theirs/pallas_call | solution.py:42
  109.9 0.1 collective-permute-start.1
  110.0 0.5 collective-permute-start.2
  110.5 0.0 copy-done.1
  110.5 3.4 %weight_grad.1 = (bf16[768,1536]{1,0:T(8,128)(2,1)S(1)}, f32[8,128]{1,0:T(8,128)S(1)}) custom-call(bf16[1024,768]{1,0:T(8,128)(2,1)S(1)} %get-tuple-element.21.refs_0_.refs_1_, bf16[1024,1536]{1,0:T(8,128)(2,1)S(1)} %copy-done.1), custom_call_target="tpu_custom_call" | custom-call | flops 1024 | bytes 1024 | tf_op jit(solution)/shard_map/weight_grad/pallas_call | solution.py:42
  113.9 0.0 copy-start.4
  113.9 1.4 copy-done.4
  115.4 0.0 collective-permute-done.1.refs_3_
  115.4 0.0 collective-permute-done.2.refs_4_
  115.4 2.8 %project_mine.1 = (bf16[128,1536]{1,0:T(8,128)(2,1)}, bf16[128,1536]{1,0:T(8,128)(2,1)}, f32[128,1536]{1,0:T(8,128)S(1)}, f32[128,1536]{1,0:T(8,128)S(1)}, f32[8,128]{1,0:T(8,128)S(1)}) custom-call(s32[3]{0:T(128)S(1)} %pad_add_fusion.refs_0_, bf16[1024,768]{1,0:T(8,128)(2,1)S(1)} %get-tuple-element.21.refs_0_.refs_1_, bf16[768,1536]{1,0:T(8,128)(2,1)S(1)} %copy-done.2, ...), custom_call_target="tpu_custom_call" | custom-call | flops 1024 | bytes 1024 | tf_op jit(solution)/shard_map/project_mine/pallas_call | solution.py:42
  118.2 0.0 copy-start.5
  118.2 0.9 copy-done.5
  119.0 0.0 copy-start.3
  119.1 4.4 %collective-permute-start.4 = (bf16[128,1536]{1,0:T(8,128)(2,1)}, bf16[128,1536]{1,0:T(8,128)(2,1)S(1)}, u32[]{:S(2)}, u32[]{:S(2)}) collective-permute-start(bf16[128,1536]{1,0:T(8,128)(2,1)} %get-tuple-element.28), channel_id=1, source_target_pairs={{0,16},{8,56},{16,32},{24,8},{32,48},{40,24},{48,0},{56,40},{1,17}... | collective-permute-start | bytes 1179656 | tf_op jit(solution)/shard_map/ppermute | solution.py:219
  123.5 0.0 reduce-scatter.2.cloned.1.call-update
  123.5 0.3 collective-permute-start.3
  123.8 0.7 all-to-all-done.2.refs_1_
  124.5 0.0 copy-done.3
  124.5 0.0 copy-start.6
  124.5 6.0 %attend_backward.1 = bf16[1024,384]{1,0:T(8,128)(2,1)} custom-call(bf16[1024,384]{1,0:T(8,128)(2,1)S(1)} %bitcast.6, bf16[8,1024,128]{2,1,0:T(8,128)(2,1)} %all-to-all-done.2.refs_1_, f32[8,128]{1,0:T(8,128)S(1)} %get-tuple-element.30.refs_2_), custom_call_target="tpu_custom_call" | custom-call | flops 1024 | bytes 1024 | tf_op jit(solution)/shard_map/attend_backward/pallas_call | solution.py:42
  130.5 4.9 %all-to-all-start.3 = ((bf16[8,128,384]{2,1,0:T(8,128)(2,1)}), bf16[8,128,384]{2,1,0:T(8,128)(2,1)S(1)}, u32[]{:S(2)}, u32[]{:S(2)}) async-start(bf16[8,128,384]{2,1,0:T(8,128)(2,1)} %bitcast.7), calls=%async_computation.3 | async-start | bytes 1572864 | tf_op jit(solution)/shard_map/all_to_all | solution.py:221
  135.4 12.8 %collective-permute-done.4.refs_1_ = bf16[128,1536]{1,0:T(8,128)(2,1)S(1)} collective-permute-done((bf16[128,1536]{1,0:T(8,128)(2,1)}, bf16[128,1536]{1,0:T(8,128)(2,1)S(1)}, u32[]{:S(2)}, u32[]{:S(2)}) %collective-permute-start.4) | collective-permute-done | bytes 393248 | tf_op jit(solution)/shard_map/ppermute | solution.py:219
  148.2 0.0 copy-done.6
  148.2 0.1 add_output.1
  148.3 4.0 %collective-permute-start.5 = (bf16[128,1536]{1,0:T(8,128)(2,1)S(1)}, bf16[128,1536]{1,0:T(8,128)(2,1)S(1)}, u32[]{:S(2)}, u32[]{:S(2)}) collective-permute-start(bf16[128,1536]{1,0:T(8,128)(2,1)S(1)} %add_output.1), channel_id=1, source_target_pairs={{0,16},{8,56},{16,32},{24,8},{32,48},{40,24},{48,0},{56,40},{1,17}... | collective-permute-start | bytes 1179656 | tf_op jit(solution)/shard_map/ppermute | solution.py:219
  152.2 0.0 collective-permute-done.3.refs_1_
  152.2 14.6 %collective-permute-done.5.refs_2_ = bf16[128,1536]{1,0:T(8,128)(2,1)S(1)} collective-permute-done((bf16[128,1536]{1,0:T(8,128)(2,1)S(1)}, bf16[128,1536]{1,0:T(8,128)(2,1)S(1)}, u32[]{:S(2)}, u32[]{:S(2)}) %collective-permute-start.5) | collective-permute-done | bytes 393248 | tf_op jit(solution)/shard_map/ppermute | solution.py:219
  166.8 0.9 sum_output.1
  167.7 0.0 all-to-all-done.3.refs_0_
  167.7 0.9 unpack_heads.1
  168.6 0.0 reduce-scatter.2.cloned.1.call-done
Async XLA Ops:
  7.2 79.3 %all-gather.2.cloned.1.call-start = ((), (), s32[]{:S(2)}) async-start(), calls=%async_computation.5 | async-start | bytes 3538944 | tf_op jit(solution)/shard_map/all_gather | solution.py:225
  61.7 24.8 %copy-start.2 = (bf16[768,1536]{1,0:T(8,128)(2,1)S(1)}, bf16[768,1536]{1,0:T(8,128)(2,1)}, u32[]{:S(2)}) copy-start(bf16[768,1536]{1,0:T(8,128)(2,1)} %refs_2_.3) | copy-start | bytes 7077892
  85.0 20.8 %collective-permute-start = (bf16[3,1024,128]{2,1,0:T(8,128)(2,1)}, bf16[3,1024,128]{2,1,0:T(8,128)(2,1)}, u32[]{:S(2)}, u32[]{:S(2)}) collective-permute-start(bf16[3,1024,128]{2,1,0:T(8,128)(2,1)} %slice.4), channel_id=1, source_target_pairs={{0,4},{1,5},{2,6},{3,7},{4,0},{5,1},{6,2},{7,3},{8,12},{9,13},{10,... | collective-permute-start | bytes 2359304 | tf_op jit(solution)/shard_map/ppermute | solution.py:247
  86.5 1.9 %copy-start = (bf16[1024,1536]{1,0:T(8,128)(2,1)S(1)}, bf16[1024,1536]{1,0:T(8,128)(2,1)}, u32[]{:S(2)}) copy-start(bf16[1024,1536]{1,0:T(8,128)(2,1)} %all-gather.2.cloned.1.call-done.refs_0_.refs_1_) | copy-start | bytes 9437188
  92.1 32.4 %all-to-all-start.2 = ((bf16[8,1024,128]{2,1,0:T(8,128)(2,1)}), bf16[8,1024,128]{2,1,0:T(8,128)(2,1)}, u32[]{:S(2)}, u32[]{:S(2)}) async-start(bf16[8,1024,128]{2,1,0:T(8,128)(2,1)} %get-tuple-element.29), calls=%async_computation.2 | async-start | bytes 4194304 | tf_op jit(solution)/shard_map/all_to_all | solution.py:221
  97.8 70.8 %reduce-scatter.2.cloned.1.call-start = ((), (), s32[]{:S(2)}) async-start(), calls=%async_computation.6 | async-start | bytes 2949120 | tf_op jit(solution)/shard_map/reduce_scatter | solution.py:285
  105.8 4.7 %copy-start.1 = (bf16[1024,1536]{1,0:T(8,128)(2,1)S(1)}, bf16[1024,1536]{1,0:T(8,128)(2,1)}, u32[]{:S(2)}) copy-start(bf16[1024,1536]{1,0:T(8,128)(2,1)} %all-gather.2.cloned.1.call-done.refs_0_.refs_1_) | copy-start | bytes 9437188
  109.9 5.4 %collective-permute-start.1 = (bf16[512,768]{1,0:T(8,128)(2,1)S(1)}, bf16[512,768]{1,0:T(8,128)(2,1)S(1)}, u32[]{:S(2)}, u32[]{:S(2)}) collective-permute-start(bf16[512,768]{1,0:T(8,128)(2,1)S(1)} %get-tuple-element.22), channel_id=1, source_target_pairs={{0,8},{8,0},{16,24},{24,16},{32,40},{40,32},{48,56},{56,48},{1,9},... | collective-permute-start | bytes 2359304 | tf_op jit(solution)/shard_map/ppermute | solution.py:219
  110.0 5.3 %collective-permute-start.2 = (bf16[512,768]{1,0:T(8,128)(2,1)S(1)}, bf16[512,768]{1,0:T(8,128)(2,1)S(1)}, u32[]{:S(2)}, u32[]{:S(2)}) collective-permute-start(bf16[512,768]{1,0:T(8,128)(2,1)S(1)} %get-tuple-element.23), channel_id=1, source_target_pairs={{0,8},{8,0},{16,24},{24,16},{32,40},{40,32},{48,56},{56,48},{1,9},... | collective-permute-start | bytes 2359304 | tf_op jit(solution)/shard_map/ppermute | solution.py:219
  113.9 1.4 copy-start.4
  118.2 0.9 copy-start.5
  119.0 5.4 %copy-start.3 = (bf16[8,128,384]{2,1,0:T(8,128)(2,1)S(1)}, bf16[8,128,384]{2,1,0:T(8,128)(2,1)}, u32[]{:S(2)}) copy-start(bf16[8,128,384]{2,1,0:T(8,128)(2,1)} %all_to_all.20) | copy-start | bytes 2359300
  119.1 29.1 %collective-permute-start.4 = (bf16[128,1536]{1,0:T(8,128)(2,1)}, bf16[128,1536]{1,0:T(8,128)(2,1)S(1)}, u32[]{:S(2)}, u32[]{:S(2)}) collective-permute-start(bf16[128,1536]{1,0:T(8,128)(2,1)} %get-tuple-element.28), channel_id=1, source_target_pairs={{0,16},{8,56},{16,32},{24,8},{32,48},{40,24},{48,0},{56,40},{1,17}... | collective-permute-start | bytes 1179656 | tf_op jit(solution)/shard_map/ppermute | solution.py:219
  123.5 28.7 %collective-permute-start.3 = (bf16[128,1536]{1,0:T(8,128)(2,1)}, bf16[128,1536]{1,0:T(8,128)(2,1)S(1)}, u32[]{:S(2)}, u32[]{:S(2)}) collective-permute-start(bf16[128,1536]{1,0:T(8,128)(2,1)} %get-tuple-element.26), channel_id=1, source_target_pairs={{0,48},{8,24},{16,0},{24,40},{32,16},{40,56},{48,32},{56,8},{1,49}... | collective-permute-start | bytes 1179656 | tf_op jit(solution)/shard_map/ppermute | solution.py:219
  124.5 23.7 %copy-start.6 = (f32[128,1536]{1,0:T(8,128)S(1)}, f32[128,1536]{1,0:T(8,128)}, u32[]{:S(2)}) copy-start(f32[128,1536]{1,0:T(8,128)} %copy-done.5) | copy-start | bytes 2359300
  130.5 37.2 %all-to-all-start.3 = ((bf16[8,128,384]{2,1,0:T(8,128)(2,1)}), bf16[8,128,384]{2,1,0:T(8,128)(2,1)S(1)}, u32[]{:S(2)}, u32[]{:S(2)}) async-start(bf16[8,128,384]{2,1,0:T(8,128)(2,1)} %bitcast.7), calls=%async_computation.3 | async-start | bytes 1572864 | tf_op jit(solution)/shard_map/all_to_all | solution.py:221
  148.3 18.6 %collective-permute-start.5 = (bf16[128,1536]{1,0:T(8,128)(2,1)S(1)}, bf16[128,1536]{1,0:T(8,128)(2,1)S(1)}, u32[]{:S(2)}, u32[]{:S(2)}) collective-permute-start(bf16[128,1536]{1,0:T(8,128)(2,1)S(1)} %add_output.1), channel_id=1, source_target_pairs={{0,16},{8,56},{16,32},{24,8},{32,48},{40,24},{48,0},{56,40},{1,17}... | collective-permute-start | bytes 1179656 | tf_op jit(solution)/shard_map/ppermute | solution.py:219
Sparse Core Ops, SparseCore 0:
  9.8 54.7 all-gather.1
  123.6 31.9 reduce-scatter.1

commit v5 on v4

--- a/solution.py
+++ b/solution.py
@@ -53,19 +53,21 @@
     )(*args, *after)
 
 
-def pack_kernel(q, k, v, slots, sems):
-    copies = [
-        pltpu.make_async_copy(
-            a.at[:, j * DH : (j + 1) * DH],
-            slots.at[slot, :, i * DH : (i + 1) * DH],
-            sems.at[i, j],
-        )
-        for i, a in enumerate((q, k, v))
-        for j, slot in enumerate(OWNERS)
+def pack_kernel(q, k, v, slots, rows, packed, sems_in, sems_out):
+    arrive = [
+        pltpu.make_async_copy(a, rows.at[i], sems_in.at[i]) for i, a in enumerate((q, k, v))
     ]
-    for copy in copies:
+    for copy in arrive:
         copy.start()
-    for copy in copies:
+    for copy in arrive:
+        copy.wait()
+    leave = []
+    for j, slot in enumerate(OWNERS):
+        for i in range(3):
+            packed[j, :, i * DH : (i + 1) * DH] = rows[i, :, j * DH : (j + 1) * DH]
+        leave.append(pltpu.make_async_copy(packed.at[j], slots.at[slot], sems_out.at[j]))
+        leave[-1].start()
+    for copy in leave:
         copy.wait()
 
 
@@ -231,7 +233,12 @@
         (queries, keys, values),
         in_specs=[HBM] * 3,
         out_specs=[HBM],
-        scratch=[pltpu.SemaphoreType.DMA((3, 6))],
+        scratch=[
+            pltpu.VMEM((3, POS, width), BF16),
+            pltpu.VMEM((6, POS, 3 * DH), BF16),
+            pltpu.SemaphoreType.DMA((3,)),
+            pltpu.SemaphoreType.DMA((6,)),
+        ],
     )
     qkv = trade(slots).reshape(seq, 3 * DH)
 

time: 176 us -> 141 us (0.80)
  blocking collectives: 52.6 us -> 35 us
  Pallas kernels: 45.3 us -> 28.3 us
    all_to_all x1, blocking collectives: 34.6 us -> 17.5 us  [shards(): trade = lambda a: lax.all_to_all(a, 'col', 0, 0, tiled=True)]
    pallas_call x10, Pallas kernels: 45.3 us -> 28.3 us  [local(): pl.pallas_call(body, out_shape=[kind(shape, dtype) for shape, dtype, kind...]
    all_to_all x2, waiting for transfers between devices: 0.72 us -> 14.1 us  [shards(): trade = lambda a: lax.all_to_all(a, 'col', 0, 0, tiled=True)]
    ppermute x5, waiting for transfers between devices: 27.4 us -> 16.1 us  [shards(): on_row = lambda a, perm: lax.ppermute(a, 'row', perm)]
    ppermute x1, waiting for transfers between devices: 8.02 us -> 1.01 us  [shards(): other = lax.ppermute(near[:3], 'col', ACROSS_Z)]
    all_gather x1, waiting for transfers between devices: 0.01 us -> 6.17 us  [shards(): grad_all = lax.all_gather(out_grad, 'row', axis=0, tiled=True)]
  transfers between devices with their start and end apart: 10 -> 10, of which waited for: 4 -> 4; matrix products, arithmetic and copies ran while one was open for 1% -> 1% of each run, Pallas kernels for 26% -> 20%
where the time goes in v5:
time: 141 us
  waiting for transfers between devices  38.1 us (27%)
  blocking collectives  35 us (25%)
  Pallas kernels  28.3 us (20%)
  starting transfers between devices  20.1 us (14%)
  between operations  14.1 us (10%)
  local copies, waits for them, and re-layouts  5.22 us (4%)
    pallas_call x10, Pallas kernels, local(): pl.pallas_call(body, out_shape=[kind(shape, dtype) for shape, dtype, kind...  28.3 us
    all_to_all x1, blocking collectives, shards(): trade = lambda a: lax.all_to_all(a, 'col', 0, 0, tiled=True)  17.5 us
    all_to_all x1, blocking collectives, shards(): lax.all_to_all(copies, 'col', 0, 0, tiled=True, axis_index_groups=SAME_Z)  17.5 us
    ppermute x5, waiting for transfers between devices, shards(): on_row = lambda a, perm: lax.ppermute(a, 'row', perm)  16.1 us
    all_to_all x2, waiting for transfers between devices, shards(): trade = lambda a: lax.all_to_all(a, 'col', 0, 0, tiled=True)  14.1 us
    all_to_all x2, starting transfers between devices, shards(): trade = lambda a: lax.all_to_all(a, 'col', 0, 0, tiled=True)  10.7 us
    ppermute x5, starting transfers between devices, shards(): on_row = lambda a, perm: lax.ppermute(a, 'row', perm)  8.27 us
    all_gather x1, waiting for transfers between devices, shards(): grad_all = lax.all_gather(out_grad, 'row', axis=0, tiled=True)  6.17 us
  transfers between devices with their start and end apart: 10, of which 4 were waited for; matrix products, arithmetic and copies ran while one was open for 1% of the time, Pallas kernels for 20%

profile of v5, /device:TPU:8, one launch (start us, length us, event | category | flops | bytes accessed | tf_op | source)
XLA Modules:
  0.0 140.8 jit_solution(5851853472559063961)
XLA Ops:
  7.2 0.0 all-gather.2.cloned.1.call-start
  7.2 0.7 all-gather.2.cloned.1.call-update
  7.9 2.1 %pack_heads.1 = bf16[8,128,384]{2,1,0:T(8,128)(2,1)} custom-call(bf16[128,768]{1,0:T(8,128)(2,1)} %refs_0_.1, bf16[128,768]{1,0:T(8,128)(2,1)} %refs_1_.2, bf16[128,768]{1,0:T(8,128)(2,1)} %refs_2_.2), custom_call_target="tpu_custom_call" | custom-call | flops 1024 | bytes 1024 | tf_op jit(solution)/shard_map/pack_heads/pallas_call | solution.py:42
  10.0 17.5 %all_to_all.20 = bf16[8,128,384]{2,1,0:T(8,128)(2,1)} all-to-all(bf16[8,128,384]{2,1,0:T(8,128)(2,1)} %pack_heads.1), channel_id=1, replica_groups=mesh['depth'=4,'row'=8,'col'=8] {'col'}, dimensions={0} | all-to-all | bytes 1572864 | tf_op jit(solution)/shard_map/all_to_all | solution.py:223
  27.5 0.0 copy-start.2
  27.5 4.3 %attend_forward.1 = bf16[4,1024,128]{2,1,0:T(8,128)(2,1)} custom-call(bf16[1024,384]{1,0:T(8,128)(2,1)} %bitcast.5), custom_call_target="tpu_custom_call" | custom-call | flops 1024 | bytes 1024 | tf_op jit(solution)/shard_map/attend_forward/pallas_call | solution.py:42
  31.8 17.5 %all_to_all.21.refs_1_ = bf16[4,1024,128]{2,1,0:T(8,128)(2,1)S(1)} all-to-all(bf16[4,1024,128]{2,1,0:T(8,128)(2,1)} %attend_forward.1), channel_id=1, replica_groups={{0,1,2,3},{4,5,6,7},{8,9,10,11},{12,13,14,15},{16,17,18,19},{20,21,22,2..., dimensions={0} | all-to-all | bytes 2097152 | tf_op jit(solution)/shard_map/all_to_all | solution.py:253
  49.3 1.0 slice.4
  50.3 1.0 collective-permute-start
  51.4 0.1 pad_add_fusion.refs_0_
  51.4 6.2 %all-gather.2.cloned.1.call-done.refs_0_.refs_1_ = bf16[1024,1536]{1,0:T(8,128)(2,1)} async-done(((bf16[128,1536]{1,0:T(8,128)(2,1)}), bf16[1024,1536]{1,0:T(8,128)(2,1)}) %all-gather.2.cloned.1.call-update) | async-done | bytes 3145744 | tf_op jit(solution)/shard_map/all_gather | solution.py:227
  57.6 0.0 copy-done.2
  57.6 0.0 copy-start
  57.6 1.9 %copy-done = bf16[1024,1536]{1,0:T(8,128)(2,1)S(1)} copy-done((bf16[1024,1536]{1,0:T(8,128)(2,1)S(1)}, bf16[1024,1536]{1,0:T(8,128)(2,1)}, u32[]{:S(2)}) %copy-start) | copy-done | bytes 3145752
  59.5 3.7 %context_grad.1 = (bf16[8,1024,128]{2,1,0:T(8,128)(2,1)}, f32[8,128]{1,0:T(8,128)S(1)}) custom-call(bf16[1024,1536]{1,0:T(8,128)(2,1)S(1)} %copy-done, bf16[768,1536]{1,0:T(8,128)(2,1)S(1)} %copy-done.2), custom_call_target="tpu_custom_call" | custom-call | flops 1024 | bytes 1024 | tf_op jit(solution)/shard_map/context_grad/pallas_call | solution.py:42
  63.2 5.9 %all-to-all-start.2 = ((bf16[8,1024,128]{2,1,0:T(8,128)(2,1)}), bf16[8,1024,128]{2,1,0:T(8,128)(2,1)}, u32[]{:S(2)}, u32[]{:S(2)}) async-start(bf16[8,1024,128]{2,1,0:T(8,128)(2,1)} %get-tuple-element.29), calls=%async_computation.2 | async-start | bytes 4194304 | tf_op jit(solution)/shard_map/all_to_all | solution.py:223
  69.1 0.0 reduce-scatter.2.cloned.1.call-start
  69.1 1.0 collective-permute-done.refs_2_
  70.1 0.0 copy-start.1
  70.1 4.1 %project_theirs.1 = (bf16[1024,768]{1,0:T(8,128)(2,1)S(1)}, bf16[512,768]{1,0:T(8,128)(2,1)S(1)}, bf16[512,768]{1,0:T(8,128)(2,1)S(1)}) custom-call(s32[3]{0:T(128)S(1)} %pad_add_fusion.refs_0_, bf16[4,1024,128]{2,1,0:T(8,128)(2,1)S(1)} %all_to_all.21.refs_1_, bf16[3,1024,128]{2,1,0:T(8,128)(2,1)} %collective-permute-done.refs_2_, ...), custom_call_target="tpu_custom_call" | custom-call | flops 60000002048 | bytes 1024 | tf_op jit(solution)/shard_map/project_theirs/pallas_call | solution.py:42
  74.2 0.1 collective-permute-start.1
  74.3 0.5 collective-permute-start.2
  74.8 0.0 copy-done.1
  74.8 3.4 %weight_grad.1 = (bf16[768,1536]{1,0:T(8,128)(2,1)S(1)}, f32[8,128]{1,0:T(8,128)S(1)}) custom-call(bf16[1024,768]{1,0:T(8,128)(2,1)S(1)} %get-tuple-element.21.refs_0_.refs_1_, bf16[1024,1536]{1,0:T(8,128)(2,1)S(1)} %copy-done.1), custom_call_target="tpu_custom_call" | custom-call | flops 1024 | bytes 1024 | tf_op jit(solution)/shard_map/weight_grad/pallas_call | solution.py:42
  78.2 0.0 copy-start.4
  78.2 1.4 %copy-done.4 = bf16[768,1536]{1,0:T(8,128)(2,1)} copy-done((bf16[768,1536]{1,0:T(8,128)(2,1)}, bf16[768,1536]{1,0:T(8,128)(2,1)S(1)}, u32[]{:S(2)}) %copy-start.4) | copy-done | bytes 2359320
  79.6 0.0 collective-permute-done.1.refs_3_
  79.6 0.0 collective-permute-done.2.refs_4_
  79.6 2.8 %project_mine.1 = (bf16[128,1536]{1,0:T(8,128)(2,1)}, bf16[128,1536]{1,0:T(8,128)(2,1)}, f32[128,1536]{1,0:T(8,128)S(1)}, f32[128,1536]{1,0:T(8,128)S(1)}, f32[8,128]{1,0:T(8,128)S(1)}) custom-call(s32[3]{0:T(128)S(1)} %pad_add_fusion.refs_0_, bf16[1024,768]{1,0:T(8,128)(2,1)S(1)} %get-tuple-element.21.refs_0_.refs_1_, bf16[768,1536]{1,0:T(8,128)(2,1)S(1)} %copy-done.2, ...), custom_call_target="tpu_custom_call" | custom-call | flops 1024 | bytes 1024 | tf_op jit(solution)/shard_map/project_mine/pallas_call | solution.py:42
  82.4 0.0 copy-start.5
  82.4 0.9 copy-done.5
  83.3 0.0 copy-start.3
  83.3 3.2 %collective-permute-start.4 = (bf16[128,1536]{1,0:T(8,128)(2,1)}, bf16[128,1536]{1,0:T(8,128)(2,1)S(1)}, u32[]{:S(2)}, u32[]{:S(2)}) collective-permute-start(bf16[128,1536]{1,0:T(8,128)(2,1)} %get-tuple-element.28), channel_id=1, source_target_pairs={{0,16},{8,56},{16,32},{24,8},{32,48},{40,24},{48,0},{56,40},{1,17}... | collective-permute-start | bytes 1179656 | tf_op jit(solution)/shard_map/ppermute | solution.py:221
  86.5 0.0 reduce-scatter.2.cloned.1.call-update
  86.5 2.7 %collective-permute-start.3 = (bf16[128,1536]{1,0:T(8,128)(2,1)}, bf16[128,1536]{1,0:T(8,128)(2,1)S(1)}, u32[]{:S(2)}, u32[]{:S(2)}) collective-permute-start(bf16[128,1536]{1,0:T(8,128)(2,1)} %get-tuple-element.26), channel_id=1, source_target_pairs={{0,48},{8,24},{16,0},{24,40},{32,16},{40,56},{48,32},{56,8},{1,49}... | collective-permute-start | bytes 1179656 | tf_op jit(solution)/shard_map/ppermute | solution.py:221
  89.2 14.1 %all-to-all-done.2.refs_1_ = bf16[8,1024,128]{2,1,0:T(8,128)(2,1)} async-done(((bf16[8,1024,128]{2,1,0:T(8,128)(2,1)}), bf16[8,1024,128]{2,1,0:T(8,128)(2,1)}, u32[]{:S(2)}, u32[]{:S(2)}) %all-to-all-start.2) | async-done | bytes 2097184 | tf_op jit(solution)/shard_map/all_to_all | solution.py:223
  103.4 0.0 copy-done.3
  103.4 0.0 copy-start.6
  103.4 6.0 %attend_backward.1 = bf16[1024,384]{1,0:T(8,128)(2,1)} custom-call(bf16[1024,384]{1,0:T(8,128)(2,1)S(1)} %bitcast.6, bf16[8,1024,128]{2,1,0:T(8,128)(2,1)} %all-to-all-done.2.refs_1_, f32[8,128]{1,0:T(8,128)S(1)} %get-tuple-element.30.refs_2_), custom_call_target="tpu_custom_call" | custom-call | flops 1024 | bytes 1024 | tf_op jit(solution)/shard_map/attend_backward/pallas_call | solution.py:42
  109.4 4.8 %all-to-all-start.3 = ((bf16[8,128,384]{2,1,0:T(8,128)(2,1)}), bf16[8,128,384]{2,1,0:T(8,128)(2,1)S(1)}, u32[]{:S(2)}, u32[]{:S(2)}) async-start(bf16[8,128,384]{2,1,0:T(8,128)(2,1)} %bitcast.7), calls=%async_computation.3 | async-start | bytes 1572864 | tf_op jit(solution)/shard_map/all_to_all | solution.py:223
  114.2 0.0 collective-permute-done.4.refs_1_
  114.3 0.0 copy-done.6
  114.3 0.1 add_output.1
  114.3 1.8 %collective-permute-start.5 = (bf16[128,1536]{1,0:T(8,128)(2,1)S(1)}, bf16[128,1536]{1,0:T(8,128)(2,1)S(1)}, u32[]{:S(2)}, u32[]{:S(2)}) collective-permute-start(bf16[128,1536]{1,0:T(8,128)(2,1)S(1)} %add_output.1), channel_id=1, source_target_pairs={{0,16},{8,56},{16,32},{24,8},{32,48},{40,24},{48,0},{56,40},{1,17}... | collective-permute-start | bytes 1179656 | tf_op jit(solution)/shard_map/ppermute | solution.py:221
  116.1 0.0 collective-permute-done.3.refs_1_
  116.1 16.0 %collective-permute-done.5.refs_2_ = bf16[128,1536]{1,0:T(8,128)(2,1)S(1)} collective-permute-done((bf16[128,1536]{1,0:T(8,128)(2,1)S(1)}, bf16[128,1536]{1,0:T(8,128)(2,1)S(1)}, u32[]{:S(2)}, u32[]{:S(2)}) %collective-permute-start.5) | collective-permute-done | bytes 393248 | tf_op jit(solution)/shard_map/ppermute | solution.py:221
  132.2 0.9 sum_output.1
  133.0 0.0 all-to-all-done.3.refs_0_
  133.1 0.9 unpack_heads.1
  134.0 0.0 reduce-scatter.2.cloned.1.call-done
Async XLA Ops:
  7.2 50.4 %all-gather.2.cloned.1.call-start = ((), (), s32[]{:S(2)}) async-start(), calls=%async_computation.5 | async-start | bytes 3538944 | tf_op jit(solution)/shard_map/all_gather | solution.py:227
  27.5 30.1 %copy-start.2 = (bf16[768,1536]{1,0:T(8,128)(2,1)S(1)}, bf16[768,1536]{1,0:T(8,128)(2,1)}, u32[]{:S(2)}) copy-start(bf16[768,1536]{1,0:T(8,128)(2,1)} %refs_2_.3) | copy-start | bytes 7077892
  50.3 19.8 %collective-permute-start = (bf16[3,1024,128]{2,1,0:T(8,128)(2,1)}, bf16[3,1024,128]{2,1,0:T(8,128)(2,1)}, u32[]{:S(2)}, u32[]{:S(2)}) collective-permute-start(bf16[3,1024,128]{2,1,0:T(8,128)(2,1)} %slice.4), channel_id=1, source_target_pairs={{0,4},{1,5},{2,6},{3,7},{4,0},{5,1},{6,2},{7,3},{8,12},{9,13},{10,... | collective-permute-start | bytes 2359304 | tf_op jit(solution)/shard_map/ppermute | solution.py:254
  57.6 1.9 %copy-start = (bf16[1024,1536]{1,0:T(8,128)(2,1)S(1)}, bf16[1024,1536]{1,0:T(8,128)(2,1)}, u32[]{:S(2)}) copy-start(bf16[1024,1536]{1,0:T(8,128)(2,1)} %all-gather.2.cloned.1.call-done.refs_0_.refs_1_) | copy-start | bytes 9437188
  63.2 40.2 %all-to-all-start.2 = ((bf16[8,1024,128]{2,1,0:T(8,128)(2,1)}), bf16[8,1024,128]{2,1,0:T(8,128)(2,1)}, u32[]{:S(2)}, u32[]{:S(2)}) async-start(bf16[8,1024,128]{2,1,0:T(8,128)(2,1)} %get-tuple-element.29), calls=%async_computation.2 | async-start | bytes 4194304 | tf_op jit(solution)/shard_map/all_to_all | solution.py:223
  69.1 64.9 %reduce-scatter.2.cloned.1.call-start = ((), (), s32[]{:S(2)}) async-start(), calls=%async_computation.6 | async-start | bytes 2949120 | tf_op jit(solution)/shard_map/reduce_scatter | solution.py:292
  70.1 4.7 %copy-start.1 = (bf16[1024,1536]{1,0:T(8,128)(2,1)S(1)}, bf16[1024,1536]{1,0:T(8,128)(2,1)}, u32[]{:S(2)}) copy-start(bf16[1024,1536]{1,0:T(8,128)(2,1)} %all-gather.2.cloned.1.call-done.refs_0_.refs_1_) | copy-start | bytes 9437188
  74.2 5.4 %collective-permute-start.1 = (bf16[512,768]{1,0:T(8,128)(2,1)S(1)}, bf16[512,768]{1,0:T(8,128)(2,1)S(1)}, u32[]{:S(2)}, u32[]{:S(2)}) collective-permute-start(bf16[512,768]{1,0:T(8,128)(2,1)S(1)} %get-tuple-element.22), channel_id=1, source_target_pairs={{0,8},{8,0},{16,24},{24,16},{32,40},{40,32},{48,56},{56,48},{1,9},... | collective-permute-start | bytes 2359304 | tf_op jit(solution)/shard_map/ppermute | solution.py:221
  74.3 5.3 %collective-permute-start.2 = (bf16[512,768]{1,0:T(8,128)(2,1)S(1)}, bf16[512,768]{1,0:T(8,128)(2,1)S(1)}, u32[]{:S(2)}, u32[]{:S(2)}) collective-permute-start(bf16[512,768]{1,0:T(8,128)(2,1)S(1)} %get-tuple-element.23), channel_id=1, source_target_pairs={{0,8},{8,0},{16,24},{24,16},{32,40},{40,32},{48,56},{56,48},{1,9},... | collective-permute-start | bytes 2359304 | tf_op jit(solution)/shard_map/ppermute | solution.py:221
  78.2 1.4 %copy-start.4 = (bf16[768,1536]{1,0:T(8,128)(2,1)}, bf16[768,1536]{1,0:T(8,128)(2,1)S(1)}, u32[]{:S(2)}) copy-start(bf16[768,1536]{1,0:T(8,128)(2,1)S(1)} %get-tuple-element.34) | copy-start | bytes 7077892
  82.4 0.9 copy-start.5
  83.3 20.1 %copy-start.3 = (bf16[8,128,384]{2,1,0:T(8,128)(2,1)S(1)}, bf16[8,128,384]{2,1,0:T(8,128)(2,1)}, u32[]{:S(2)}) copy-start(bf16[8,128,384]{2,1,0:T(8,128)(2,1)} %all_to_all.20) | copy-start | bytes 2359300
  83.3 30.9 %collective-permute-start.4 = (bf16[128,1536]{1,0:T(8,128)(2,1)}, bf16[128,1536]{1,0:T(8,128)(2,1)S(1)}, u32[]{:S(2)}, u32[]{:S(2)}) collective-permute-start(bf16[128,1536]{1,0:T(8,128)(2,1)} %get-tuple-element.28), channel_id=1, source_target_pairs={{0,16},{8,56},{16,32},{24,8},{32,48},{40,24},{48,0},{56,40},{1,17}... | collective-permute-start | bytes 1179656 | tf_op jit(solution)/shard_map/ppermute | solution.py:221
  86.5 29.6 %collective-permute-start.3 = (bf16[128,1536]{1,0:T(8,128)(2,1)}, bf16[128,1536]{1,0:T(8,128)(2,1)S(1)}, u32[]{:S(2)}, u32[]{:S(2)}) collective-permute-start(bf16[128,1536]{1,0:T(8,128)(2,1)} %get-tuple-element.26), channel_id=1, source_target_pairs={{0,48},{8,24},{16,0},{24,40},{32,16},{40,56},{48,32},{56,8},{1,49}... | collective-permute-start | bytes 1179656 | tf_op jit(solution)/shard_map/ppermute | solution.py:221
  103.4 10.9 %copy-start.6 = (f32[128,1536]{1,0:T(8,128)S(1)}, f32[128,1536]{1,0:T(8,128)}, u32[]{:S(2)}) copy-start(f32[128,1536]{1,0:T(8,128)} %copy-done.5) | copy-start | bytes 2359300
  109.4 23.6 %all-to-all-start.3 = ((bf16[8,128,384]{2,1,0:T(8,128)(2,1)}), bf16[8,128,384]{2,1,0:T(8,128)(2,1)S(1)}, u32[]{:S(2)}, u32[]{:S(2)}) async-start(bf16[8,128,384]{2,1,0:T(8,128)(2,1)} %bitcast.7), calls=%async_computation.3 | async-start | bytes 1572864 | tf_op jit(solution)/shard_map/all_to_all | solution.py:223
  114.3 17.8 %collective-permute-start.5 = (bf16[128,1536]{1,0:T(8,128)(2,1)S(1)}, bf16[128,1536]{1,0:T(8,128)(2,1)S(1)}, u32[]{:S(2)}, u32[]{:S(2)}) collective-permute-start(bf16[128,1536]{1,0:T(8,128)(2,1)S(1)} %add_output.1), channel_id=1, source_target_pairs={{0,16},{8,56},{16,32},{24,8},{32,48},{40,24},{48,0},{56,40},{1,17}... | collective-permute-start | bytes 1179656 | tf_op jit(solution)/shard_map/ppermute | solution.py:221
Sparse Core Ops, SparseCore 0:
  9.8 47.7 all-gather.1
  86.7 34.7 reduce-scatter.1

commit v6 on v2

--- a/solution.py
+++ b/solution.py
@@ -171,7 +171,8 @@
         out[...] = jnp.dot(rows, w[:, lanes[i]], preferred_element_type=F32).astype(BF16)
 
 
-def mine_kernel(place, ctx, w, left, right, far, now, later, own):
+def mine_kernel(place, ctx, w, left, right, far, now, later, own, token):
+    token[...] = jnp.zeros(token.shape, token.dtype)
     h, core = place[0], place[1]
     rows = rows_for(ctx, h, core)
     wide = left.shape[1]
@@ -227,6 +228,7 @@
         (qkv,),
         out_specs=[HBM],
         scratch=[pltpu.VMEM((seq, DH), BF16), pltpu.SemaphoreType.DMA((steps, 4))],
+        vmem=24,
     )
     near = lax.all_to_all(copies, "col", 0, 0, tiled=True, axis_index_groups=SAME_Z)
     other = lax.ppermute(near[:3], "col", ACROSS_Z)
@@ -255,6 +257,7 @@
         ],
         after=[token],
         flops=60_000_000_000,
+        vmem=24,
     )
     w_part, token = local(
         weight_kernel,
@@ -269,10 +272,10 @@
     weight_grad = lax.psum_scatter(w_part, "depth", scatter_dimension=0, tiled=True)
 
     block = (POS, feats)
-    far, now, later, own = local(
+    far, now, later, own, token = local(
         mine_kernel,
         "project_mine",
-        [(block, BF16, ARRAY), (block, BF16, ARRAY), (block, F32, ARRAY), (block, F32, ARRAY)],
+        [(block, dtype, ARRAY) for dtype in (BF16, BF16, F32, F32)] + [((8, DH), F32, ARRAY)],
         (place, ctx, weight, *[on_row(a, ACROSS_CORE) for a in theirs]),
         in_specs=[scalars] + [WHOLE] * 4,
         after=[token],
@@ -295,7 +298,7 @@
         "attend_backward",
         [((seq, 3 * DH), BF16, IN_HBM)],
         (qkv, parts),
-        after=[own],
+        after=[token],
         vmem=24,
         grid=(steps,),
         in_specs=[

time: 140 us -> 141 us (level)
  waiting for transfers between devices: 29.2 us -> 33.6 us
  Pallas kernels: 29.7 us -> 28.1 us
  local copies, waits for them, and re-layouts: 11.2 us -> 9.62 us
    pallas_call x10, Pallas kernels: 29.7 us -> 28.1 us  [local(): pl.pallas_call(body, out_shape=[kind(shape, dtype) for shape, dtype, kind...]
    unnamed x32 -> x20, local copies, waits for them, and re-layouts: 10.1 us -> 8.6 us
    all_to_all x2, waiting for transfers between devices: 10.6 us -> 12 us  [shards(): trade = lambda a: lax.all_to_all(a, 'col', 0, 0, tiled=True)]
  transfers between devices with their start and end apart: 10 -> 10, of which waited for: 4 -> 4; matrix products, arithmetic and copies ran while one was open for 1% -> 1% of each run, Pallas kernels for 21% -> 20%
where the time goes in v6:
time: 141 us
  blocking collectives  34.9 us (25%)
  waiting for transfers between devices  33.6 us (24%)
  Pallas kernels  28.1 us (20%)
  starting transfers between devices  20.2 us (14%)
  between operations  14.1 us (10%)
  local copies, waits for them, and re-layouts  9.62 us (7%)
    pallas_call x10, Pallas kernels, local(): pl.pallas_call(body, out_shape=[kind(shape, dtype) for shape, dtype, kind...  28.1 us
    all_to_all x1, blocking collectives, shards(): lax.all_to_all(copies, 'col', 0, 0, tiled=True, axis_index_groups=SAME_Z)  17.5 us
    all_to_all x1, blocking collectives, shards(): trade = lambda a: lax.all_to_all(a, 'col', 0, 0, tiled=True)  17.4 us
    ppermute x5, waiting for transfers between devices, shards(): on_row = lambda a, perm: lax.ppermute(a, 'row', perm)  13.6 us
    all_to_all x2, waiting for transfers between devices, shards(): trade = lambda a: lax.all_to_all(a, 'col', 0, 0, tiled=True)  12 us
    all_to_all x2, starting transfers between devices, shards(): trade = lambda a: lax.all_to_all(a, 'col', 0, 0, tiled=True)  10.9 us
    unnamed x20, local copies, waits for them, and re-layouts  8.6 us
    ppermute x5, starting transfers between devices, shards(): on_row = lambda a, perm: lax.ppermute(a, 'row', perm)  8.23 us
  transfers between devices with their start and end apart: 10, of which 4 were waited for; matrix products, arithmetic and copies ran while one was open for 1% of the time, Pallas kernels for 20%

profile of v6, /device:TPU:8, one launch (start us, length us, event | category | flops | bytes accessed | tf_op | source)
XLA Modules:
  0.0 140.7 jit_solution(3992714648319817417)
XLA Ops:
  7.2 0.0 all-gather.2.cloned.1.call-start
  7.2 0.7 all-gather.2.cloned.1.call-update
  7.9 2.1 %pack_heads.1 = bf16[8,128,384]{2,1,0:T(8,128)(2,1)} custom-call(bf16[128,768]{1,0:T(8,128)(2,1)} %refs_0_.1, bf16[128,768]{1,0:T(8,128)(2,1)} %refs_1_.2, bf16[128,768]{1,0:T(8,128)(2,1)} %refs_2_.2), custom_call_target="tpu_custom_call" | custom-call | flops 1024 | bytes 1024 | tf_op jit(solution)/shard_map/pack_heads/pallas_call | solution.py:42
  10.0 17.4 %all_to_all.20 = bf16[8,128,384]{2,1,0:T(8,128)(2,1)S(1)} all-to-all(bf16[8,128,384]{2,1,0:T(8,128)(2,1)} %pack_heads.1), channel_id=1, replica_groups=mesh['depth'=4,'row'=8,'col'=8] {'col'}, dimensions={0} | all-to-all | bytes 1572864 | tf_op jit(solution)/shard_map/all_to_all | solution.py:213
  27.4 0.0 copy-start.2
  27.4 3.0 %attend_forward.1 = bf16[4,1024,128]{2,1,0:T(8,128)(2,1)} custom-call(bf16[1024,384]{1,0:T(8,128)(2,1)S(1)} %bitcast.5), custom_call_target="tpu_custom_call" | custom-call | flops 1024 | bytes 1024 | tf_op jit(solution)/shard_map/attend_forward/pallas_call | solution.py:42
  30.5 17.5 %all_to_all.21.refs_1_ = bf16[4,1024,128]{2,1,0:T(8,128)(2,1)S(1)} all-to-all(bf16[4,1024,128]{2,1,0:T(8,128)(2,1)} %attend_forward.1), channel_id=1, replica_groups={{0,1,2,3},{4,5,6,7},{8,9,10,11},{12,13,14,15},{16,17,18,19},{20,21,22,2..., dimensions={0} | all-to-all | bytes 2097152 | tf_op jit(solution)/shard_map/all_to_all | solution.py:233
  48.0 1.0 slice.4
  49.0 0.0 copy-start.3
  49.0 1.1 copy-done.3
  50.1 1.0 collective-permute-start
  51.1 0.1 pad_add_fusion.refs_0_
  51.2 6.3 %all-gather.2.cloned.1.call-done.refs_0_.refs_1_ = bf16[1024,1536]{1,0:T(8,128)(2,1)} async-done(((bf16[128,1536]{1,0:T(8,128)(2,1)}), bf16[1024,1536]{1,0:T(8,128)(2,1)}) %all-gather.2.cloned.1.call-update) | async-done | bytes 3145744 | tf_op jit(solution)/shard_map/all_gather | solution.py:217
  57.5 0.0 copy-done.2
  57.5 0.0 copy-start
  57.5 1.9 %copy-done = bf16[1024,1536]{1,0:T(8,128)(2,1)S(1)} copy-done((bf16[1024,1536]{1,0:T(8,128)(2,1)S(1)}, bf16[1024,1536]{1,0:T(8,128)(2,1)}, u32[]{:S(2)}) %copy-start) | copy-done | bytes 3145752
  59.3 3.7 %context_grad.1 = (bf16[8,1024,128]{2,1,0:T(8,128)(2,1)}, f32[8,128]{1,0:T(8,128)S(1)}) custom-call(bf16[1024,1536]{1,0:T(8,128)(2,1)S(1)} %copy-done, bf16[768,1536]{1,0:T(8,128)(2,1)S(1)} %copy-done.2), custom_call_target="tpu_custom_call" | custom-call | flops 1024 | bytes 1024 | tf_op jit(solution)/shard_map/context_grad/pallas_call | solution.py:42
  63.0 6.1 %all-to-all-start.2 = ((bf16[8,1024,128]{2,1,0:T(8,128)(2,1)}), bf16[8,1024,128]{2,1,0:T(8,128)(2,1)}, u32[]{:S(2)}, u32[]{:S(2)}) async-start(bf16[8,1024,128]{2,1,0:T(8,128)(2,1)} %get-tuple-element.29), calls=%async_computation.2 | async-start | bytes 4194304 | tf_op jit(solution)/shard_map/all_to_all | solution.py:213
  69.1 0.0 reduce-scatter.2.cloned.1.call-start
  69.1 1.0 collective-permute-done.refs_2_
  70.1 0.0 copy-start.4
  70.1 1.2 copy-done.4
  71.4 0.0 copy-start.1
  71.4 4.1 %project_theirs.1 = (bf16[1024,768]{1,0:T(8,128)(2,1)S(1)}, bf16[512,768]{1,0:T(8,128)(2,1)S(1)}, bf16[512,768]{1,0:T(8,128)(2,1)S(1)}) custom-call(s32[3]{0:T(128)S(1)} %pad_add_fusion.refs_0_, bf16[4,1024,128]{2,1,0:T(8,128)(2,1)S(1)} %copy-done.4, bf16[3,1024,128]{2,1,0:T(8,128)(2,1)} %collective-permute-done.refs_2_, bf16[768,1536]{1,0:T(8,128)(2,1)S(1)} %copy-done.2, ...), custom_call_target="tpu_custom_call" | custom-call | flops 60000002048 | bytes 1024 | tf_op jit(solution)/shard_map/project_theirs/pallas_call | solution.py:42
  75.5 0.1 collective-permute-start.1
  75.6 0.5 collective-permute-start.2
  76.1 0.0 copy-done.1
  76.1 3.4 %weight_grad.1 = (bf16[768,1536]{1,0:T(8,128)(2,1)S(1)}, f32[8,128]{1,0:T(8,128)S(1)}) custom-call(bf16[1024,768]{1,0:T(8,128)(2,1)S(1)} %get-tuple-element.21.refs_0_.refs_1_, bf16[1024,1536]{1,0:T(8,128)(2,1)S(1)} %copy-done.1), custom_call_target="tpu_custom_call" | custom-call | flops 1024 | bytes 1024 | tf_op jit(solution)/shard_map/weight_grad/pallas_call | solution.py:42
  79.5 0.0 copy-start.5
  79.5 1.4 %copy-done.5 = bf16[768,1536]{1,0:T(8,128)(2,1)} copy-done((bf16[768,1536]{1,0:T(8,128)(2,1)}, bf16[768,1536]{1,0:T(8,128)(2,1)S(1)}, u32[]{:S(2)}) %copy-start.5) | copy-done | bytes 2359320
  80.9 0.0 collective-permute-done.1.refs_3_
  80.9 0.0 collective-permute-done.2.refs_4_
  80.9 2.8 %project_mine.1 = (bf16[128,1536]{1,0:T(8,128)(2,1)}, bf16[128,1536]{1,0:T(8,128)(2,1)}, f32[128,1536]{1,0:T(8,128)S(1)}, f32[128,1536]{1,0:T(8,128)S(1)}, f32[8,128]{1,0:T(8,128)S(1)}) custom-call(s32[3]{0:T(128)S(1)} %pad_add_fusion.refs_0_, bf16[1024,768]{1,0:T(8,128)(2,1)S(1)} %get-tuple-element.21.refs_0_.refs_1_, bf16[768,1536]{1,0:T(8,128)(2,1)S(1)} %copy-done.2, ...), custom_call_target="tpu_custom_call" | custom-call | flops 1024 | bytes 1024 | tf_op jit(solution)/shard_map/project_mine/pallas_call | solution.py:42
  83.7 0.0 copy-start.6
  83.7 0.9 copy-done.6
  84.6 0.0 copy-start.8
  84.6 0.9 copy-done.8
  85.5 3.4 %collective-permute-start.4 = (bf16[128,1536]{1,0:T(8,128)(2,1)}, bf16[128,1536]{1,0:T(8,128)(2,1)}, u32[]{:S(2)}, u32[]{:S(2)}) collective-permute-start(bf16[128,1536]{1,0:T(8,128)(2,1)} %get-tuple-element.28), channel_id=1, source_target_pairs={{0,16},{8,56},{16,32},{24,8},{32,48},{40,24},{48,0},{56,40},{1,17}... | collective-permute-start | bytes 1179656 | tf_op jit(solution)/shard_map/ppermute | solution.py:211
  89.0 0.0 reduce-scatter.2.cloned.1.call-update
  89.0 2.4 %collective-permute-start.3 = (bf16[128,1536]{1,0:T(8,128)(2,1)}, bf16[128,1536]{1,0:T(8,128)(2,1)S(1)}, u32[]{:S(2)}, u32[]{:S(2)}) collective-permute-start(bf16[128,1536]{1,0:T(8,128)(2,1)} %get-tuple-element.26), channel_id=1, source_target_pairs={{0,48},{8,24},{16,0},{24,40},{32,16},{40,56},{48,32},{56,8},{1,49}... | collective-permute-start | bytes 1179656 | tf_op jit(solution)/shard_map/ppermute | solution.py:211
  91.4 12.0 %all-to-all-done.2.refs_1_ = bf16[8,1024,128]{2,1,0:T(8,128)(2,1)} async-done(((bf16[8,1024,128]{2,1,0:T(8,128)(2,1)}), bf16[8,1024,128]{2,1,0:T(8,128)(2,1)}, u32[]{:S(2)}, u32[]{:S(2)}) %all-to-all-start.2) | async-done | bytes 2097184 | tf_op jit(solution)/shard_map/all_to_all | solution.py:213
  103.4 6.1 %attend_backward.1 = bf16[1024,384]{1,0:T(8,128)(2,1)} custom-call(bf16[1024,384]{1,0:T(8,128)(2,1)S(1)} %bitcast.6, bf16[8,1024,128]{2,1,0:T(8,128)(2,1)} %all-to-all-done.2.refs_1_, f32[8,128]{1,0:T(8,128)S(1)} %get-tuple-element.30.refs_2_), custom_call_target="tpu_custom_call" | custom-call | flops 1024 | bytes 1024 | tf_op jit(solution)/shard_map/attend_backward/pallas_call | solution.py:42
  109.5 4.9 %all-to-all-start.3 = ((bf16[8,128,384]{2,1,0:T(8,128)(2,1)}), bf16[8,128,384]{2,1,0:T(8,128)(2,1)S(1)}, u32[]{:S(2)}, u32[]{:S(2)}) async-start(bf16[8,128,384]{2,1,0:T(8,128)(2,1)} %bitcast.7), calls=%async_computation.3 | async-start | bytes 1572864 | tf_op jit(solution)/shard_map/all_to_all | solution.py:213
  114.4 0.0 collective-permute-done.4.refs_1_
  114.4 0.0 copy-start.9
  114.4 1.1 copy-done.9
  115.5 0.0 copy-start.7
  115.5 1.1 add_output.1
  116.6 1.8 %collective-permute-start.5 = (bf16[128,1536]{1,0:T(8,128)(2,1)S(1)}, bf16[128,1536]{1,0:T(8,128)(2,1)S(1)}, u32[]{:S(2)}, u32[]{:S(2)}) collective-permute-start(bf16[128,1536]{1,0:T(8,128)(2,1)S(1)} %add_output.1), channel_id=1, source_target_pairs={{0,16},{8,56},{16,32},{24,8},{32,48},{40,24},{48,0},{56,40},{1,17}... | collective-permute-start | bytes 1179656 | tf_op jit(solution)/shard_map/ppermute | solution.py:211
  118.5 0.0 collective-permute-done.3.refs_1_
  118.5 13.6 %collective-permute-done.5.refs_2_ = bf16[128,1536]{1,0:T(8,128)(2,1)S(1)} collective-permute-done((bf16[128,1536]{1,0:T(8,128)(2,1)S(1)}, bf16[128,1536]{1,0:T(8,128)(2,1)S(1)}, u32[]{:S(2)}, u32[]{:S(2)}) %collective-permute-start.5) | collective-permute-done | bytes 393248 | tf_op jit(solution)/shard_map/ppermute | solution.py:211
  132.1 0.0 copy-done.7
  132.1 0.9 sum_output.1
  132.9 0.0 all-to-all-done.3.refs_0_
  132.9 0.9 unpack_heads.1
  133.8 0.0 reduce-scatter.2.cloned.1.call-done
Async XLA Ops:
  7.2 50.3 %all-gather.2.cloned.1.call-start = ((), (), s32[]{:S(2)}) async-start(), calls=%async_computation.5 | async-start | bytes 3538944 | tf_op jit(solution)/shard_map/all_gather | solution.py:217
  27.4 30.1 %copy-start.2 = (bf16[768,1536]{1,0:T(8,128)(2,1)S(1)}, bf16[768,1536]{1,0:T(8,128)(2,1)}, u32[]{:S(2)}) copy-start(bf16[768,1536]{1,0:T(8,128)(2,1)} %refs_2_.3) | copy-start | bytes 7077892
  49.0 1.1 copy-start.3
  50.1 20.1 %collective-permute-start = (bf16[3,1024,128]{2,1,0:T(8,128)(2,1)}, bf16[3,1024,128]{2,1,0:T(8,128)(2,1)}, u32[]{:S(2)}, u32[]{:S(2)}) collective-permute-start(bf16[3,1024,128]{2,1,0:T(8,128)(2,1)} %slice.4), channel_id=1, source_target_pairs={{0,4},{1,5},{2,6},{3,7},{4,0},{5,1},{6,2},{7,3},{8,12},{9,13},{10,... | collective-permute-start | bytes 2359304 | tf_op jit(solution)/shard_map/ppermute | solution.py:234
  57.5 1.9 %copy-start = (bf16[1024,1536]{1,0:T(8,128)(2,1)S(1)}, bf16[1024,1536]{1,0:T(8,128)(2,1)}, u32[]{:S(2)}) copy-start(bf16[1024,1536]{1,0:T(8,128)(2,1)} %all-gather.2.cloned.1.call-done.refs_0_.refs_1_) | copy-start | bytes 9437188
  63.0 40.4 %all-to-all-start.2 = ((bf16[8,1024,128]{2,1,0:T(8,128)(2,1)}), bf16[8,1024,128]{2,1,0:T(8,128)(2,1)}, u32[]{:S(2)}, u32[]{:S(2)}) async-start(bf16[8,1024,128]{2,1,0:T(8,128)(2,1)} %get-tuple-element.29), calls=%async_computation.2 | async-start | bytes 4194304 | tf_op jit(solution)/shard_map/all_to_all | solution.py:213
  69.1 64.7 %reduce-scatter.2.cloned.1.call-start = ((), (), s32[]{:S(2)}) async-start(), calls=%async_computation.6 | async-start | bytes 2949120 | tf_op jit(solution)/shard_map/reduce_scatter | solution.py:272
  70.1 1.2 copy-start.4
  71.4 4.7 %copy-start.1 = (bf16[1024,1536]{1,0:T(8,128)(2,1)S(1)}, bf16[1024,1536]{1,0:T(8,128)(2,1)}, u32[]{:S(2)}) copy-start(bf16[1024,1536]{1,0:T(8,128)(2,1)} %all-gather.2.cloned.1.call-done.refs_0_.refs_1_) | copy-start | bytes 9437188
  75.5 5.4 %collective-permute-start.1 = (bf16[512,768]{1,0:T(8,128)(2,1)S(1)}, bf16[512,768]{1,0:T(8,128)(2,1)S(1)}, u32[]{:S(2)}, u32[]{:S(2)}) collective-permute-start(bf16[512,768]{1,0:T(8,128)(2,1)S(1)} %get-tuple-element.22), channel_id=1, source_target_pairs={{0,8},{8,0},{16,24},{24,16},{32,40},{40,32},{48,56},{56,48},{1,9},... | collective-permute-start | bytes 2359304 | tf_op jit(solution)/shard_map/ppermute | solution.py:211
  75.6 5.3 %collective-permute-start.2 = (bf16[512,768]{1,0:T(8,128)(2,1)S(1)}, bf16[512,768]{1,0:T(8,128)(2,1)S(1)}, u32[]{:S(2)}, u32[]{:S(2)}) collective-permute-start(bf16[512,768]{1,0:T(8,128)(2,1)S(1)} %get-tuple-element.23), channel_id=1, source_target_pairs={{0,8},{8,0},{16,24},{24,16},{32,40},{40,32},{48,56},{56,48},{1,9},... | collective-permute-start | bytes 2359304 | tf_op jit(solution)/shard_map/ppermute | solution.py:211
  79.5 1.4 %copy-start.5 = (bf16[768,1536]{1,0:T(8,128)(2,1)}, bf16[768,1536]{1,0:T(8,128)(2,1)S(1)}, u32[]{:S(2)}) copy-start(bf16[768,1536]{1,0:T(8,128)(2,1)S(1)} %get-tuple-element.34) | copy-start | bytes 7077892
  83.7 0.9 copy-start.6
  84.6 0.9 copy-start.8
  85.5 28.8 %collective-permute-start.4 = (bf16[128,1536]{1,0:T(8,128)(2,1)}, bf16[128,1536]{1,0:T(8,128)(2,1)}, u32[]{:S(2)}, u32[]{:S(2)}) collective-permute-start(bf16[128,1536]{1,0:T(8,128)(2,1)} %get-tuple-element.28), channel_id=1, source_target_pairs={{0,16},{8,56},{16,32},{24,8},{32,48},{40,24},{48,0},{56,40},{1,17}... | collective-permute-start | bytes 1179656 | tf_op jit(solution)/shard_map/ppermute | solution.py:211
  89.0 29.5 %collective-permute-start.3 = (bf16[128,1536]{1,0:T(8,128)(2,1)}, bf16[128,1536]{1,0:T(8,128)(2,1)S(1)}, u32[]{:S(2)}, u32[]{:S(2)}) collective-permute-start(bf16[128,1536]{1,0:T(8,128)(2,1)} %get-tuple-element.26), channel_id=1, source_target_pairs={{0,48},{8,24},{16,0},{24,40},{32,16},{40,56},{48,32},{56,8},{1,49}... | collective-permute-start | bytes 1179656 | tf_op jit(solution)/shard_map/ppermute | solution.py:211
  109.5 23.4 %all-to-all-start.3 = ((bf16[8,128,384]{2,1,0:T(8,128)(2,1)}), bf16[8,128,384]{2,1,0:T(8,128)(2,1)S(1)}, u32[]{:S(2)}, u32[]{:S(2)}) async-start(bf16[8,128,384]{2,1,0:T(8,128)(2,1)} %bitcast.7), calls=%async_computation.3 | async-start | bytes 1572864 | tf_op jit(solution)/shard_map/all_to_all | solution.py:213
  114.4 1.1 copy-start.9
  115.5 16.6 %copy-start.7 = (f32[128,1536]{1,0:T(8,128)S(1)}, f32[128,1536]{1,0:T(8,128)}, u32[]{:S(2)}) copy-start(f32[128,1536]{1,0:T(8,128)} %copy-done.6) | copy-start | bytes 2359300
  116.6 15.4 %collective-permute-start.5 = (bf16[128,1536]{1,0:T(8,128)(2,1)S(1)}, bf16[128,1536]{1,0:T(8,128)(2,1)S(1)}, u32[]{:S(2)}, u32[]{:S(2)}) collective-permute-start(bf16[128,1536]{1,0:T(8,128)(2,1)S(1)} %add_output.1), channel_id=1, source_target_pairs={{0,16},{8,56},{16,32},{24,8},{32,48},{40,24},{48,0},{56,40},{1,17}... | collective-permute-start | bytes 1179656 | tf_op jit(solution)/shard_map/ppermute | solution.py:211
Sparse Core Ops, SparseCore 0:
  9.8 47.5 all-gather.1
  89.1 34.2 reduce-scatter.1
